TPU v7x, 32 devices: a whole 2x2x4 slice. The times are simulated.
32 devices in a mesh: row: 8 (over y, x, core), team: 4 (over z).
Axes of the slice: x: 2, y: 2, z: 4, core: 2. Of those that a mesh axis runs over, the one named last changes fastest.
Arguments:
- features: bfloat16 [16384, 512], P('row'), may hold values from -6 to 6
- weight: bfloat16 [512, 512], replicated, may hold values from -0.25 to 0.25
- table: bfloat16 [8, 512], replicated, may hold values from -5 to 5
- labels: int32 [16384], P('row'), may hold values from 0 to 7
- label_mask: int32 [16384], P('row'), may hold values 0 or 1
- block_vals: bfloat16 [8, 4, 16, 128, 128], P('row', 'team'), may hold values from -0.25 to 0.25
- block_row: int32 [8, 4, 16], P('row', 'team'), may hold values from 0 to 15, as said below
- block_col: int32 [8, 4, 16], P('row', 'team'), may hold values from 0 to 31
- block_count: int32 [8, 4], P('row', 'team'), may hold values from 1 to 16, as said below
Outputs:
- output: bfloat16 [16384, 512], P(('row', 'team'))
- grad_weight: float32 [512, 512], replicated
- grad_features: bfloat16 [4, 4096, 512], P('team', 'row')
Inputs may be any that keep to these rules, and one draw needn't show every extreme that they name: Within one [r, t] list the pairs (block_row, block_col) of all 16 slots are distinct. Only the first block_count[r, t] slots of a list are live; some [r, t] has exactly 16 live slots in every draw.
All inputs are finite; a program needn't handle non-finite values. No bound on the sum of `label_mask` on one device may be relied on, other than what follows from the above.
Results may differ from a plain program's by a relative error of at most 0.0059.
Values may be sent and summed in bfloat16 or wider, within the bound.
No kernel may reach another device: no remote copies, remote signals or barrier semaphores. Data moves between devices by JAX's collectives and lax.ppermute only.
A program may use at most 64 MiB of HBM per device.

v0:
```python
import math

import jax
import jax.numpy as jnp
from jax import lax
from jax.sharding import PartitionSpec as P


def spread_2(value, axis, source):
    kept = jnp.where(lax.axis_index(axis) == source, value, 0).astype(value.dtype)
    return lax.psum(kept, axis)


def silu_slope(preact):
    sigma = jax.nn.sigmoid(preact)
    return sigma * (1.0 + preact * (1.0 - sigma))


def block_product(sources, values, gather_ids, target_ids, live_count, out_blocks, form):
    total_slots = values.shape[0]
    group_size = min(32, total_slots)
    feature_width = sources.shape[1]
    source_blocks = sources.reshape(sources.shape[0] // 128, 128, feature_width)
    target_table = jnp.arange(out_blocks, dtype=jnp.int32)

    def add_group(group_index, totals):
        first_slot = group_index * group_size
        group_values = values
        live_slots = first_slot + jnp.arange(group_size, dtype=jnp.int32) < live_count
        group_values = jnp.where(
            live_slots[:, None, None], group_values, jnp.zeros_like(group_values)
        )
        picked = source_blocks[gather_ids]
        product = jnp.einsum(form, group_values, picked, preferred_element_type=jnp.float32)
        upper = product.astype(jnp.bfloat16)
        upper_wide = lax.optimization_barrier(upper).astype(jnp.float32)
        lower = (product - upper_wide).astype(jnp.bfloat16)
        selector = (target_ids[None, :] == target_table[:, None]).astype(jnp.bfloat16)
        folded = jnp.einsum("sk,kif->sif", selector, upper, preferred_element_type=jnp.float32)
        folded = folded + jnp.einsum(
            "sk,kif->sif", selector, lower, preferred_element_type=jnp.float32
        )
        return totals + folded

    groups = (live_count + group_size - 1) // group_size
    totals = lax.fori_loop(
        jnp.int32(0), groups, add_group, jnp.zeros((out_blocks, 128, feature_width), jnp.float32)
    )
    return totals.reshape(out_blocks * 128, feature_width)


def local_layer(agg, weight, table, labels, label_mask):
    preact = jnp.dot(agg, weight, preferred_element_type=jnp.float32)
    active = jax.nn.silu(preact)
    classes = jnp.arange(table.shape[0], dtype=jnp.int32)
    onehot = (labels[:, None] == classes[None, :]).astype(jnp.float32)
    target = jnp.dot(onehot, table.astype(jnp.float32), precision=lax.Precision.HIGHEST)
    residual = label_mask.astype(jnp.float32)[:, None] * (active - target)
    grad_pre = (residual * silu_slope(preact)).astype(jnp.bfloat16)
    back_rows = jnp.dot(grad_pre, weight.T, preferred_element_type=jnp.float32).astype(jnp.bfloat16)
    return (active.astype(jnp.bfloat16), grad_pre, back_rows)


def per_device(
    features, weight, table, labels, label_mask, block_vals, block_row, block_col, block_count
):
    slab_rows = features.shape[0]
    row_count = lax.axis_size("row")
    team_count = lax.axis_size("team")
    sections = row_count // team_count
    team_index = lax.axis_index("team")
    share_rows = slab_rows // team_count
    share_start = team_index * share_rows
    slab_blocks = slab_rows // 128
    values = block_vals[0, 0]
    row_ids = block_row[0, 0]
    col_ids = block_col[0, 0]
    live_count = block_count[0, 0]
    pieces = [
        spread_2(features, "row", team_index * sections + section_index)
        for section_index in range(sections)
    ]
    feature_panel = jnp.concatenate(pieces, axis=0)
    partial_value = block_product(
        feature_panel, values, col_ids, row_ids, live_count, slab_blocks, "kij,kjf->kif"
    )
    agg_share = lax.psum_scatter(partial_value, "team", scatter_dimension=0, tiled=True).astype(
        jnp.bfloat16
    )
    label_share = lax.dynamic_slice_in_dim(labels, share_start, share_rows, 0)
    mask_share = lax.dynamic_slice_in_dim(label_mask, share_start, share_rows, 0)
    output, grad_share, back_share = local_layer(agg_share, weight, table, label_share, mask_share)
    back_rows = lax.all_gather(back_share, "team", axis=0, tiled=True)
    weight_term = jnp.dot(agg_share.T, grad_share, preferred_element_type=jnp.float32)
    grad_weight = lax.psum(weight_term, ("row", "team")) * (1.0 / math.sqrt(slab_rows * row_count))
    spread = block_product(
        back_rows, values, row_ids, col_ids, live_count, sections * slab_blocks, "kji,kjf->kif"
    )
    grad_piece = lax.psum_scatter(spread, "row", scatter_dimension=0, tiled=True).astype(
        jnp.bfloat16
    )
    return (output, grad_weight, grad_piece[None])


def solution(mesh):
    placed = (
        P("row", None),
        P(),
        P(),
        P("row"),
        P("row"),
        P("row", "team", None, None, None),
        P("row", "team", None),
        P("row", "team", None),
        P("row", "team"),
    )
    return jax.shard_map(
        per_device,
        mesh=mesh,
        in_specs=placed,
        out_specs=(P(("row", "team"), None), P(), P("team", "row", None)),
        check_vma=False,
    )
```

profile of v0, /device:TPU:9, one launch (start us, length us, event | category | flops | bytes accessed | tf_op | source)
XLA Modules:
  0.0 464.0 jit_solution(2303166604231541543)
XLA Ops:
  7.2 0.0 copy-start
  7.2 0.0 all-reduce.6.cloned.1.call-start
  7.2 3.9 broadcast_select_fusion.1
  11.1 0.0 all-reduce.6.cloned.1.call-update
  11.1 0.0 reduce-scatter.3.cloned.1.call-start
  11.8 0.0 copy-done.7
  11.9 81.8 %all-reduce.6.cloned.1.call-done = (bf16[2048,512]{1,0:T(8,128)(2,1)}, bf16[2048,512]{1,0:T(8,128)(2,1)}) async-done(((bf16[2048,512]{1,0:T(8,128)(2,1)}, bf16[2048,512]{1,0:T(8,128)(2,1)}), (bf16[2048,512]{1,0:T(8,128)(2,1)}, bf16[2048,512]{1,0:T(8,128)(2,1)})) %all-reduce.6.cloned.1.call-update) | async-done | bytes 4194320 | tf_op jit(solution)/shard_map/psum | solution.py:11
  93.7 4.4 pad_maximum_fusion
  98.1 2.9 gather_fusion
  101.0 0.0 copy-start.5
  101.0 0.0 copy-start.8
  101.0 2.5 broadcast_in_dim.42
  103.6 0.0 copy-done.5
  103.6 0.0 copy-done.8
  103.6 8.8 %while.26 = (s32[]{:T(128)}, f32[16,128,512]{2,0,1:T(8,128)}, s32[]{:T(128)}, s32[1,1,16]{2,1,0:T(1,128)S(1)}, s32[]{:T(128)}, /*index=5*/bf16[16,128,128]{2,1,0...) while((s32[]{:T(128)}, f32[16,128,512]{2,0,1:T(8,128)}, s32[]{:T(128)}, ...), condition=%wide.region_3.4_spmd.clone, body=%wide.region_2.3_spmd.clone.sunk | while | flops 342098464 | bytes 71827784 | solution.py:46
  103.6 0.7 add_compare_fusion.4
  104.2 0.7 fusion.70
  105.0 0.8 subtract_convert_fusion.4
  105.8 0.0 copy-start.3
  105.8 1.3 fusion.71
  107.1 0.8 copy-done.3
  108.0 2.4 add_add_fusion.4
  110.4 0.0 copy-start.4
  110.4 2.0 copy-done.4
  112.4 6.6 %copy.25 = f32[16,128,512]{2,1,0:T(8,128)} copy(f32[16,128,512]{2,0,1:T(8,128)} %get-tuple-element.213) | data formatting | bytes 8388608 | tf_op jit(solution)/shard_map/while | solution.py:46
  119.0 0.0 reduce-scatter.3.cloned.1.call-update
  119.0 0.0 all-gather.2.cloned.1.call-start
  119.0 0.8 dynamic_slice.7
  119.8 0.8 dynamic-slice_convert_fusion
  120.6 75.5 %reduce-scatter.3.cloned.1.call-done = f32[512,512]{1,0:T(8,128)} async-done(((f32[2048,512]{1,0:T(8,128)}), f32[512,512]{1,0:T(8,128)}) %reduce-scatter.3.cloned.1.call-update) | async-done | bytes 1048592 | tf_op jit(solution)/shard_map/reduce_scatter | solution.py:87
  196.1 0.0 copy-done
  196.1 2.6 fusion.34
  198.7 0.0 copy-done.9
  198.7 0.7 fusion.32
  199.4 0.0 copy-start.6
  199.4 1.3 convolution_convert_fusion
  200.6 0.0 all-gather.2.cloned.1.call-update
  200.7 0.0 all-reduce.4.cloned.1.call-start
  200.7 0.3 copy.23
  201.0 0.0 copy-done.6
  201.0 1.5 fusion.35
  202.5 0.0 all-reduce.4.cloned.1.call-update
  202.5 0.2 reduce-scatter.5.cloned.1.call-start
  202.7 42.6 %all-gather.2.cloned.1.call-done = bf16[2048,512]{1,0:T(8,128)(2,1)} async-done(((bf16[512,512]{1,0:T(8,128)(2,1)}), bf16[2048,512]{1,0:T(8,128)(2,1)}) %all-gather.2.cloned.1.call-update) | async-done | bytes 2097168 | tf_op jit(solution)/shard_map/all_gather | solution.py:93
  245.3 2.3 gather_fusion.1
  247.6 4.3 broadcast_in_dim.44
  251.9 12.2 %while.27 = (s32[]{:T(128)}, f32[32,128,512]{2,0,1:T(8,128)}, s32[]{:T(128)}, s32[1,1,16]{2,1,0:T(1,128)S(1)}, s32[]{:T(128)}, /*index=5*/bf16[16,128,128]{1,2,0...) while((s32[]{:T(128)}, f32[32,128,512]{2,0,1:T(8,128)}, s32[]{:T(128)}, ...), condition=%wide.region_7.8_spmd.clone, body=%wide.region_6.7_spmd.clone.sunk | while | flops 411304992 | bytes 113770840 | solution.py:46
  251.9 0.7 add_compare_fusion.5
  252.6 0.7 fusion.77
  253.4 0.0 slice-start
  253.4 0.8 subtract_convert_fusion.5
  254.2 0.0 slice-start.1
  254.2 1.6 fusion.78
  255.8 0.0 slice-done
  255.8 1.2 slice-done.1
  257.0 3.9 add_add_fusion.5
  260.9 3.3 copy-done.2
  264.2 11.5 %copy.26 = f32[32,128,512]{2,1,0:T(8,128)} copy(f32[32,128,512]{2,0,1:T(8,128)} %get-tuple-element.214) | data formatting | bytes 16777216 | tf_op jit(solution)/shard_map/while | solution.py:46
  275.7 0.0 reduce-scatter.5.cloned.1.call-update
  275.8 0.0 copy-start.1
  275.8 103.7 %all-reduce.4.cloned.1.call-done = f32[512,512]{1,0:T(8,128)} async-done(((f32[512,512]{1,0:T(8,128)}), f32[512,512]{1,0:T(8,128)}) %all-reduce.4.cloned.1.call-update) | async-done | bytes 1048592 | tf_op jit(solution)/shard_map/psum | solution.py:95
  379.4 2.3 broadcast_multiply_fusion
  381.7 73.6 %reduce-scatter.5.cloned.1.call-done = f32[512,512]{1,0:T(8,128)} async-done(((f32[4096,512]{1,0:T(8,128)}), f32[512,512]{1,0:T(8,128)}) %reduce-scatter.5.cloned.1.call-update) | async-done | bytes 1048592 | tf_op jit(solution)/shard_map/reduce_scatter | solution.py:99
  455.4 2.1 convert_bitcast_fusion
  (9 shorter events, 0.0 us)
Async XLA Ops:
  7.2 188.9 %copy-start = (bf16[512,512]{1,0:T(8,128)(2,1)S(1)}, bf16[512,512]{1,0:T(8,128)(2,1)}, u32[]{:S(2)}) copy-start(bf16[512,512]{1,0:T(8,128)(2,1)} %param.14) | copy-start | bytes 1572868
  7.2 86.5 %all-reduce.6.cloned.1.call-start = ((), (), s32[]{:S(2)}) async-start(), calls=%async_computation.6 | async-start | bytes 8388608 | tf_op jit(solution)/shard_map/psum | solution.py:11
  11.1 0.7 copy-start.7
  11.1 185.0 %reduce-scatter.3.cloned.1.call-start = ((), (), s32[]{:S(2)}) async-start(), calls=%async_computation.2 | async-start | bytes 5242880 | tf_op jit(solution)/shard_map/reduce_scatter | solution.py:87
  101.0 2.6 copy-start.5
  101.0 2.6 copy-start.8
  105.8 2.2 copy-start.3
  110.4 2.0 copy-start.4
  119.0 126.4 %all-gather.2.cloned.1.call-start = ((), (), s32[]{:S(2)}) async-start(), calls=%async_computation.4 | async-start | bytes 2621440 | tf_op jit(solution)/shard_map/all_gather | solution.py:93
  120.5 78.1 %copy-start.9 = (bf16[8,512]{1,0:T(8,128)(2,1)S(1)}, bf16[8,512]{1,0:T(8,128)(2,1)}, u32[]{:S(2)}) copy-start(bf16[8,512]{1,0:T(8,128)(2,1)} %param.15) | copy-start | bytes 24580
  199.4 1.7 copy-start.6
  200.7 178.8 %all-reduce.4.cloned.1.call-start = ((), (), s32[]{:S(2)}) async-start(), calls=%async_computation.3 | async-start | bytes 2097152 | tf_op jit(solution)/shard_map/psum | solution.py:95
  202.5 252.9 %reduce-scatter.5.cloned.1.call-start = ((), (), s32[]{:S(2)}) async-start(), calls=%async_computation.5 | async-start | bytes 9437184 | tf_op jit(solution)/shard_map/reduce_scatter | solution.py:99
  253.4 2.4 slice-start
  254.2 2.8 slice-start.1
  260.9 3.3 copy-start.2
  275.8 181.7 %copy-start.1 = (bf16[512,512]{1,0:T(8,128)(2,1)S(1)}, bf16[512,512]{1,0:T(8,128)(2,1)}, u32[]{:S(2)}) copy-start(bf16[512,512]{1,0:T(8,128)(2,1)} %param.14) | copy-start | bytes 1572868
Sparse Core Ops, SparseCore 0:
  11.3 82.3 all-reduce.5
  119.1 76.9 reduce-scatter.2
  200.8 44.5 all-gather.1
  250.9 128.4 all-reduce.3
  383.1 72.1 reduce-scatter.4
where the time goes:
time: 466 us; the launch traced here: 464 us
  waiting for transfers between devices  377 us (81%)
  local copies, waits for them, and re-layouts  38.5 us (8%)
  matrix products  16.7 us (4%)
  other arithmetic  16.4 us (4%)
  between operations  14.6 us (3%)
    psum x1, waiting for transfers between devices, per_device(): lax.psum(weight_term, ('row', 'team'))  104 us
    psum x1, waiting for transfers between devices, spread_2(): return lax.psum(kept, axis)  81.8 us
    reduce_scatter x1, waiting for transfers between devices, per_device(): lax.psum_scatter(partial_value, 'team', scatter_dimension=0, tiled=True)  75.5 us
    reduce_scatter x1, waiting for transfers between devices, per_device(): lax.psum_scatter(spread, 'row', scatter_dimension=0, tiled=True)  73.6 us
    all_gather x1, waiting for transfers between devices, per_device(): back_rows = lax.all_gather(back_share, 'team', axis=0, tiled=True)  42.6 us
    while x2, local copies, waits for them, and re-layouts, block_product(): lax.fori_loop(jnp.int32(0), groups, add_group, jnp.zeros((out_blocks, 128...  18.1 us
  transfers between devices with their start and end apart: 5, of which 5 were waited for; matrix products, arithmetic and copies ran while one was open for 7% of the time, Pallas kernels for 0%

commit v1 on v0

v1 whole, which is shorter than its diff:
```python
import functools
import math

import jax
import jax.numpy as jnp
from jax import lax
from jax.experimental import pallas as pl
from jax.experimental.pallas import tpu as pltpu
from jax.sharding import PartitionSpec as P

BLOCK = 128
GROUP = 4
ID_ROWS = 16
MIB = 1 << 20


def lanes(width):
    return -(-width // 128) * 128


def swap(value, axis, flip):
    size = lax.axis_size(axis)
    return lax.ppermute(value, axis, [(i, i ^ flip) for i in range(size)])


def load_ids(ids_vmem, ids_smem, lists, slots, sem):
    for d in range(lists.shape[0]):
        rows = lists[d, slots * BLOCK :, :].astype(jnp.float32)
        ids_vmem[d] = rows.astype(jnp.int32)[:8]
    copy = pltpu.make_async_copy(ids_vmem, ids_smem, sem)
    copy.start()
    copy.wait()


def each_group(ids, place, teams, visit):
    for d in range(teams):
        live = ids[d, 2, 0]

        def step(group, carry, d=d, live=live):
            visit(d, place[0] ^ d, group * GROUP, live)
            return carry

        lax.fori_loop(0, (live + GROUP - 1) // GROUP, step, 0)


def forward_kernel(chips, teams, slots, place, *refs):
    near = refs[:chips]
    far = refs[chips : 2 * chips]
    given = refs[2 * chips : 2 * chips + teams]
    outs = refs[2 * chips + teams : 2 * chips + 2 * teams]
    panels, lists, totals, ids_vmem, ids_smem, sems, id_sem = refs[2 * chips + 2 * teams :]
    slab = near[0].shape[0]
    panel_rows = panels.shape[0] // teams
    share = slab // teams
    team, chip, core = place[0], place[1], place[2]
    copies = []
    for d in range(teams):
        copies.append(pltpu.make_async_copy(given[d], lists.at[d], sems.at[d]))
    for d in range(chips):
        for side, source in ((core, near[d]), (1 - core, far[d])):
            start = pl.multiple_of((2 * (chip ^ d) + side) * slab, slab)
            target = panels.at[pl.ds(start, slab), :]
            copies.append(pltpu.make_async_copy(source, target, sems.at[len(copies)]))
    for copy in copies:
        copy.start()
    totals[...] = jnp.zeros_like(totals)
    for copy in copies[:teams]:
        copy.wait()
    load_ids(ids_vmem, ids_smem, lists, slots, id_sem)
    for copy in copies[teams:]:
        copy.wait()

    def visit(d, panel, first, live):
        products = []
        for u in range(GROUP):
            slot = first + u
            start = panel * panel_rows + ids_smem[d, 1, slot] * BLOCK
            source = panels[pl.ds(pl.multiple_of(start, BLOCK), BLOCK), :]
            block = lists[d, pl.ds(pl.multiple_of(slot * BLOCK, BLOCK), BLOCK), :]
            product = jnp.dot(block, source, preferred_element_type=jnp.float32)
            products.append(jnp.where(slot < live, product, 0.0))
        for u in range(GROUP):
            start = pl.multiple_of(ids_smem[d, 0, first + u] * BLOCK, BLOCK)
            totals[pl.ds(start, BLOCK), :] += products[u]

    each_group(ids_smem, place, teams, visit)
    for d in range(teams):
        start = pl.multiple_of((team ^ d) * share, share)
        outs[d][...] = totals[pl.ds(start, share), :].astype(jnp.bfloat16)


def layer_kernel(teams, place, *refs):
    parts = refs[:teams]
    weight, table, labels, mask = refs[teams : teams + 4]
    output, grad_pre = refs[teams + 4 : teams + 6]
    backs = refs[teams + 6 :]
    team = place[0]
    width = parts[0].shape[1]

    def weight_rows(d):
        return weight[pl.ds(pl.multiple_of((team ^ d) * width, width), width), :]

    preact = jnp.dot(parts[0][...], weight_rows(0), preferred_element_type=jnp.float32)
    for d in range(1, teams):
        preact += jnp.dot(parts[d][...], weight_rows(d), preferred_element_type=jnp.float32)
    sigma = 1.0 / (1.0 + jnp.exp(-preact))
    active = preact * sigma
    output[...] = active.astype(jnp.bfloat16)
    classes = table.shape[0]
    row_labels = labels[pl.ds(team, 1), :]
    row_mask = mask[pl.ds(team, 1), :].astype(jnp.float32)
    rows = row_labels.shape[1]
    index = lax.broadcasted_iota(jnp.int32, (classes, rows), 0)
    known = jnp.where(index == row_labels, row_mask, 0.0).astype(jnp.bfloat16)
    held = jnp.broadcast_to(row_mask * (1.0 / 8.0), (8, rows)).astype(jnp.bfloat16)
    across = (((0,), (0,)), ((), ()))
    target = lax.dot_general(known, table[...], across, preferred_element_type=jnp.float32)
    ones = jnp.ones((8, table.shape[1]), jnp.bfloat16)
    masked = lax.dot_general(held, ones, across, preferred_element_type=jnp.float32)
    slope = sigma * (1.0 + preact * (1.0 - sigma))
    grad = ((masked * active - target) * slope).astype(jnp.bfloat16)
    grad_pre[...] = grad
    for d in range(teams):
        backs[d][...] = lax.dot_general(
            grad, weight_rows(d), (((1,), (1,)), ((), ())), preferred_element_type=jnp.float32
        ).astype(jnp.bfloat16)


def weight_kernel(teams, place, *refs):
    parts = refs[:teams]
    grad_pre, keep, send, term = refs[teams:]
    width = parts[0].shape[1]
    half = keep.shape[0]
    for d in range(teams):
        start = pl.multiple_of((place[0] ^ d) * width, width)
        term[pl.ds(start, width), :] = lax.dot_general(
            parts[d][...], grad_pre[...], (((0,), (0,)), ((), ())), preferred_element_type=jnp.float32
        )
    core = place[2]
    keep[...] = term[pl.ds(pl.multiple_of(core * half, half), half), :]
    send[...] = term[pl.ds(pl.multiple_of((1 - core) * half, half), half), :].astype(jnp.bfloat16)


def backward_kernel(chips, teams, slots, piece, place, *refs):
    given = refs[:teams]
    backs = refs[teams : 2 * teams]
    keep, send, lists, rows, totals, ids_vmem, ids_smem, sems, id_sem = refs[2 * teams :]
    team, core = place[0], place[2]
    share = backs[0].shape[0]
    per_piece = piece // BLOCK
    copies = []
    for d in range(teams):
        copies.append(pltpu.make_async_copy(given[d], lists.at[d], sems.at[d]))
    for d in range(teams):
        start = pl.multiple_of((team ^ d) * share, share)
        target = rows.at[pl.ds(start, share), :]
        copies.append(pltpu.make_async_copy(backs[d], target, sems.at[teams + d]))
    for copy in copies:
        copy.start()
    totals[...] = jnp.zeros_like(totals)
    for copy in copies[:teams]:
        copy.wait()
    load_ids(ids_vmem, ids_smem, lists, slots, id_sem)
    for copy in copies[teams:]:
        copy.wait()

    def visit(d, panel, first, live):
        products = []
        for u in range(GROUP):
            slot = first + u
            start = pl.multiple_of(ids_smem[d, 0, slot] * BLOCK, BLOCK)
            source = rows[pl.ds(start, BLOCK), :]
            block = lists[d, pl.ds(pl.multiple_of(slot * BLOCK, BLOCK), BLOCK), :]
            product = lax.dot_general(
                block, source, (((0,), (0,)), ((), ())), preferred_element_type=jnp.float32
            )
            products.append(jnp.where(slot < live, product, 0.0))
        for u in range(GROUP):
            col = ids_smem[d, 1, first + u]
            owner = col // per_piece
            slot_half = (owner % 2) ^ core
            slot_chip = owner // 2
            start = ((slot_half * chips + slot_chip) * teams + panel) * piece
            start = pl.multiple_of(start + (col % per_piece) * BLOCK, BLOCK)
            totals[pl.ds(start, BLOCK), :] += products[u]

    each_group(ids_smem, place, teams, visit)
    half = totals.shape[0] // 2
    keep[...] = totals[:half, :].astype(jnp.bfloat16)
    send[...] = totals[half:, :].astype(jnp.bfloat16)


def pair_kernel(chips, place, keep, taken, *outs):
    rows = outs[0].shape[0]
    for d in range(chips):
        here = pl.ds(pl.multiple_of((place[1] ^ d) * rows, rows), rows)
        total = keep[here, :].astype(jnp.float32) + taken[here, :].astype(jnp.float32)
        outs[d][...] = total.astype(jnp.bfloat16)


def plane_kernel(chips, teams, place, *refs):
    parts = refs[:chips]
    outs = refs[chips:]
    rows = outs[0].shape[0]
    for d in range(teams):
        here = pl.ds(pl.multiple_of((place[0] ^ d) * rows, rows), rows)
        total = parts[0][here, :].astype(jnp.float32)
        for part in parts[1:]:
            total += part[here, :].astype(jnp.float32)
        outs[d][...] = total.astype(jnp.bfloat16)


def join_kernel(teams, place, *refs):
    parts = refs[:teams]
    out, held = refs[teams:]
    width = parts[0].shape[1]
    for d in range(teams):
        held[place[0] ^ d] = parts[d][...]
    for d in range(teams):
        out[:, d * width : (d + 1) * width] = held[d]


def call(kernel, name, place, operands, spaces, out_shapes, scratch, flops, limit):
    moved = sum(math.prod(x.shape) * x.dtype.itemsize for x in (*operands, *out_shapes))
    specs = [pl.BlockSpec(memory_space=pltpu.SMEM)]
    specs += [pl.BlockSpec(memory_space=space) for space in spaces]
    return pl.pallas_call(
        kernel,
        name=name,
        in_specs=specs,
        out_specs=[pl.BlockSpec(memory_space=pltpu.VMEM) for _ in out_shapes],
        out_shape=out_shapes,
        scratch_shapes=scratch,
        cost_estimate=pl.CostEstimate(flops=flops, bytes_accessed=moved, transcendentals=0),
        compiler_params=pltpu.CompilerParams(vmem_limit_bytes=limit),
    )(place, *operands)


def per_device(
    features, weight, table, labels, label_mask, block_vals, block_row, block_col, block_count
):
    slab, width = features.shape
    slots = block_vals.shape[2]
    rows_n = lax.axis_size("row")
    teams = lax.axis_size("team")
    chips = rows_n // 2
    nodes = slab * rows_n
    part = width // teams
    share = slab // teams
    piece = nodes // teams // rows_n
    team = lax.axis_index("team")
    row = lax.axis_index("row")
    place = jnp.stack([team, row // 2, row % 2]).astype(jnp.int32)
    bf16 = jnp.bfloat16

    def shaped(*dims, kind=bf16):
        return jax.ShapeDtypeStruct(dims, kind)

    ids = jnp.zeros((ID_ROWS, BLOCK), jnp.int32)
    ids = ids.at[0, :slots].set(block_row[0, 0]).at[1, :slots].set(block_col[0, 0])
    ids = ids.at[2, 0].set(block_count[0, 0]).astype(bf16)
    mine = jnp.concatenate([block_vals.reshape(slots * BLOCK, BLOCK), ids], axis=0)
    lists = [mine] + [None] * (teams - 1)
    for d in sorted(range(1, teams), key=lambda d: -d):
        lists[d] = swap(mine, "team", d)
    near = [lax.dynamic_slice_in_dim(features, team * part, part, 1)]
    near += [swap(near[0], "row", 2 * d) for d in range(1, chips)]
    far = [swap(value, "row", 1) for value in near]

    any_space, vmem = pl.ANY, pltpu.VMEM
    padded = lanes(part)
    list_scratch = pltpu.VMEM((teams, slots * BLOCK + ID_ROWS, BLOCK), bf16)
    id_scratch = [
        pltpu.VMEM((teams, 8, BLOCK), jnp.int32),
        pltpu.SMEM((teams, 8, BLOCK), jnp.int32),
    ]
    list_bytes = teams * (slots * BLOCK + ID_ROWS) * BLOCK * 2
    product_flops = 2 * teams * slots * BLOCK * BLOCK * part
    sent = call(
        functools.partial(forward_kernel, chips, teams, slots),
        "forward",
        place,
        [*near, *far, *lists],
        [any_space] * (2 * chips + teams),
        [shaped(share, part)] * teams,
        [
            pltpu.VMEM((nodes, part), bf16),
            list_scratch,
            pltpu.VMEM((slab, part), jnp.float32),
            *id_scratch,
            pltpu.SemaphoreType.DMA((2 * chips + teams,)),
            pltpu.SemaphoreType.DMA,
        ],
        product_flops,
        nodes * padded * 2 + list_bytes + slab * padded * 8 + 4 * MIB,
    )
    aggs = [sent[0]] + [swap(sent[d], "team", d) for d in range(1, teams)]

    output, grad_pre, *backs = call(
        functools.partial(layer_kernel, teams),
        "layer",
        place,
        [*aggs, weight, table, labels.reshape(teams, share), label_mask.reshape(teams, share)],
        [vmem] * (teams + 4),
        [shaped(share, width)] * 2 + [shaped(share, part)] * teams,
        [],
        4 * share * width * width,
        16 * MIB,
    )
    backs = [backs[0]] + [swap(backs[d], "team", d) for d in range(1, teams)]

    half = width // 2
    w_keep, w_send = call(
        functools.partial(weight_kernel, teams),
        "weight_term",
        place,
        [*aggs, grad_pre],
        [vmem] * (teams + 1),
        [shaped(half, width, kind=jnp.float32), shaped(half, width)],
        [pltpu.VMEM((width, width), jnp.float32)],
        2 * share * width * width,
        12 * MIB,
    )
    w_pair = (w_keep + swap(w_send, "row", 1).astype(jnp.float32)).astype(bf16)
    w_rows = half // chips
    w_pieces = [
        lax.dynamic_slice_in_dim(w_pair, ((row // 2) ^ d) * w_rows, w_rows, 0) for d in range(chips)
    ]
    w_plane = w_pieces[0].astype(jnp.float32)
    for d in range(1, chips):
        w_plane = w_plane + swap(w_pieces[d], "row", 2 * d).astype(jnp.float32)
    w_plane = w_plane.astype(bf16)
    w_total = w_plane.astype(jnp.float32)
    for d in range(1, teams):
        w_total = w_total + swap(w_plane, "team", d).astype(jnp.float32)
    w_total = w_total * (1.0 / math.sqrt(nodes))
    w_half = jnp.zeros((half, width), jnp.float32)
    for d in range(chips):
        taken = swap(w_total, "row", 2 * d) if d else w_total
        w_half = lax.dynamic_update_slice_in_dim(w_half, taken, ((row // 2) ^ d) * w_rows, 0)
    w_other = swap(w_half, "row", 1)
    first = row % 2 == 0
    grad_weight = jnp.concatenate(
        [jnp.where(first, w_half, w_other), jnp.where(first, w_other, w_half)], axis=0
    )

    half_rows = nodes // 2
    keep, send = call(
        functools.partial(backward_kernel, chips, teams, slots, piece),
        "backward",
        place,
        [*lists, *backs],
        [any_space] * (2 * teams),
        [shaped(half_rows, part)] * 2,
        [
            list_scratch,
            pltpu.VMEM((slab, part), bf16),
            pltpu.VMEM((nodes, part), jnp.float32),
            *id_scratch,
            pltpu.SemaphoreType.DMA((2 * teams,)),
            pltpu.SemaphoreType.DMA,
        ],
        product_flops,
        nodes * padded * 6 + list_bytes + slab * padded * 2 + 4 * MIB,
    )
    pieces = call(
        functools.partial(pair_kernel, chips),
        "pair_sum",
        place,
        [keep, swap(send, "row", 1)],
        [vmem] * 2,
        [shaped(teams * piece, part)] * chips,
        [],
        half_rows * part,
        half_rows * padded * 6 + 4 * MIB,
    )
    parts = [pieces[0]] + [swap(pieces[d], "row", 2 * d) for d in range(1, chips)]
    slices = call(
        functools.partial(plane_kernel, chips, teams),
        "plane_sum",
        place,
        parts,
        [vmem] * chips,
        [shaped(piece, part)] * teams,
        [],
        half_rows * part,
        half_rows * padded * 4 + 4 * MIB,
    )
    taken = [slices[0]] + [swap(slices[d], "team", d) for d in range(1, teams)]
    (grad_features,) = call(
        functools.partial(join_kernel, teams),
        "join",
        place,
        taken,
        [vmem] * teams,
        [shaped(piece, width)],
        [pltpu.VMEM((teams, piece, part), bf16)],
        piece * width,
        teams * piece * padded * 8 + 4 * MIB,
    )
    return (output, grad_weight, grad_features[None])


def solution(mesh):
    placed = (
        P("row", None),
        P(),
        P(),
        P("row"),
        P("row"),
        P("row", "team", None, None, None),
        P("row", "team", None),
        P("row", "team", None),
        P("row", "team"),
    )
    return jax.shard_map(
        per_device,
        mesh=mesh,
        in_specs=placed,
        out_specs=(P(("row", "team"), None), P(), P("team", "row", None)),
        check_vma=False,
    )
```

time: 466 us -> 184 us (0.39)
  waiting for transfers between devices: 377 us -> 107 us
  starting transfers between devices: 0.39 us -> 32.5 us
  local copies, waits for them, and re-layouts: 38.5 us -> 13.9 us
  Pallas kernels: 0 us -> 22 us
  matrix products: 16.7 us -> 0 us
  between operations: 14.6 us -> 1.47 us
  other arithmetic: 16.4 us -> 4.3 us
    psum x2 -> x0, waiting for transfers between devices: 185 us -> none  [the longest x1 104 us: per_device(): lax.psum(weight_term, ('row', 'team'))]
    reduce_scatter x2 -> x0, waiting for transfers between devices: 149 us -> none  [the longest x1 75.5 us: per_device(): lax.psum_scatter(partial_value, 'team', scatter_dimension=0, tiled=True)]
    ppermute x0 -> x34, waiting for transfers between devices: none -> 107 us  [swap(): return lax.ppermute(value, axis, [(i, i ^ flip) for i in range(size)])]
    all_gather x1 -> x0, waiting for transfers between devices: 42.6 us -> none  [per_device(): back_rows = lax.all_gather(back_share, 'team', axis=0, tiled=True)]
    ppermute x0 -> x34, starting transfers between devices: none -> 32.5 us  [swap(): return lax.ppermute(value, axis, [(i, i ^ flip) for i in range(size)])]
    while x12 -> x0, local copies, waits for them, and re-layouts: 25.4 us -> none  [the longest x2 18.1 us: block_product(): lax.fori_loop(jnp.int32(0), groups, add_group, jnp.zeros((out_blocks, 128...]
    pallas_call x0 -> x7, Pallas kernels: none -> 22 us  [call(): pl.pallas_call(kernel, name=name, in_specs=specs, out_specs=[pl.BlockSpec...]
    dot_general x10 -> x0, matrix products: 16.7 us -> none  [the longest x2 6.28 us: add_group(): jnp.einsum('sk,kif->sif', selector, lower, preferred_element_type=jnp.flo...]
  transfers between devices with their start and end apart: 5 -> 34, of which waited for: 5 -> 24; matrix products, arithmetic and copies ran while one was open for 7% -> 6% of each run, Pallas kernels for 0% -> 2%
where the time goes in v1:
time: 184 us; the launch traced here: 181 us
  waiting for transfers between devices  107 us (58%)
  starting transfers between devices  32.5 us (18%)
  Pallas kernels  22 us (12%)
  local copies, waits for them, and re-layouts  13.9 us (8%)
  other arithmetic  4.3 us (2%)
    ppermute x34, waiting for transfers between devices, swap(): return lax.ppermute(value, axis, [(i, i ^ flip) for i in range(size)])  107 us
    ppermute x34, starting transfers between devices, swap(): return lax.ppermute(value, axis, [(i, i ^ flip) for i in range(size)])  32.5 us
    pallas_call x7, Pallas kernels, call(): pl.pallas_call(kernel, name=name, in_specs=specs, out_specs=[pl.BlockSpec...  22 us
    unnamed x14, local copies, waits for them, and re-layouts  6.07 us
  transfers between devices with their start and end apart: 34, of which 24 were waited for; matrix products, arithmetic and copies ran while one was open for 6% of the time, Pallas kernels for 2%

profile of v1, /device:TPU:9, one launch (start us, length us, event | category | flops | bytes accessed | tf_op | source)
XLA Modules:
  0.0 180.8 jit_solution(9671180391865637325)
XLA Ops:
  0.6 1.6 copy-done
  2.2 0.9 constant_dynamic-slice_fusion.3.refs_0_
  3.1 0.7 collective-permute-start.3
  3.8 2.2 %collective-permute-start.2 = (bf16[2048,128]{1,0:T(8,128)(2,1)}, bf16[2048,128]{1,0:T(8,128)(2,1)}, u32[]{:S(2)}, u32[]{:S(2)}) collective-permute-start(bf16[2048,128]{1,0:T(8,128)(2,1)} %constant_dynamic-slice_fusion.3.refs_0_), channel_id=1, source_target_pairs={{0,24},{4,28},{8,16},{12,20},{16,8},{20,12},{24,0},{28,4},{1,25},{... | collective-permute-start | bytes 1572872 | tf_op jit(solution)/shard_map/ppermute | solution.py:23
  7.2 0.7 scatter.11
  8.1 1.1 pad_maximum_fusion.1.refs_8_.refs_0_
  9.2 1.4 collective-permute-start.9
  11.0 1.1 collective-permute-start.8
  12.1 6.5 %collective-permute-done.2.refs_3_ = bf16[2048,128]{1,0:T(8,128)(2,1)} collective-permute-done((bf16[2048,128]{1,0:T(8,128)(2,1)}, bf16[2048,128]{1,0:T(8,128)(2,1)}, u32[]{:S(2)}, u32[]{:S(2)}) %collective-permute-start.2) | collective-permute-done | bytes 524320 | tf_op jit(solution)/shard_map/ppermute | solution.py:23
  18.8 11.3 %collective-permute-done.1.refs_2_ = bf16[2048,128]{1,0:T(8,128)(2,1)} collective-permute-done((bf16[2048,128]{1,0:T(8,128)(2,1)}, bf16[2048,128]{1,0:T(8,128)(2,1)}, u32[]{:S(2)}, u32[]{:S(2)}) %collective-permute-start.1) | collective-permute-done | bytes 524320 | tf_op jit(solution)/shard_map/ppermute | solution.py:23
  30.7 14.7 %collective-permute-done.9.refs_11_.refs_3_ = bf16[2064,128]{1,0:T(8,128)(2,1)S(1)} collective-permute-done((bf16[2064,128]{1,0:T(8,128)(2,1)S(1)}, bf16[2064,128]{1,0:T(8,128)(2,1)S(1)}, u32[]{:S(2)}, u32[]{:S(2)}) %collective-permute-start.9) | collective-permute-done | bytes 528416 | tf_op jit(solution)/shard_map/ppermute | solution.py:23
  45.3 1.7 collective-permute-start.4
  47.1 8.5 %collective-permute-done.8.refs_10_.refs_2_ = bf16[2064,128]{1,0:T(8,128)(2,1)} collective-permute-done((bf16[2064,128]{1,0:T(8,128)(2,1)S(1)}, bf16[2064,128]{1,0:T(8,128)(2,1)}, u32[]{:S(2)}, u32[]{:S(2)}) %collective-permute-start.8) | collective-permute-done | bytes 528416 | tf_op jit(solution)/shard_map/ppermute | solution.py:23
  55.6 5.5 %forward.1 = (bf16[512,128]{1,0:T(8,128)(2,1)S(1)}, bf16[512,128]{1,0:T(8,128)(2,1)}, bf16[512,128]{1,0:T(8,128)(2,1)}, bf16[512,128]{1,0:T(8,128)(2,1)}) custom-call(s32[3]{0:T(128)S(1)} %pad_add_fusion.place, bf16[2048,128]{1,0:T(8,128)(2,1)} %constant_dynamic-slice_fusion.3.refs_0_, bf16[2048,128]{1,0:T(8,128)(2,1)} %collective-permute-done.refs_1_, ...), custom_call_target="tpu_custom_call" | custom-call | flops 268435456 | bytes 6832128 | tf_op jit(solution)/shard_map/forward/pallas_call | solution.py:227
  61.2 2.3 %collective-permute-start.10 = (bf16[512,128]{1,0:T(8,128)(2,1)}, bf16[512,128]{1,0:T(8,128)(2,1)S(1)}, u32[]{:S(2)}, u32[]{:S(2)}) collective-permute-start(bf16[512,128]{1,0:T(8,128)(2,1)} %get-tuple-element.62), channel_id=1, source_target_pairs={{0,1},{1,0},{2,3},{3,2},{4,5},{5,4},{6,7},{7,6},{8,9},{9,8},{10,11... | collective-permute-start | bytes 393224 | tf_op jit(solution)/shard_map/ppermute | solution.py:23
  63.4 1.1 collective-permute-start.11
  64.7 1.3 reshape.108.refs_6_
  66.0 1.3 reshape.109.refs_7_
  67.3 3.1 %collective-permute-done.11.refs_2_ = bf16[512,128]{1,0:T(8,128)(2,1)S(1)} collective-permute-done((bf16[512,128]{1,0:T(8,128)(2,1)}, bf16[512,128]{1,0:T(8,128)(2,1)S(1)}, u32[]{:S(2)}, u32[]{:S(2)}) %collective-permute-start.11) | collective-permute-done | bytes 131104 | tf_op jit(solution)/shard_map/ppermute | solution.py:23
  70.4 5.8 %collective-permute-done.12.refs_3_ = bf16[512,128]{1,0:T(8,128)(2,1)} collective-permute-done((bf16[512,128]{1,0:T(8,128)(2,1)}, bf16[512,128]{1,0:T(8,128)(2,1)}, u32[]{:S(2)}, u32[]{:S(2)}) %collective-permute-start.12) | collective-permute-done | bytes 131104 | tf_op jit(solution)/shard_map/ppermute | solution.py:23
  76.2 0.7 copy-done.3
  76.9 0.7 copy-done.4
  77.6 1.0 copy-done.5
  78.6 0.7 copy-done.6
  79.3 2.8 %layer.1 = (bf16[512,512]{1,0:T(8,128)(2,1)}, bf16[512,512]{1,0:T(8,128)(2,1)S(1)}, bf16[512,128]{1,0:T(8,128)(2,1)S(1)}, bf16[512,128]{1,0:T(8,128)(2,1)S(1)}, ...) custom-call(s32[3]{0:T(128)S(1)} %pad_add_fusion.place, bf16[512,128]{1,0:T(8,128)(2,1)S(1)} %get-tuple-element.61.refs_0_, ...), custom_call_target="tpu_custom_call" | custom-call | flops 536870912 | bytes 2646016 | tf_op jit(solution)/shard_map/layer/pallas_call | solution.py:227
  82.1 2.5 %collective-permute-start.25 = (bf16[512,128]{1,0:T(8,128)(2,1)S(1)}, bf16[512,128]{1,0:T(8,128)(2,1)S(1)}, u32[]{:S(2)}, u32[]{:S(2)}) collective-permute-start(bf16[512,128]{1,0:T(8,128)(2,1)S(1)} %get-tuple-element.71), channel_id=1, source_target_pairs={{0,2},{1,3},{2,0},{3,1},{4,6},{5,7},{6,4},{7,5},{8,10},{9,11},{10,... | collective-permute-start | bytes 393224 | tf_op jit(solution)/shard_map/ppermute | solution.py:23
  84.7 1.2 collective-permute-done.24.refs_5_
  85.9 6.7 %collective-permute-done.25.refs_6_ = bf16[512,128]{1,0:T(8,128)(2,1)S(1)} collective-permute-done((bf16[512,128]{1,0:T(8,128)(2,1)S(1)}, bf16[512,128]{1,0:T(8,128)(2,1)S(1)}, u32[]{:S(2)}, u32[]{:S(2)}) %collective-permute-start.25) | collective-permute-done | bytes 131104 | tf_op jit(solution)/shard_map/ppermute | solution.py:23
  92.6 3.0 %collective-permute-done.26.refs_7_ = bf16[512,128]{1,0:T(8,128)(2,1)S(1)} collective-permute-done((bf16[512,128]{1,0:T(8,128)(2,1)S(1)}, bf16[512,128]{1,0:T(8,128)(2,1)S(1)}, u32[]{:S(2)}, u32[]{:S(2)}) %collective-permute-start.26) | collective-permute-done | bytes 131104 | tf_op jit(solution)/shard_map/ppermute | solution.py:23
  95.5 6.2 %backward.1 = (bf16[8192,128]{1,0:T(8,128)(2,1)S(1)}, bf16[8192,128]{1,0:T(8,128)(2,1)}) custom-call(s32[3]{0:T(128)S(1)} %pad_add_fusion.place, bf16[2064,128]{1,0:T(8,128)(2,1)S(1)} %pad_maximum_fusion.1.refs_8_.refs_0_, bf16[2064,128]{1,0:T(8,128)(2,1)} %collective-permute-done.7.refs_9_.refs_1_, ...), custom_call_target="tpu_custom_call" | custom-call | flops 268435456 | bytes 6832128 | tf_op jit(solution)/shard_map/backward/pallas_call | solution.py:227
  101.8 1.3 copy-done.1
  103.2 1.9 %collective-permute-start.27 = (bf16[8192,128]{1,0:T(8,128)(2,1)}, bf16[8192,128]{1,0:T(8,128)(2,1)}, u32[]{:S(2)}, u32[]{:S(2)}) collective-permute-start(bf16[8192,128]{1,0:T(8,128)(2,1)} %get-tuple-element.74), channel_id=1, source_target_pairs={{0,4},{4,0},{8,12},{12,8},{16,20},{20,16},{24,28},{28,24},{1,5},{5... | collective-permute-start | bytes 6291464 | tf_op jit(solution)/shard_map/ppermute | solution.py:23
  105.0 1.5 weight_term.1
  106.6 2.6 %collective-permute-done.13 = bf16[256,512]{1,0:T(8,128)(2,1)S(1)} collective-permute-done((bf16[256,512]{1,0:T(8,128)(2,1)S(1)}, bf16[256,512]{1,0:T(8,128)(2,1)S(1)}, u32[]{:S(2)}, u32[]{:S(2)}) %collective-permute-start.13) | collective-permute-done | bytes 262176 | tf_op jit(solution)/shard_map/ppermute | solution.py:23
  109.4 1.9 %collective-permute-start.16 = (bf16[64,512]{1,0:T(8,128)(2,1)S(1)}, bf16[64,512]{1,0:T(8,128)(2,1)S(1)}, u32[]{:S(2)}, u32[]{:S(2)}) collective-permute-start(bf16[64,512]{1,0:T(8,128)(2,1)S(1)} %get-tuple-element.88), channel_id=1, source_target_pairs={{0,24},{4,28},{8,16},{12,20},{16,8},{20,12},{24,0},{28,4},{1,25},{... | collective-permute-start | bytes 196616 | tf_op jit(solution)/shard_map/ppermute | solution.py:23
  111.3 0.8 collective-permute-start.15
  112.5 1.7 collective-permute-done.16
  114.2 1.6 collective-permute-done.15
  115.9 1.3 collective-permute-start.19
  117.7 0.9 collective-permute-start.17
  118.6 1.2 collective-permute-done.19
  119.7 2.5 %collective-permute-done.18 = bf16[64,512]{1,0:T(8,128)(2,1)S(1)} collective-permute-done((bf16[64,512]{1,0:T(8,128)(2,1)S(1)}, bf16[64,512]{1,0:T(8,128)(2,1)S(1)}, u32[]{:S(2)}, u32[]{:S(2)}) %collective-permute-start.18) | collective-permute-done | bytes 65568 | tf_op jit(solution)/shard_map/ppermute | solution.py:23
  122.4 0.9 broadcast_in_dim.7
  123.2 0.7 constant_dynamic-update-slice_fusion.3
  124.2 1.4 collective-permute-start.21
  125.6 1.0 collective-permute-start.22
  126.6 1.2 collective-permute-done.20
  128.4 0.7 constant_dynamic-update-slice_fusion.1
  129.1 2.9 %collective-permute-done.22 = f32[64,512]{1,0:T(8,128)S(1)} collective-permute-done((f32[64,512]{1,0:T(8,128)S(1)}, f32[64,512]{1,0:T(8,128)S(1)}, u32[]{:S(2)}, u32[]{:S(2)}) %collective-permute-start.22) | collective-permute-done | bytes 131104 | tf_op jit(solution)/shard_map/ppermute | solution.py:23
  132.7 1.7 collective-permute-start.23
  134.5 3.1 %pair_sum.1 = (bf16[2048,128]{1,0:T(8,128)(2,1)S(1)}, bf16[2048,128]{1,0:T(8,128)(2,1)}, bf16[2048,128]{1,0:T(8,128)(2,1)}, bf16[2048,128]{1,0:T(8,128)(2,1)}) custom-call(s32[3]{0:T(128)S(1)} %pad_add_fusion.place, bf16[8192,128]{1,0:T(8,128)(2,1)S(1)} %copy-done.2, bf16[8192,128]{1,0:T(8,128)(2,1)} %collective-permute-done.27.taken), custom_call_target="tpu_custom_call" | custom-call | flops 1048576 | bytes 6291456 | tf_op jit(solution)/shard_map/pair_sum/pallas_call | solution.py:227
  137.5 1.7 collective-permute-start.28
  140.4 1.3 broadcast_select_fusion.1
  141.7 10.0 %collective-permute-done.28.refs_1_ = bf16[2048,128]{1,0:T(8,128)(2,1)S(1)} collective-permute-done((bf16[2048,128]{1,0:T(8,128)(2,1)}, bf16[2048,128]{1,0:T(8,128)(2,1)S(1)}, u32[]{:S(2)}, u32[]{:S(2)}) %collective-permute-start.28) | collective-permute-done | bytes 524320 | tf_op jit(solution)/shard_map/ppermute | solution.py:23
  151.7 1.4 collective-permute-done.29.refs_2_
  153.1 10.5 %collective-permute-done.30.refs_3_ = bf16[2048,128]{1,0:T(8,128)(2,1)} collective-permute-done((bf16[2048,128]{1,0:T(8,128)(2,1)}, bf16[2048,128]{1,0:T(8,128)(2,1)}, u32[]{:S(2)}, u32[]{:S(2)}) %collective-permute-start.30) | collective-permute-done | bytes 524320 | tf_op jit(solution)/shard_map/ppermute | solution.py:23
  163.6 1.5 plane_sum.1
  165.1 2.1 %collective-permute-start.31 = (bf16[512,128]{1,0:T(8,128)(2,1)S(1)}, bf16[512,128]{1,0:T(8,128)(2,1)S(1)}, u32[]{:S(2)}, u32[]{:S(2)}) collective-permute-start(bf16[512,128]{1,0:T(8,128)(2,1)S(1)} %get-tuple-element.80), channel_id=1, source_target_pairs={{0,1},{1,0},{2,3},{3,2},{4,5},{5,4},{6,7},{7,6},{8,9},{9,8},{10,11... | collective-permute-start | bytes 393224 | tf_op jit(solution)/shard_map/ppermute | solution.py:23
  167.2 1.1 collective-permute-start.32
  168.5 1.0 pad_maximum_fusion
  169.6 0.9 collective-permute-done.31.refs_1_
  170.4 2.9 %collective-permute-done.32.refs_2_ = bf16[512,128]{1,0:T(8,128)(2,1)S(1)} collective-permute-done((bf16[512,128]{1,0:T(8,128)(2,1)S(1)}, bf16[512,128]{1,0:T(8,128)(2,1)S(1)}, u32[]{:S(2)}, u32[]{:S(2)}) %collective-permute-start.32) | collective-permute-done | bytes 131104 | tf_op jit(solution)/shard_map/ppermute | solution.py:23
  173.4 5.9 %collective-permute-done.33.refs_3_ = bf16[512,128]{1,0:T(8,128)(2,1)S(1)} collective-permute-done((bf16[512,128]{1,0:T(8,128)(2,1)S(1)}, bf16[512,128]{1,0:T(8,128)(2,1)S(1)}, u32[]{:S(2)}, u32[]{:S(2)}) %collective-permute-start.33) | collective-permute-done | bytes 131104 | tf_op jit(solution)/shard_map/ppermute | solution.py:23
  179.3 1.5 join.1
  (44 shorter events, 6.8 us)
Async XLA Ops:
  0.6 1.6 copy-start
  3.1 7.9 %collective-permute-start.3 = (bf16[2048,128]{1,0:T(8,128)(2,1)}, bf16[2048,128]{1,0:T(8,128)(2,1)}, u32[]{:S(2)}, u32[]{:S(2)}) collective-permute-start(bf16[2048,128]{1,0:T(8,128)(2,1)} %constant_dynamic-slice_fusion.3.refs_0_), channel_id=1, source_target_pairs={{0,4},{4,0},{8,12},{12,8},{16,20},{20,16},{24,28},{28,24},{1,5},{5... | collective-permute-start | bytes 1572872 | tf_op jit(solution)/shard_map/ppermute | solution.py:23
  3.8 14.8 %collective-permute-start.2 = (bf16[2048,128]{1,0:T(8,128)(2,1)}, bf16[2048,128]{1,0:T(8,128)(2,1)}, u32[]{:S(2)}, u32[]{:S(2)}) collective-permute-start(bf16[2048,128]{1,0:T(8,128)(2,1)} %constant_dynamic-slice_fusion.3.refs_0_), channel_id=1, source_target_pairs={{0,24},{4,28},{8,16},{12,20},{16,8},{20,12},{24,0},{28,4},{1,25},{... | collective-permute-start | bytes 1572872 | tf_op jit(solution)/shard_map/ppermute | solution.py:23
  9.2 36.1 %collective-permute-start.9 = (bf16[2064,128]{1,0:T(8,128)(2,1)S(1)}, bf16[2064,128]{1,0:T(8,128)(2,1)S(1)}, u32[]{:S(2)}, u32[]{:S(2)}) collective-permute-start(bf16[2064,128]{1,0:T(8,128)(2,1)S(1)} %pad_maximum_fusion.1.refs_8_.refs_0_), channel_id=1, source_target_pairs={{0,3},{1,2},{2,1},{3,0},{4,7},{5,6},{6,5},{7,4},{8,11},{9,10},{10,... | collective-permute-start | bytes 1585160 | tf_op jit(solution)/shard_map/ppermute | solution.py:23
  10.5 19.5 %collective-permute-start.1 = (bf16[2048,128]{1,0:T(8,128)(2,1)}, bf16[2048,128]{1,0:T(8,128)(2,1)}, u32[]{:S(2)}, u32[]{:S(2)}) collective-permute-start(bf16[2048,128]{1,0:T(8,128)(2,1)} %constant_dynamic-slice_fusion.3.refs_0_), channel_id=1, source_target_pairs={{0,16},{4,20},{8,24},{12,28},{16,0},{20,4},{24,8},{28,12},{1,17},{... | collective-permute-start | bytes 1572872 | tf_op jit(solution)/shard_map/ppermute | solution.py:23
  10.8 19.8 %collective-permute-start = (bf16[2048,128]{1,0:T(8,128)(2,1)}, bf16[2048,128]{1,0:T(8,128)(2,1)}, u32[]{:S(2)}, u32[]{:S(2)}) collective-permute-start(bf16[2048,128]{1,0:T(8,128)(2,1)} %constant_dynamic-slice_fusion.3.refs_0_), channel_id=1, source_target_pairs={{0,8},{4,12},{8,0},{12,4},{16,24},{20,28},{24,16},{28,20},{1,9},{5... | collective-permute-start | bytes 1572872 | tf_op jit(solution)/shard_map/ppermute | solution.py:23
  11.0 44.6 %collective-permute-start.8 = (bf16[2064,128]{1,0:T(8,128)(2,1)S(1)}, bf16[2064,128]{1,0:T(8,128)(2,1)}, u32[]{:S(2)}, u32[]{:S(2)}) collective-permute-start(bf16[2064,128]{1,0:T(8,128)(2,1)S(1)} %pad_maximum_fusion.1.refs_8_.refs_0_), channel_id=1, source_target_pairs={{0,2},{1,3},{2,0},{3,1},{4,6},{5,7},{6,4},{7,5},{8,10},{9,11},{10,... | collective-permute-start | bytes 1585160 | tf_op jit(solution)/shard_map/ppermute | solution.py:23
  18.6 37.0 %collective-permute-start.7 = (bf16[2064,128]{1,0:T(8,128)(2,1)S(1)}, bf16[2064,128]{1,0:T(8,128)(2,1)}, u32[]{:S(2)}, u32[]{:S(2)}) collective-permute-start(bf16[2064,128]{1,0:T(8,128)(2,1)S(1)} %pad_maximum_fusion.1.refs_8_.refs_0_), channel_id=1, source_target_pairs={{0,1},{1,0},{2,3},{3,2},{4,5},{5,4},{6,7},{7,6},{8,9},{9,8},{10,11... | collective-permute-start | bytes 1585160 | tf_op jit(solution)/shard_map/ppermute | solution.py:23
  30.1 25.6 %collective-permute-start.6 = (bf16[2048,128]{1,0:T(8,128)(2,1)}, bf16[2048,128]{1,0:T(8,128)(2,1)}, u32[]{:S(2)}, u32[]{:S(2)}) collective-permute-start(bf16[2048,128]{1,0:T(8,128)(2,1)} %collective-permute-done.2.refs_3_), channel_id=1, source_target_pairs={{0,4},{4,0},{8,12},{12,8},{16,20},{20,16},{24,28},{28,24},{1,5},{5... | collective-permute-start | bytes 1572872 | tf_op jit(solution)/shard_map/ppermute | solution.py:23
  30.6 25.1 %collective-permute-start.5 = (bf16[2048,128]{1,0:T(8,128)(2,1)}, bf16[2048,128]{1,0:T(8,128)(2,1)}, u32[]{:S(2)}, u32[]{:S(2)}) collective-permute-start(bf16[2048,128]{1,0:T(8,128)(2,1)} %collective-permute-done.1.refs_2_), channel_id=1, source_target_pairs={{0,4},{4,0},{8,12},{12,8},{16,20},{20,16},{24,28},{28,24},{1,5},{5... | collective-permute-start | bytes 1572872 | tf_op jit(solution)/shard_map/ppermute | solution.py:23
  45.3 10.3 %collective-permute-start.4 = (bf16[2048,128]{1,0:T(8,128)(2,1)}, bf16[2048,128]{1,0:T(8,128)(2,1)}, u32[]{:S(2)}, u32[]{:S(2)}) collective-permute-start(bf16[2048,128]{1,0:T(8,128)(2,1)} %collective-permute-done.refs_1_), channel_id=1, source_target_pairs={{0,4},{4,0},{8,12},{12,8},{16,20},{20,16},{24,28},{28,24},{1,5},{5... | collective-permute-start | bytes 1572872 | tf_op jit(solution)/shard_map/ppermute | solution.py:23
  61.2 6.2 %collective-permute-start.10 = (bf16[512,128]{1,0:T(8,128)(2,1)}, bf16[512,128]{1,0:T(8,128)(2,1)S(1)}, u32[]{:S(2)}, u32[]{:S(2)}) collective-permute-start(bf16[512,128]{1,0:T(8,128)(2,1)} %get-tuple-element.62), channel_id=1, source_target_pairs={{0,1},{1,0},{2,3},{3,2},{4,5},{5,4},{6,7},{7,6},{8,9},{9,8},{10,11... | collective-permute-start | bytes 393224 | tf_op jit(solution)/shard_map/ppermute | solution.py:23
  63.4 7.0 %collective-permute-start.11 = (bf16[512,128]{1,0:T(8,128)(2,1)}, bf16[512,128]{1,0:T(8,128)(2,1)S(1)}, u32[]{:S(2)}, u32[]{:S(2)}) collective-permute-start(bf16[512,128]{1,0:T(8,128)(2,1)} %get-tuple-element.63), channel_id=1, source_target_pairs={{0,2},{1,3},{2,0},{3,1},{4,6},{5,7},{6,4},{7,5},{8,10},{9,11},{10,... | collective-permute-start | bytes 393224 | tf_op jit(solution)/shard_map/ppermute | solution.py:23
  64.5 11.7 %collective-permute-start.12 = (bf16[512,128]{1,0:T(8,128)(2,1)}, bf16[512,128]{1,0:T(8,128)(2,1)}, u32[]{:S(2)}, u32[]{:S(2)}) collective-permute-start(bf16[512,128]{1,0:T(8,128)(2,1)} %get-tuple-element.64), channel_id=1, source_target_pairs={{0,3},{1,2},{2,1},{3,0},{4,7},{5,6},{6,5},{7,4},{8,11},{9,10},{10,... | collective-permute-start | bytes 393224 | tf_op jit(solution)/shard_map/ppermute | solution.py:23
  76.2 0.7 copy-start.3
  76.9 0.7 copy-start.4
  77.6 1.0 copy-start.5
  78.6 0.7 copy-start.6
  82.1 3.8 %collective-permute-start.24 = (bf16[512,128]{1,0:T(8,128)(2,1)S(1)}, bf16[512,128]{1,0:T(8,128)(2,1)S(1)}, u32[]{:S(2)}, u32[]{:S(2)}) collective-permute-start(bf16[512,128]{1,0:T(8,128)(2,1)S(1)} %get-tuple-element.70), channel_id=1, source_target_pairs={{0,1},{1,0},{2,3},{3,2},{4,5},{5,4},{6,7},{7,6},{8,9},{9,8},{10,11... | collective-permute-start | bytes 393224 | tf_op jit(solution)/shard_map/ppermute | solution.py:23
  82.1 10.5 %collective-permute-start.25 = (bf16[512,128]{1,0:T(8,128)(2,1)S(1)}, bf16[512,128]{1,0:T(8,128)(2,1)S(1)}, u32[]{:S(2)}, u32[]{:S(2)}) collective-permute-start(bf16[512,128]{1,0:T(8,128)(2,1)S(1)} %get-tuple-element.71), channel_id=1, source_target_pairs={{0,2},{1,3},{2,0},{3,1},{4,6},{5,7},{6,4},{7,5},{8,10},{9,11},{10,... | collective-permute-start | bytes 393224 | tf_op jit(solution)/shard_map/ppermute | solution.py:23
  84.6 10.9 %collective-permute-start.26 = (bf16[512,128]{1,0:T(8,128)(2,1)S(1)}, bf16[512,128]{1,0:T(8,128)(2,1)S(1)}, u32[]{:S(2)}, u32[]{:S(2)}) collective-permute-start(bf16[512,128]{1,0:T(8,128)(2,1)S(1)} %get-tuple-element.72), channel_id=1, source_target_pairs={{0,3},{1,2},{2,1},{3,0},{4,7},{5,6},{6,5},{7,4},{8,11},{9,10},{10,... | collective-permute-start | bytes 393224 | tf_op jit(solution)/shard_map/ppermute | solution.py:23
  101.8 1.4 copy-start.1
  103.2 31.3 %collective-permute-start.27 = (bf16[8192,128]{1,0:T(8,128)(2,1)}, bf16[8192,128]{1,0:T(8,128)(2,1)}, u32[]{:S(2)}, u32[]{:S(2)}) collective-permute-start(bf16[8192,128]{1,0:T(8,128)(2,1)} %get-tuple-element.74), channel_id=1, source_target_pairs={{0,4},{4,0},{8,12},{12,8},{16,20},{20,16},{24,28},{28,24},{1,5},{5... | collective-permute-start | bytes 6291464 | tf_op jit(solution)/shard_map/ppermute | solution.py:23
  106.5 2.7 %collective-permute-start.13 = (bf16[256,512]{1,0:T(8,128)(2,1)S(1)}, bf16[256,512]{1,0:T(8,128)(2,1)S(1)}, u32[]{:S(2)}, u32[]{:S(2)}) collective-permute-start(bf16[256,512]{1,0:T(8,128)(2,1)S(1)} %get-tuple-element.68), channel_id=1, source_target_pairs={{0,4},{4,0},{8,12},{12,8},{16,20},{20,16},{24,28},{28,24},{1,5},{5... | collective-permute-start | bytes 786440 | tf_op jit(solution)/shard_map/ppermute | solution.py:23
  109.3 3.2 %collective-permute-start.14 = (bf16[64,512]{1,0:T(8,128)(2,1)S(1)}, bf16[64,512]{1,0:T(8,128)(2,1)S(1)}, u32[]{:S(2)}, u32[]{:S(2)}) collective-permute-start(bf16[64,512]{1,0:T(8,128)(2,1)S(1)} %get-tuple-element.87), channel_id=1, source_target_pairs={{0,8},{4,12},{8,0},{12,4},{16,24},{20,28},{24,16},{28,20},{1,9},{5... | collective-permute-start | bytes 196616 | tf_op jit(solution)/shard_map/ppermute | solution.py:23
  109.4 4.8 %collective-permute-start.16 = (bf16[64,512]{1,0:T(8,128)(2,1)S(1)}, bf16[64,512]{1,0:T(8,128)(2,1)S(1)}, u32[]{:S(2)}, u32[]{:S(2)}) collective-permute-start(bf16[64,512]{1,0:T(8,128)(2,1)S(1)} %get-tuple-element.88), channel_id=1, source_target_pairs={{0,24},{4,28},{8,16},{12,20},{16,8},{20,12},{24,0},{28,4},{1,25},{... | collective-permute-start | bytes 196616 | tf_op jit(solution)/shard_map/ppermute | solution.py:23
  111.3 4.6 %collective-permute-start.15 = (bf16[64,512]{1,0:T(8,128)(2,1)S(1)}, bf16[64,512]{1,0:T(8,128)(2,1)S(1)}, u32[]{:S(2)}, u32[]{:S(2)}) collective-permute-start(bf16[64,512]{1,0:T(8,128)(2,1)S(1)} %get-tuple-element.89), channel_id=1, source_target_pairs={{0,16},{4,20},{8,24},{12,28},{16,0},{20,4},{24,8},{28,12},{1,17},{... | collective-permute-start | bytes 196616 | tf_op jit(solution)/shard_map/ppermute | solution.py:23
  112.0 22.4 %copy-start.2 = (bf16[8192,128]{1,0:T(8,128)(2,1)S(1)}, bf16[8192,128]{1,0:T(8,128)(2,1)}, u32[]{:S(2)}) copy-start(bf16[8192,128]{1,0:T(8,128)(2,1)} %copy-done.1) | copy-start | bytes 6291460
  115.9 3.9 %collective-permute-start.19 = (bf16[64,512]{1,0:T(8,128)(2,1)S(1)}, bf16[64,512]{1,0:T(8,128)(2,1)S(1)}, u32[]{:S(2)}, u32[]{:S(2)}) collective-permute-start(bf16[64,512]{1,0:T(8,128)(2,1)S(1)} %add_convert_fusion.1), channel_id=1, source_target_pairs={{0,3},{1,2},{2,1},{3,0},{4,7},{5,6},{6,5},{7,4},{8,11},{9,10},{10,... | collective-permute-start | bytes 196616 | tf_op jit(solution)/shard_map/ppermute | solution.py:23
  117.2 5.1 %collective-permute-start.18 = (bf16[64,512]{1,0:T(8,128)(2,1)S(1)}, bf16[64,512]{1,0:T(8,128)(2,1)S(1)}, u32[]{:S(2)}, u32[]{:S(2)}) collective-permute-start(bf16[64,512]{1,0:T(8,128)(2,1)S(1)} %add_convert_fusion.1), channel_id=1, source_target_pairs={{0,2},{1,3},{2,0},{3,1},{4,6},{5,7},{6,4},{7,5},{8,10},{9,11},{10,... | collective-permute-start | bytes 196616 | tf_op jit(solution)/shard_map/ppermute | solution.py:23
  117.7 4.7 %collective-permute-start.17 = (bf16[64,512]{1,0:T(8,128)(2,1)S(1)}, bf16[64,512]{1,0:T(8,128)(2,1)S(1)}, u32[]{:S(2)}, u32[]{:S(2)}) collective-permute-start(bf16[64,512]{1,0:T(8,128)(2,1)S(1)} %add_convert_fusion.1), channel_id=1, source_target_pairs={{0,1},{1,0},{2,3},{3,2},{4,5},{5,4},{6,7},{7,6},{8,9},{9,8},{10,11... | collective-permute-start | bytes 196616 | tf_op jit(solution)/shard_map/ppermute | solution.py:23
  123.9 3.8 %collective-permute-start.20 = (f32[64,512]{1,0:T(8,128)S(1)}, f32[64,512]{1,0:T(8,128)S(1)}, u32[]{:S(2)}, u32[]{:S(2)}) collective-permute-start(f32[64,512]{1,0:T(8,128)S(1)} %get-tuple-element.84), channel_id=1, source_target_pairs={{0,8},{4,12},{8,0},{12,4},{16,24},{20,28},{24,16},{28,20},{1,9},{5... | collective-permute-start | bytes 393224 | tf_op jit(solution)/shard_map/ppermute | solution.py:23
  124.2 4.2 %collective-permute-start.21 = (f32[64,512]{1,0:T(8,128)S(1)}, f32[64,512]{1,0:T(8,128)S(1)}, u32[]{:S(2)}, u32[]{:S(2)}) collective-permute-start(f32[64,512]{1,0:T(8,128)S(1)} %get-tuple-element.84), channel_id=1, source_target_pairs={{0,16},{4,20},{8,24},{12,28},{16,0},{20,4},{24,8},{28,12},{1,17},{... | collective-permute-start | bytes 393224 | tf_op jit(solution)/shard_map/ppermute | solution.py:23
  125.6 6.4 %collective-permute-start.22 = (f32[64,512]{1,0:T(8,128)S(1)}, f32[64,512]{1,0:T(8,128)S(1)}, u32[]{:S(2)}, u32[]{:S(2)}) collective-permute-start(f32[64,512]{1,0:T(8,128)S(1)} %get-tuple-element.84), channel_id=1, source_target_pairs={{0,24},{4,28},{8,16},{12,20},{16,8},{20,12},{24,0},{28,4},{1,25},{... | collective-permute-start | bytes 393224 | tf_op jit(solution)/shard_map/ppermute | solution.py:23
  132.7 7.7 %collective-permute-start.23 = (f32[256,512]{1,0:T(8,128)}, f32[256,512]{1,0:T(8,128)}, u32[]{:S(2)}, u32[]{:S(2)}) collective-permute-start(f32[256,512]{1,0:T(8,128)} %constant_dynamic-update-slice_fusion), channel_id=1, source_target_pairs={{0,4},{4,0},{8,12},{12,8},{16,20},{20,16},{24,28},{28,24},{1,5},{5... | collective-permute-start | bytes 1572872 | tf_op jit(solution)/shard_map/ppermute | solution.py:23
  137.5 14.2 %collective-permute-start.28 = (bf16[2048,128]{1,0:T(8,128)(2,1)}, bf16[2048,128]{1,0:T(8,128)(2,1)S(1)}, u32[]{:S(2)}, u32[]{:S(2)}) collective-permute-start(bf16[2048,128]{1,0:T(8,128)(2,1)} %get-tuple-element.76), channel_id=1, source_target_pairs={{0,8},{4,12},{8,0},{12,4},{16,24},{20,28},{24,16},{28,20},{1,9},{5... | collective-permute-start | bytes 1572872 | tf_op jit(solution)/shard_map/ppermute | solution.py:23
  139.2 13.9 %collective-permute-start.29 = (bf16[2048,128]{1,0:T(8,128)(2,1)}, bf16[2048,128]{1,0:T(8,128)(2,1)}, u32[]{:S(2)}, u32[]{:S(2)}) collective-permute-start(bf16[2048,128]{1,0:T(8,128)(2,1)} %get-tuple-element.77), channel_id=1, source_target_pairs={{0,16},{4,20},{8,24},{12,28},{16,0},{20,4},{24,8},{28,12},{1,17},{... | collective-permute-start | bytes 1572872 | tf_op jit(solution)/shard_map/ppermute | solution.py:23
  139.8 23.8 %collective-permute-start.30 = (bf16[2048,128]{1,0:T(8,128)(2,1)}, bf16[2048,128]{1,0:T(8,128)(2,1)}, u32[]{:S(2)}, u32[]{:S(2)}) collective-permute-start(bf16[2048,128]{1,0:T(8,128)(2,1)} %get-tuple-element.78), channel_id=1, source_target_pairs={{0,24},{4,28},{8,16},{12,20},{16,8},{20,12},{24,0},{28,4},{1,25},{... | collective-permute-start | bytes 1572872 | tf_op jit(solution)/shard_map/ppermute | solution.py:23
  165.1 5.4 %collective-permute-start.31 = (bf16[512,128]{1,0:T(8,128)(2,1)S(1)}, bf16[512,128]{1,0:T(8,128)(2,1)S(1)}, u32[]{:S(2)}, u32[]{:S(2)}) collective-permute-start(bf16[512,128]{1,0:T(8,128)(2,1)S(1)} %get-tuple-element.80), channel_id=1, source_target_pairs={{0,1},{1,0},{2,3},{3,2},{4,5},{5,4},{6,7},{7,6},{8,9},{9,8},{10,11... | collective-permute-start | bytes 393224 | tf_op jit(solution)/shard_map/ppermute | solution.py:23
  167.2 6.2 %collective-permute-start.32 = (bf16[512,128]{1,0:T(8,128)(2,1)S(1)}, bf16[512,128]{1,0:T(8,128)(2,1)S(1)}, u32[]{:S(2)}, u32[]{:S(2)}) collective-permute-start(bf16[512,128]{1,0:T(8,128)(2,1)S(1)} %get-tuple-element.81), channel_id=1, source_target_pairs={{0,2},{1,3},{2,0},{3,1},{4,6},{5,7},{6,4},{7,5},{8,10},{9,11},{10,... | collective-permute-start | bytes 393224 | tf_op jit(solution)/shard_map/ppermute | solution.py:23
  168.3 11.0 %collective-permute-start.33 = (bf16[512,128]{1,0:T(8,128)(2,1)S(1)}, bf16[512,128]{1,0:T(8,128)(2,1)S(1)}, u32[]{:S(2)}, u32[]{:S(2)}) collective-permute-start(bf16[512,128]{1,0:T(8,128)(2,1)S(1)} %get-tuple-element.82), channel_id=1, source_target_pairs={{0,3},{1,2},{2,1},{3,0},{4,7},{5,6},{6,5},{7,4},{8,11},{9,10},{10,... | collective-permute-start | bytes 393224 | tf_op jit(solution)/shard_map/ppermute | solution.py:23

commit v2 on v1

v2 whole, which is shorter than its diff:
```python
import functools
import math

import jax
import jax.numpy as jnp
from jax import lax
from jax.experimental import pallas as pl
from jax.experimental.pallas import tpu as pltpu
from jax.sharding import PartitionSpec as P

BLOCK = 128
GROUP = 4
ID_ROWS = 16
MIB = 1 << 20


def lanes(width):
    return -(-width // 128) * 128


def swap(value, axis, flip):
    size = lax.axis_size(axis)
    return lax.ppermute(value, axis, [(i, i ^ flip) for i in range(size)])


def load_ids(ids_vmem, ids_smem, lists, slots, sem):
    for d in range(lists.shape[0]):
        rows = lists[d, slots * BLOCK :, :].astype(jnp.float32)
        ids_vmem[d] = rows.astype(jnp.int32)[:8]
    copy = pltpu.make_async_copy(ids_vmem, ids_smem, sem)
    copy.start()
    copy.wait()


def each_group(ids, place, given, visit):
    for i, d in enumerate(given):
        live = ids[i, 2, 0]

        def step(group, carry, i=i, d=d, live=live):
            visit(i, place[0] ^ d, group * GROUP, live)
            return carry

        lax.fori_loop(0, (live + GROUP - 1) // GROUP, step, 0)


def fetch_late(place, teams, middle, relayed, target, sem):
    at_end = (place[0] == 0) | (place[0] == teams - 1)

    @pl.when(at_end)
    def _():
        pltpu.make_async_copy(relayed, target, sem).start()

    @pl.when(jnp.logical_not(at_end))
    def _():
        pltpu.make_async_copy(middle, target, sem).start()

    return pltpu.make_async_copy(middle, target, sem)


def forward_visit(panels, panel_rows, lists, ids, totals):
    def visit(i, panel, first, live):
        products = []
        for u in range(GROUP):
            slot = first + u
            start = panel * panel_rows + ids[i, 1, slot] * BLOCK
            source = panels[pl.ds(pl.multiple_of(start, BLOCK), BLOCK), :]
            block = lists[i, pl.ds(pl.multiple_of(slot * BLOCK, BLOCK), BLOCK), :]
            product = jnp.dot(block, source, preferred_element_type=jnp.float32)
            products.append(jnp.where(slot < live, product, 0.0))
        for u in range(GROUP):
            start = pl.multiple_of(ids[i, 0, first + u] * BLOCK, BLOCK)
            totals[pl.ds(start, BLOCK), :] += products[u]

    return visit


def prepare_kernel(slots, place, *refs):
    vals, row_ids, col_ids, count = refs[:4]
    rows, cols, lives, tail, sems = refs[-5:]
    mine = refs[4] if len(refs) == 10 else refs[5]
    blocks = slots * BLOCK
    moves = [(row_ids, rows), (col_ids, cols), (count, lives), (vals, mine.at[pl.ds(0, blocks), :])]
    if len(refs) > 10:
        features, near = refs[4], refs[6]
        width = near.shape[1]
        start = pl.multiple_of(place[0] * width, width)
        moves.append((features.at[:, pl.ds(start, width)], near))
    copies = [
        pltpu.make_async_copy(source, target, sems.at[i])
        for i, (source, target) in enumerate(moves)
    ]
    for copy in copies:
        copy.start()
    tail[...] = jnp.zeros_like(tail)
    for copy in copies[:3]:
        copy.wait()
    tail[0:1, 0:slots] = rows[...].astype(jnp.float32)
    tail[1:2, 0:slots] = cols[...].astype(jnp.float32)
    tail[2:3, 0:1] = lives[...].astype(jnp.float32)
    mine[pl.ds(blocks, ID_ROWS), :] = tail[...].astype(jnp.bfloat16)
    for copy in copies[3:]:
        copy.wait()


def early_kernel(chips, teams, slots, place, *refs):
    near = refs[:chips]
    far = refs[chips : 2 * chips]
    early = teams - 1
    given = refs[2 * chips : 2 * chips + early]
    weight, table = refs[2 * chips + early : 2 * chips + early + 2]
    totals, late_panel, *kept = refs[2 * chips + early + 2 : 2 * chips + early + 6]
    panels, lists, ids_vmem, ids_smem, sems, id_sem = refs[2 * chips + early + 6 :]
    slab = near[0].shape[0]
    panel_rows = panels.shape[0] // teams
    team, chip, core = place[0], place[1], place[2]
    copies = []
    for d in range(early):
        copies.append(pltpu.make_async_copy(given[d], lists.at[d], sems.at[d]))
    for d in range(chips):
        for side, source in ((core, near[d]), (1 - core, far[d])):
            start = pl.multiple_of((2 * (chip ^ d) + side) * slab, slab)
            target = panels.at[pl.ds(start, slab), :]
            copies.append(pltpu.make_async_copy(source, target, sems.at[len(copies)]))
    for source, target in zip((weight, table), kept):
        copies.append(pltpu.make_async_copy(source, target, sems.at[len(copies)]))
    for copy in copies:
        copy.start()
    totals[...] = jnp.zeros_like(totals)
    for copy in copies[:early]:
        copy.wait()
    load_ids(ids_vmem, ids_smem, lists, slots, id_sem)
    for copy in copies[early:]:
        copy.wait()
    visit = forward_visit(panels, panel_rows, lists, ids_smem, totals)
    each_group(ids_smem, place, range(early), visit)
    start = pl.multiple_of((team ^ early) * panel_rows, panel_rows)
    late_panel[...] = panels[pl.ds(start, panel_rows), :]


def late_kernel(teams, slots, place, *refs):
    middle, relayed, begun, panel = refs[:4]
    outs = refs[4 : 4 + teams]
    totals, lists, ids_vmem, ids_smem, sem, id_sem = refs[4 + teams :]
    fetch = fetch_late(place, teams, middle, relayed, lists.at[0], sem)
    totals[...] = begun[...]
    fetch.wait()
    load_ids(ids_vmem, ids_smem, lists, slots, id_sem)
    visit = forward_visit(panel, 0, lists, ids_smem, totals)
    each_group(ids_smem, place, [teams - 1], visit)
    share = outs[0].shape[0]
    for d in range(teams):
        start = pl.multiple_of((place[0] ^ d) * share, share)
        outs[d][...] = totals[pl.ds(start, share), :].astype(jnp.bfloat16)


def layer_kernel(teams, place, *refs):
    parts = refs[:teams]
    weight, table, *fixed = refs[teams : teams + 4]
    output, grad_pre = refs[teams + 4 : teams + 6]
    backs = refs[teams + 6 : 2 * teams + 6]
    labels, mask, sems = refs[2 * teams + 6 :]
    team = place[0]
    width = parts[0].shape[1]
    copies = [
        pltpu.make_async_copy(source, target, sems.at[i])
        for i, (source, target) in enumerate(zip(fixed, (labels, mask)))
    ]
    for copy in copies:
        copy.start()

    def weight_rows(d):
        return weight[pl.ds(pl.multiple_of((team ^ d) * width, width), width), :]

    preact = jnp.dot(parts[0][...], weight_rows(0), preferred_element_type=jnp.float32)
    for d in range(1, teams):
        preact += jnp.dot(parts[d][...], weight_rows(d), preferred_element_type=jnp.float32)
    sigma = 1.0 / (1.0 + jnp.exp(-preact))
    active = preact * sigma
    output[...] = active.astype(jnp.bfloat16)
    classes = table.shape[0]
    for copy in copies:
        copy.wait()
    row_labels = labels[pl.ds(team, 1), :]
    row_mask = mask[pl.ds(team, 1), :].astype(jnp.float32)
    rows = row_labels.shape[1]
    index = lax.broadcasted_iota(jnp.int32, (classes, rows), 0)
    known = jnp.where(index == row_labels, row_mask, 0.0).astype(jnp.bfloat16)
    held = jnp.broadcast_to(row_mask * (1.0 / 8.0), (8, rows)).astype(jnp.bfloat16)
    across = (((0,), (0,)), ((), ()))
    target = lax.dot_general(known, table[...], across, preferred_element_type=jnp.float32)
    ones = jnp.ones((8, table.shape[1]), jnp.bfloat16)
    masked = lax.dot_general(held, ones, across, preferred_element_type=jnp.float32)
    slope = sigma * (1.0 + preact * (1.0 - sigma))
    grad = ((masked * active - target) * slope).astype(jnp.bfloat16)
    grad_pre[...] = grad
    for d in range(teams):
        backs[d][...] = lax.dot_general(
            grad, weight_rows(d), (((1,), (1,)), ((), ())), preferred_element_type=jnp.float32
        ).astype(jnp.bfloat16)


def weight_kernel(teams, chips, place, *refs):
    parts = refs[:teams]
    grad_pre, keep, send, term = refs[teams:]
    width = parts[0].shape[1]
    for d in range(teams):
        start = pl.multiple_of((place[0] ^ d) * width, width)
        term[pl.ds(start, width), :] = lax.dot_general(
            parts[d][...], grad_pre[...], (((0,), (0,)), ((), ())), preferred_element_type=jnp.float32
        ).astype(jnp.bfloat16)
    half = term.shape[0] // 2
    rows = half // chips
    for out, side in ((keep, place[2]), (send, 1 - place[2])):
        for q in range(chips):
            held = pl.ds(pl.multiple_of(side * half + q * rows, rows), rows)
            for t in range(teams):
                start = (q * teams + t) * rows
                out[start : start + rows, :] = term[held, t * width : (t + 1) * width]


def tree(values):
    while len(values) > 1:
        values = [values[i] + values[i + 1] for i in range(0, len(values), 2)]
    return values[0]


def weight_total_kernel(teams, place, *refs):
    out = refs[teams]
    rows = out.shape[0]
    values = [ref[ref.shape[0] - rows :, :].astype(jnp.float32) for ref in refs[:teams]]
    out[...] = tree(values).astype(out.dtype)


def weight_half_kernel(chips, teams, place, *refs):
    out = refs[chips]
    rows = refs[0].shape[0] // teams
    width = refs[0].shape[1]
    for d in range(chips):
        held = pl.ds(pl.multiple_of((place[1] ^ d) * rows, rows), rows)
        for t in range(teams):
            out[held, t * width : (t + 1) * width] = refs[d][t * rows : (t + 1) * rows, :]


def whole_kernel(scale, place, mine, taken, out):
    rows = mine.shape[0]
    for value, here in ((mine, place[2]), (taken, 1 - place[2])):
        held = pl.ds(pl.multiple_of(here * rows, rows), rows)
        out[held, :] = value[...].astype(jnp.float32) * scale


def backward_kernel(chips, teams, slots, piece, chunk, riders, place, *refs):
    count = len(chunk)
    last = teams - 1 in chunk
    given = refs[: count + last]
    backs = refs[count + last : count + last + teams]
    refs = refs[count + last + teams :]
    rider_refs, refs = refs[:riders], refs[riders:]
    keep, send, lists, rows, totals, ids_vmem, ids_smem, sems, id_sem = refs
    team, core = place[0], place[2]
    share = backs[0].shape[0]
    per_piece = piece // BLOCK
    plain = count - last
    copies = []
    for i in range(plain):
        copies.append(pltpu.make_async_copy(given[i], lists.at[i], sems.at[i]))
        copies[-1].start()
    if last:
        target = lists.at[plain]
        copies.append(fetch_late(place, teams, *given[plain:], target, sems.at[plain]))
    moves = []
    for d in range(teams):
        start = pl.multiple_of((team ^ d) * share, share)
        target = rows.at[pl.ds(start, share), :]
        moves.append(pltpu.make_async_copy(backs[d], target, sems.at[count + d]))
        moves[-1].start()
    totals[...] = jnp.zeros_like(totals)
    for copy in copies:
        copy.wait()
    load_ids(ids_vmem, ids_smem, lists, slots, id_sem)
    for copy in moves:
        copy.wait()

    def visit(i, panel, first, live):
        products = []
        for u in range(GROUP):
            slot = first + u
            start = pl.multiple_of(ids_smem[i, 0, slot] * BLOCK, BLOCK)
            source = rows[pl.ds(start, BLOCK), :]
            block = lists[i, pl.ds(pl.multiple_of(slot * BLOCK, BLOCK), BLOCK), :]
            product = lax.dot_general(
                block, source, (((0,), (0,)), ((), ())), preferred_element_type=jnp.float32
            )
            products.append(jnp.where(slot < live, product, 0.0))
        for u in range(GROUP):
            col = ids_smem[i, 1, first + u]
            owner = col // per_piece
            slot_half = (owner % 2) ^ core
            slot_chip = owner // 2
            start = ((slot_half * chips + slot_chip) * count + i) * piece
            start = pl.multiple_of(start + (col % per_piece) * BLOCK, BLOCK)
            totals[pl.ds(start, BLOCK), :] += products[u]

    each_group(ids_smem, place, chunk, visit)
    size = count * piece
    step = keep.shape[0] // chips
    for side, out in enumerate((keep, send)):
        for q in range(chips):
            here = (side * chips + q) * size
            out[q * step : q * step + size, :] = totals[here : here + size, :].astype(jnp.bfloat16)
            if riders:
                more = step - size
                rider = rider_refs[side][q * more : (q + 1) * more, :]
                out[q * step + size : (q + 1) * step, :] = rider


def pair_kernel(chips, place, keep, taken, *outs):
    rows = outs[0].shape[0]
    for d in range(chips):
        here = pl.ds(pl.multiple_of((place[1] ^ d) * rows, rows), rows)
        total = keep[here, :].astype(jnp.float32) + taken[here, :].astype(jnp.float32)
        outs[d][...] = total.astype(jnp.bfloat16)


def plane_kernel(chips, count, place, *refs):
    parts, outs = refs[:chips], refs[chips:]
    rider = outs[count] if len(outs) > count else None
    rows = outs[0].shape[0] - (rider.shape[0] if rider is not None else 0)

    def total(here):
        value = parts[0][here, :].astype(jnp.float32)
        for part in parts[1:]:
            value += part[here, :].astype(jnp.float32)
        return value.astype(jnp.bfloat16)

    for i in range(count):
        outs[i][:rows, :] = total(slice(i * rows, (i + 1) * rows))
    if rider is not None:
        value = total(slice(count * rows, None))
        rider[...] = value
        for i in range(count):
            outs[i][rows:, :] = value


def join_kernel(teams, place, *refs):
    parts = refs[:teams]
    out, held = refs[teams:]
    width = parts[0].shape[1]
    for d in range(teams):
        held[place[0] ^ d] = parts[d][: held.shape[1], :]
    for d in range(teams):
        out[:, d * width : (d + 1) * width] = held[d]


def call(kernel, name, operands, spaces, out_shapes, scratch, flops, limit, after=()):
    moved = sum(math.prod(x.shape) * x.dtype.itemsize for x in (*operands, *out_shapes))
    specs = [pl.BlockSpec(memory_space=space) for space in spaces]
    specs += [pl.BlockSpec(memory_space=pl.ANY) for _ in after]
    given = len(operands)

    def body(*refs):
        row = lax.axis_index("row")
        place = (lax.axis_index("team"), row // 2, row % 2)
        kernel(place, *refs[:given], *refs[given + len(after) :])

    return pl.pallas_call(
        body,
        name=name,
        in_specs=specs,
        out_specs=[pl.BlockSpec(memory_space=pltpu.VMEM) for _ in out_shapes],
        out_shape=out_shapes,
        scratch_shapes=scratch,
        cost_estimate=pl.CostEstimate(flops=flops, bytes_accessed=moved, transcendentals=0),
        compiler_params=pltpu.CompilerParams(vmem_limit_bytes=limit),
    )(*operands, *after)


def gather_lists(mine, teams):
    if teams == 4:
        two = swap(mine, "team", 2)
        one = swap(mine, "team", 1)
        held, two = lax.optimization_barrier((mine, two))
        relayed = lax.ppermute(two, "team", [(2, 3), (1, 0)])
        middle = lax.ppermute(held, "team", [(1, 2), (2, 1)])
        return [mine, one, two], [middle, relayed]
    early = [mine] + [swap(mine, "team", d) for d in range(1, teams - 1)]
    last = swap(mine, "team", teams - 1)
    return early, [last, last]


def per_device(
    features, weight, table, labels, label_mask, block_vals, block_row, block_col, block_count
):
    slab, width = features.shape
    slots = block_vals.shape[2]
    rows_n = lax.axis_size("row")
    teams = lax.axis_size("team")
    chips = rows_n // 2
    nodes = slab * rows_n
    panel_rows = nodes // teams
    part = width // teams
    share = slab // teams
    piece = panel_rows // rows_n
    team = lax.axis_index("team")
    bf16, f32 = jnp.bfloat16, jnp.float32
    any_space, vmem = pl.ANY, pltpu.VMEM
    padded = lanes(part)
    payload = slots * BLOCK + ID_ROWS

    def shaped(*dims, kind=bf16):
        return jax.ShapeDtypeStruct(dims, kind)

    def id_scratch(count):
        return [
            pltpu.VMEM((count, payload, BLOCK), bf16),
            pltpu.VMEM((count, 8, BLOCK), jnp.int32),
            pltpu.SMEM((count, 8, BLOCK), jnp.int32),
        ]

    list_bytes = payload * BLOCK * 2
    list_flops = 2 * slots * BLOCK * BLOCK * part

    aligned = part % 128 == 0
    prepared = call(
        functools.partial(prepare_kernel, slots),
        "prepare",
        [
            block_vals.reshape(slots * BLOCK, BLOCK),
            block_row.reshape(1, slots),
            block_col.reshape(1, slots),
            block_count,
            *([features] if aligned else []),
        ],
        [pltpu.HBM] * (4 + aligned),
        [shaped(payload, BLOCK)] + [shaped(slab, part)] * aligned,
        [
            pltpu.VMEM((1, slots), jnp.int32),
            pltpu.VMEM((1, slots), jnp.int32),
            pltpu.VMEM((1, 1), jnp.int32),
            pltpu.VMEM((ID_ROWS, BLOCK), f32),
            pltpu.SemaphoreType.DMA((5,)),
        ],
        0,
        60 * MIB,
    )
    mine = prepared[0]
    own = prepared[1] if aligned else lax.dynamic_slice_in_dim(features, team * part, part, 1)
    early, late = gather_lists(mine, teams)
    near = [own] + [swap(own, "row", 2 * d) for d in range(1, chips)]
    far = [swap(value, "row", 1) for value in near]

    ids = id_scratch(teams - 1)
    begun, late_panel, weight_here, table_here = call(
        functools.partial(early_kernel, chips, teams, slots),
        "early_products",
        [*near, *far, *early, weight, table],
        [any_space] * (2 * chips + teams + 1),
        [
            shaped(slab, part, kind=f32),
            shaped(panel_rows, part),
            shaped(*weight.shape),
            shaped(*table.shape),
        ],
        [
            pltpu.VMEM((nodes, part), bf16),
            *ids,
            pltpu.SemaphoreType.DMA((2 * chips + teams + 1,)),
            pltpu.SemaphoreType.DMA,
        ],
        (teams - 1) * list_flops,
        (nodes + panel_rows) * padded * 2 + teams * list_bytes + slab * padded * 4 + 4 * MIB,
    )
    ids = id_scratch(1)
    sent = call(
        functools.partial(late_kernel, teams, slots),
        "late_products",
        [*late, begun, late_panel],
        [any_space, any_space, vmem, vmem],
        [shaped(share, part)] * teams,
        [
            pltpu.VMEM((slab, part), f32),
            *ids,
            pltpu.SemaphoreType.DMA,
            pltpu.SemaphoreType.DMA,
        ],
        list_flops,
        (panel_rows + 5 * slab) * padded * 2 + list_bytes + 3 * MIB,
    )
    aggs = [sent[0]] + [swap(sent[d], "team", d) for d in range(1, teams)]

    output, grad_pre, *backs = call(
        functools.partial(layer_kernel, teams),
        "layer",
        [
            *aggs,
            weight_here,
            table_here,
            labels.reshape(teams, share),
            label_mask.reshape(teams, share),
        ],
        [vmem] * (teams + 2) + [any_space] * 2,
        [shaped(share, width)] * 2 + [shaped(share, part)] * teams,
        [
            pltpu.VMEM((teams, share), jnp.int32),
            pltpu.VMEM((teams, share), jnp.int32),
            pltpu.SemaphoreType.DMA((2,)),
        ],
        4 * share * width * width,
        16 * MIB,
    )
    backs = [backs[0]] + [swap(backs[d], "team", d) for d in range(1, teams)]

    half = width // 2
    rider = half // chips * teams
    w_keep, w_send = call(
        functools.partial(weight_kernel, teams, chips),
        "weight_term",
        [*aggs, grad_pre],
        [vmem] * (teams + 1),
        [shaped(chips * rider, part)] * 2,
        [pltpu.VMEM((width, width), bf16)],
        2 * share * width * width,
        12 * MIB,
    )

    def plane_total(pieces):
        return [pieces[0]] + [swap(pieces[d], "row", 2 * d) for d in range(1, chips)]

    chunks = [list(range(teams // 2, teams)), list(range(teams // 2))]
    lists = early + late
    slices = [None] * teams
    held, paired = [], []
    for chunk in chunks:
        count = len(chunk)
        first = chunk is chunks[0]
        rows = chips * count * piece
        moved = rows + first * chips * rider
        given = [lists[d] for d in chunk] + (lists[-1:] if teams - 1 in chunk else [])
        riders = [w_keep, w_send] if first else []
        held.append(
            call(
                functools.partial(
                    backward_kernel, chips, teams, slots, piece, chunk, len(riders)
                ),
                "backward",
                [*given, *backs, *riders],
                [any_space] * (len(given) + teams) + [vmem] * len(riders),
                [shaped(moved, part)] * 2,
                [
                    id_scratch(count)[0],
                    pltpu.VMEM((slab, part), bf16),
                    pltpu.VMEM((2 * rows, part), f32),
                    *id_scratch(count)[1:],
                    pltpu.SemaphoreType.DMA((count + teams,)),
                    pltpu.SemaphoreType.DMA,
                ],
                count * list_flops,
                rows * padded * 14 + count * list_bytes + slab * padded * 2 + 4 * MIB,
                after=[value[0] for value in held],
            )
        )
    mark = [held[1][0]]
    for chunk, (keep, send) in zip(chunks, held):
        moved = keep.shape[0]
        paired.append(
            call(
                functools.partial(pair_kernel, chips),
                "pair_sum",
                [keep, swap(send, "row", 1)],
                [vmem] * 2,
                [shaped(moved // chips, part)] * chips,
                [],
                moved * part,
                moved * padded * 6 + 3 * MIB,
                after=mark,
            )
        )
        mark = paired[0][:1]
    mark = paired[1][:1]
    for chunk, pieces in zip(chunks, paired):
        count = len(chunk)
        first = chunk is chunks[0]
        outs = [shaped(piece + first * rider, part)] * count + [shaped(rider, part)] * first
        sums = call(
            functools.partial(plane_kernel, chips, count),
            "plane_sum",
            plane_total(pieces),
            [vmem] * chips,
            outs,
            [],
            chips * count * piece * part,
            chips * (count * piece + rider) * padded * 4 + 3 * MIB,
            after=mark,
        )
        for d, value in zip(chunk, sums):
            slices[d] = swap(value, "team", d) if d else value
        mark = []
        if first:
            w_plane = sums[count]
    w_parts = [w_plane] + [
        slices[d] if d in chunks[0] else swap(w_plane, "team", d) for d in range(1, teams)
    ]
    (w_total,) = call(
        functools.partial(weight_total_kernel, teams),
        "weight_total",
        w_parts,
        [vmem] * teams,
        [shaped(rider, part)],
        [],
        half * width,
        6 * MIB,
        after=sums[:1],
    )
    (w_half,) = call(
        functools.partial(weight_half_kernel, chips, teams),
        "weight_half",
        plane_total([w_total] * chips),
        [vmem] * chips,
        [shaped(half, width)],
        [],
        half * width,
        6 * MIB,
        after=[slices[d] for d in chunks[1][1:]],
    )
    (grad_weight,) = call(
        functools.partial(whole_kernel, 1.0 / math.sqrt(nodes)),
        "weight_whole",
        [w_half, swap(w_half, "row", 1)],
        [vmem] * 2,
        [shaped(width, width, kind=f32)],
        [],
        half * width,
        6 * MIB,
    )
    (grad_features,) = call(
        functools.partial(join_kernel, teams),
        "join",
        slices,
        [vmem] * teams,
        [shaped(piece, width)],
        [pltpu.VMEM((teams, piece, part), bf16)],
        piece * width,
        teams * piece * padded * 8 + 3 * MIB,
    )

    return (output, grad_weight, grad_features[None])


def solution(mesh):
    placed = (
        P("row", None),
        P(),
        P(),
        P("row"),
        P("row"),
        P("row", "team", None, None, None),
        P("row", "team", None),
        P("row", "team", None),
        P("row", "team"),
    )
    return jax.shard_map(
        per_device,
        mesh=mesh,
        in_specs=placed,
        out_specs=(P(("row", "team"), None), P(), P("team", "row", None)),
        check_vma=False,
    )
```

time: 184 us -> 137 us (0.74); the launches traced: 181 us -> 136 us
  waiting for transfers between devices: 107 us -> 78.5 us
  local copies, waits for them, and re-layouts: 13.9 us -> 2.12 us
  Pallas kernels: 22 us -> 17.2 us
  starting transfers between devices: 32.5 us -> 36.9 us
  other arithmetic: 4.3 us -> 0 us
    ppermute x34 -> x31, waiting for transfers between devices: 107 us -> 70.4 us  [swap(): return lax.ppermute(value, axis, [(i, i ^ flip) for i in range(size)])]
    ppermute x0 -> x2, waiting for transfers between devices: none -> 8.17 us  [the longest x1 4.12 us: gather_lists(): relayed = lax.ppermute(two, 'team', [(2, 3), (1, 0)])]
    pallas_call x7 -> x15, Pallas kernels: 22 us -> 17.2 us  [call(): pl.pallas_call(body, name=name, in_specs=specs, out_specs=[pl.BlockSpec(m...]
    ppermute x0 -> x2, starting transfers between devices: none -> 4.67 us  [the longest x1 2.57 us: gather_lists(): middle = lax.ppermute(held, 'team', [(1, 2), (2, 1)])]
    unnamed x14, local copies, waits for them, and re-layouts: 6.07 us -> 2.1 us
    concatenate x2 -> x0, other arithmetic: 2.12 us -> none  [the longest x1 1.08 us: per_device(): jnp.concatenate([block_vals.reshape(slots * BLOCK, BLOCK), ids], axis=0)]
    dynamic_update_slice x3 -> x0, local copies, waits for them, and re-layouts: 1.99 us -> none  [per_device(): lax.dynamic_update_slice_in_dim(w_half, taken, (row // 2 ^ d) * w_rows, 0)]
    ppermute x34 -> x31, starting transfers between devices: 32.5 us -> 32.3 us  [swap(): return lax.ppermute(value, axis, [(i, i ^ flip) for i in range(size)])]
  transfers between devices with their start and end apart: 34 -> 33, of which waited for: 24 -> 20; matrix products, arithmetic and copies ran while one was open for 6% -> 0% of each run, Pallas kernels for 2% -> 6%
where the time goes in v2:
time: 137 us; the launch traced here: 136 us
  waiting for transfers between devices  78.5 us (57%)
  starting transfers between devices  36.9 us (27%)
  Pallas kernels  17.2 us (13%)
  local copies, waits for them, and re-layouts  2.12 us (2%)
  between operations  1.54 us (1%)
    ppermute x31, waiting for transfers between devices, swap(): return lax.ppermute(value, axis, [(i, i ^ flip) for i in range(size)])  70.4 us
    ppermute x31, starting transfers between devices, swap(): return lax.ppermute(value, axis, [(i, i ^ flip) for i in range(size)])  32.3 us
    pallas_call x15, Pallas kernels, call(): pl.pallas_call(body, name=name, in_specs=specs, out_specs=[pl.BlockSpec(m...  17.2 us
    ppermute x1, waiting for transfers between devices, gather_lists(): relayed = lax.ppermute(two, 'team', [(2, 3), (1, 0)])  4.12 us
    ppermute x1, waiting for transfers between devices, gather_lists(): middle = lax.ppermute(held, 'team', [(1, 2), (2, 1)])  4.05 us
  transfers between devices with their start and end apart: 33, of which 20 were waited for; matrix products, arithmetic and copies ran while one was open for 0% of the time, Pallas kernels for 6%

profile of v2, /device:TPU:9, one launch (start us, length us, event | category | flops | bytes accessed | tf_op | source)
XLA Modules:
  0.0 136.3 jit_solution(14108097457680865141)
XLA Ops:
  1.3 2.3 %prepare.1 = (bf16[2064,128]{1,0:T(8,128)(2,1)}, bf16[2048,128]{1,0:T(8,128)(2,1)}) custom-call(bf16[2048,128]{1,0:T(8,128)(2,1)} %bitcast.5, s32[1,16]{1,0:T(1,128)} %bitcast.6, s32[1,16]{1,0:T(1,128)} %bitcast.7, s32[1,1]{1,0:T(1,128)S(6)} %copy.12.refs_3_, bf16[2048,512]{1,0:T(8,128)(2,1)} %refs_4_.1), custom_call_target="tpu_custom_call" | custom-call | bytes 3674244 | tf_op jit(solution)/shard_map/prepare/pallas_call | solution.py:365
  3.6 1.3 collective-permute-start.3
  4.9 2.3 %collective-permute-start = (bf16[2064,128]{1,0:T(8,128)(2,1)}, bf16[2064,128]{1,0:T(8,128)(2,1)S(1)}, u32[]{:S(2)}, u32[]{:S(2)}) collective-permute-start(bf16[2064,128]{1,0:T(8,128)(2,1)} %get-tuple-element.41.refs_8_.refs_0_), channel_id=1, source_target_pairs={{0,2},{1,3},{2,0},{3,1},{4,6},{5,7},{6,4},{7,5},{8,10},{9,11},{10,... | collective-permute-start | bytes 1585160 | tf_op jit(solution)/shard_map/ppermute | solution.py:23
  7.2 1.2 collective-permute-start.4
  8.4 0.2 collective-permute-start.5
  8.6 0.2 collective-permute-start.10
  8.8 7.9 %collective-permute-done.3.refs_1_ = bf16[2048,128]{1,0:T(8,128)(2,1)S(1)} collective-permute-done((bf16[2048,128]{1,0:T(8,128)(2,1)}, bf16[2048,128]{1,0:T(8,128)(2,1)S(1)}, u32[]{:S(2)}, u32[]{:S(2)}) %collective-permute-start.3) | collective-permute-done | bytes 524320 | tf_op jit(solution)/shard_map/ppermute | solution.py:23
  16.7 2.7 %collective-permute-start.6 = (bf16[2048,128]{1,0:T(8,128)(2,1)}, bf16[2048,128]{1,0:T(8,128)(2,1)S(1)}, u32[]{:S(2)}, u32[]{:S(2)}) collective-permute-start(bf16[2048,128]{1,0:T(8,128)(2,1)} %get-tuple-element.43.refs_0_), channel_id=1, source_target_pairs={{0,4},{4,0},{8,12},{12,8},{16,20},{20,16},{24,28},{28,24},{1,5},{5... | collective-permute-start | bytes 1572872 | tf_op jit(solution)/shard_map/ppermute | solution.py:23
  19.4 11.4 %collective-permute-done.4.refs_2_ = bf16[2048,128]{1,0:T(8,128)(2,1)S(1)} collective-permute-done((bf16[2048,128]{1,0:T(8,128)(2,1)}, bf16[2048,128]{1,0:T(8,128)(2,1)S(1)}, u32[]{:S(2)}, u32[]{:S(2)}) %collective-permute-start.4) | collective-permute-done | bytes 524320 | tf_op jit(solution)/shard_map/ppermute | solution.py:23
  30.8 2.2 %collective-permute-start.7 = (bf16[2048,128]{1,0:T(8,128)(2,1)S(1)}, bf16[2048,128]{1,0:T(8,128)(2,1)S(1)}, u32[]{:S(2)}, u32[]{:S(2)}) collective-permute-start(bf16[2048,128]{1,0:T(8,128)(2,1)S(1)} %collective-permute-done.3.refs_1_), channel_id=1, source_target_pairs={{0,4},{4,0},{8,12},{12,8},{16,20},{20,16},{24,28},{28,24},{1,5},{5... | collective-permute-start | bytes 1572872 | tf_op jit(solution)/shard_map/ppermute | solution.py:23
  33.0 0.5 collective-permute-start.9
  33.5 2.1 %collective-permute-start.2 = (bf16[2064,128]{1,0:T(8,128)(2,1)S(1)}, bf16[2064,128]{1,0:T(8,128)(2,1)S(1)}, u32[]{:S(2)}, u32[]{:S(2)}) collective-permute-start(bf16[2064,128]{1,0:T(8,128)(2,1)S(1)} %collective-permute-done.refs_10_.refs_0_), channel_id=1, source_target_pairs={{2,3},{1,0},{6,7},{5,4},{10,11},{9,8},{14,15},{13,12},{18,19},{17,... | collective-permute-start | bytes 1585160 | tf_op jit(solution)/shard_map/ppermute | solution.py:382
  35.6 2.6 %collective-permute-start.1 = (bf16[2064,128]{1,0:T(8,128)(2,1)}, bf16[2064,128]{1,0:T(8,128)(2,1)S(1)}, u32[]{:S(2)}, u32[]{:S(2)}) collective-permute-start(bf16[2064,128]{1,0:T(8,128)(2,1)} %get-tuple-element.41.refs_8_.refs_0_), channel_id=1, source_target_pairs={{1,2},{2,1},{5,6},{6,5},{9,10},{10,9},{13,14},{14,13},{17,18},{18,... | collective-permute-start | bytes 1585160 | tf_op jit(solution)/shard_map/ppermute | solution.py:383
  38.3 1.0 copy-done
  39.3 1.0 copy-done.3
  40.3 2.5 %early_products.1 = (f32[2048,128]{1,0:T(8,128)S(1)}, bf16[4096,128]{1,0:T(8,128)(2,1)S(1)}, bf16[512,512]{1,0:T(8,128)(2,1)S(1)}, bf16[8,512]{1,0:T(8,128)(2,1)S(1)}) custom-call(bf16[2048,128]{1,0:T(8,128)(2,1)S(1)} %copy-done.3, bf16[2048,128]{1,0:T(8,128)(2,1)S(1)} %collective-permute-done.3.refs_1_, ...), custom_call_target="tpu_custom_call" | custom-call | flops 201326592 | bytes 8941568 | tf_op jit(solution)/shard_map/early_products/pallas_call | solution.py:365
  42.8 4.1 %collective-permute-done.2.refs_1_.refs_2_ = bf16[2064,128]{1,0:T(8,128)(2,1)S(1)} collective-permute-done((bf16[2064,128]{1,0:T(8,128)(2,1)S(1)}, bf16[2064,128]{1,0:T(8,128)(2,1)S(1)}, u32[]{:S(2)}, u32[]{:S(2)}) %collective-permute-start.2) | collective-permute-done | bytes 528416 | tf_op jit(solution)/shard_map/ppermute | solution.py:382
  46.9 4.0 %collective-permute-done.1.refs_0_.refs_1_ = bf16[2064,128]{1,0:T(8,128)(2,1)S(1)} collective-permute-done((bf16[2064,128]{1,0:T(8,128)(2,1)}, bf16[2064,128]{1,0:T(8,128)(2,1)S(1)}, u32[]{:S(2)}, u32[]{:S(2)}) %collective-permute-start.1) | collective-permute-done | bytes 528416 | tf_op jit(solution)/shard_map/ppermute | solution.py:383
  51.0 1.6 %late_products.1 = (bf16[512,128]{1,0:T(8,128)(2,1)S(1)}, bf16[512,128]{1,0:T(8,128)(2,1)}, bf16[512,128]{1,0:T(8,128)(2,1)S(1)}, bf16[512,128]{1,0:T(8,128)(2,1)S(1)}) custom-call(bf16[2064,128]{1,0:T(8,128)(2,1)S(1)} %collective-permute-done.1.refs_0_.refs_1_, bf16[2064,128]{1,0:T(8,128)(2,1)S(1)} %collective-permute-done.2.refs_1_.refs_2_, ...), custom_call_target="tpu_custom_call" | custom-call | flops 67108864 | bytes 3678208 | tf_op jit(solution)/shard_map/late_products/pallas_call | solution.py:365
  52.6 0.1 collective-permute-start.11
  52.7 2.1 %collective-permute-start.12 = (bf16[512,128]{1,0:T(8,128)(2,1)S(1)}, bf16[512,128]{1,0:T(8,128)(2,1)S(1)}, u32[]{:S(2)}, u32[]{:S(2)}) collective-permute-start(bf16[512,128]{1,0:T(8,128)(2,1)S(1)} %get-tuple-element.48), channel_id=1, source_target_pairs={{0,2},{1,3},{2,0},{3,1},{4,6},{5,7},{6,4},{7,5},{8,10},{9,11},{10,... | collective-permute-start | bytes 393224 | tf_op jit(solution)/shard_map/ppermute | solution.py:23
  54.8 0.5 collective-permute-start.13
  55.4 1.4 collective-permute-done.11.refs_1_
  56.7 3.4 %collective-permute-done.12.refs_2_ = bf16[512,128]{1,0:T(8,128)(2,1)S(1)} collective-permute-done((bf16[512,128]{1,0:T(8,128)(2,1)S(1)}, bf16[512,128]{1,0:T(8,128)(2,1)S(1)}, u32[]{:S(2)}, u32[]{:S(2)}) %collective-permute-start.12) | collective-permute-done | bytes 131104 | tf_op jit(solution)/shard_map/ppermute | solution.py:23
  60.1 5.8 %collective-permute-done.13.refs_3_ = bf16[512,128]{1,0:T(8,128)(2,1)S(1)} collective-permute-done((bf16[512,128]{1,0:T(8,128)(2,1)S(1)}, bf16[512,128]{1,0:T(8,128)(2,1)S(1)}, u32[]{:S(2)}, u32[]{:S(2)}) %collective-permute-start.13) | collective-permute-done | bytes 131104 | tf_op jit(solution)/shard_map/ppermute | solution.py:23
  65.9 2.0 %layer.1 = (bf16[512,512]{1,0:T(8,128)(2,1)}, bf16[512,512]{1,0:T(8,128)(2,1)S(1)}, bf16[512,128]{1,0:T(8,128)(2,1)S(1)}, bf16[512,128]{1,0:T(8,128)(2,1)S(1)}, ...) custom-call(bf16[512,128]{1,0:T(8,128)(2,1)S(1)} %get-tuple-element.46.refs_0_, ...), custom_call_target="tpu_custom_call" | custom-call | flops 536870912 | bytes 2646016 | tf_op jit(solution)/shard_map/layer/pallas_call | solution.py:365
  68.0 0.1 collective-permute-start.14
  68.0 3.0 %collective-permute-start.15 = (bf16[512,128]{1,0:T(8,128)(2,1)S(1)}, bf16[512,128]{1,0:T(8,128)(2,1)S(1)}, u32[]{:S(2)}, u32[]{:S(2)}) collective-permute-start(bf16[512,128]{1,0:T(8,128)(2,1)S(1)} %get-tuple-element.55), channel_id=1, source_target_pairs={{0,2},{1,3},{2,0},{3,1},{4,6},{5,7},{6,4},{7,5},{8,10},{9,11},{10,... | collective-permute-start | bytes 393224 | tf_op jit(solution)/shard_map/ppermute | solution.py:23
  71.0 0.6 weight_term.1
  71.6 0.3 collective-permute-done.14.refs_4_.refs_3_
  71.8 7.1 %collective-permute-done.15.refs_5_.refs_4_ = bf16[512,128]{1,0:T(8,128)(2,1)S(1)} collective-permute-done((bf16[512,128]{1,0:T(8,128)(2,1)S(1)}, bf16[512,128]{1,0:T(8,128)(2,1)S(1)}, u32[]{:S(2)}, u32[]{:S(2)}) %collective-permute-start.15) | collective-permute-done | bytes 131104 | tf_op jit(solution)/shard_map/ppermute | solution.py:23
  78.9 3.0 %collective-permute-done.16.refs_6_.refs_5_ = bf16[512,128]{1,0:T(8,128)(2,1)S(1)} collective-permute-done((bf16[512,128]{1,0:T(8,128)(2,1)S(1)}, bf16[512,128]{1,0:T(8,128)(2,1)S(1)}, u32[]{:S(2)}, u32[]{:S(2)}) %collective-permute-start.16) | collective-permute-done | bytes 131104 | tf_op jit(solution)/shard_map/ppermute | solution.py:23
  81.9 2.5 %backward.2 = (bf16[5120,128]{1,0:T(8,128)(2,1)S(1)}, bf16[5120,128]{1,0:T(8,128)(2,1)S(1)}) custom-call(bf16[2064,128]{1,0:T(8,128)(2,1)S(1)} %collective-permute-done.refs_10_.refs_0_, bf16[2064,128]{1,0:T(8,128)(2,1)S(1)} %collective-permute-done.1.refs_0_.refs_1_, bf16[2064,128]{1,0:T(8,128)(2,1)S(1)} %collective-permute-done.2.refs_1_.refs_2_, ...), custom_call_target="tpu_custom_call" | custom-call | flops 134217728 | bytes 5255168 | tf_op jit(solution)/shard_map/backward/pallas_call | solution.py:365
  84.4 2.5 %collective-permute-start.17 = (bf16[5120,128]{1,0:T(8,128)(2,1)S(1)}, bf16[5120,128]{1,0:T(8,128)(2,1)S(1)}, u32[]{:S(2)}, u32[]{:S(2)}) collective-permute-start(bf16[5120,128]{1,0:T(8,128)(2,1)S(1)} %get-tuple-element.61), channel_id=1, source_target_pairs={{0,4},{4,0},{8,12},{12,8},{16,20},{20,16},{24,28},{28,24},{1,5},{5... | collective-permute-start | bytes 3932168 | tf_op jit(solution)/shard_map/ppermute | solution.py:23
  86.9 2.9 %backward.3 = (bf16[4096,128]{1,0:T(8,128)(2,1)S(1)}, bf16[4096,128]{1,0:T(8,128)(2,1)S(1)}) custom-call(bf16[2064,128]{1,0:T(8,128)(2,1)S(1)} %copy-done.1, bf16[2064,128]{1,0:T(8,128)(2,1)S(1)} %collective-permute-done.10.refs_9_.refs_1_, bf16[512,128]{1,0:T(8,128)(2,1)S(1)} %get-tuple-element.53.refs_3_.refs_2_, ...), custom_call_target="tpu_custom_call" | custom-call | flops 134217728 | bytes 3678208 | tf_op jit(solution)/shard_map/backward/pallas_call | solution.py:365
  89.8 0.1 collective-permute-start.21
  89.9 0.3 pair_sum.2
  90.2 1.1 collective-permute-start.18
  91.2 0.5 collective-permute-start.19
  91.8 1.1 collective-permute-start.20
  92.9 0.2 pair_sum.3
  93.1 1.1 collective-permute-start.25
  94.2 0.5 collective-permute-start.26
  94.7 4.3 %collective-permute-done.18.refs_1_ = bf16[1280,128]{1,0:T(8,128)(2,1)S(1)} collective-permute-done((bf16[1280,128]{1,0:T(8,128)(2,1)S(1)}, bf16[1280,128]{1,0:T(8,128)(2,1)S(1)}, u32[]{:S(2)}, u32[]{:S(2)}) %collective-permute-start.18) | collective-permute-done | bytes 327712 | tf_op jit(solution)/shard_map/ppermute | solution.py:23
  99.1 1.2 collective-permute-start.27
  100.3 6.9 %collective-permute-done.20.refs_3_ = bf16[1280,128]{1,0:T(8,128)(2,1)S(1)} collective-permute-done((bf16[1280,128]{1,0:T(8,128)(2,1)S(1)}, bf16[1280,128]{1,0:T(8,128)(2,1)S(1)}, u32[]{:S(2)}, u32[]{:S(2)}) %collective-permute-start.20) | collective-permute-done | bytes 327712 | tf_op jit(solution)/shard_map/ppermute | solution.py:23
  107.2 0.2 plane_sum.2
  107.4 0.6 collective-permute-start.23
  108.0 0.8 collective-permute-start.24
  108.8 2.9 %collective-permute-done.25.refs_1_ = bf16[1024,128]{1,0:T(8,128)(2,1)S(1)} collective-permute-done((bf16[1024,128]{1,0:T(8,128)(2,1)S(1)}, bf16[1024,128]{1,0:T(8,128)(2,1)S(1)}, u32[]{:S(2)}, u32[]{:S(2)}) %collective-permute-start.25) | collective-permute-done | bytes 262176 | tf_op jit(solution)/shard_map/ppermute | solution.py:23
  111.7 1.1 collective-permute-done.26.refs_2_
  112.9 5.6 %collective-permute-done.27.refs_3_ = bf16[1024,128]{1,0:T(8,128)(2,1)S(1)} collective-permute-done((bf16[1024,128]{1,0:T(8,128)(2,1)S(1)}, bf16[1024,128]{1,0:T(8,128)(2,1)S(1)}, u32[]{:S(2)}, u32[]{:S(2)}) %collective-permute-start.27) | collective-permute-done | bytes 262176 | tf_op jit(solution)/shard_map/ppermute | solution.py:23
  118.5 0.1 plane_sum.3
  118.6 0.1 collective-permute-start.31
  118.7 6.8 %collective-permute-done.24.refs_3_ = bf16[768,128]{1,0:T(8,128)(2,1)S(1)} collective-permute-done((bf16[768,128]{1,0:T(8,128)(2,1)S(1)}, bf16[768,128]{1,0:T(8,128)(2,1)S(1)}, u32[]{:S(2)}, u32[]{:S(2)}) %collective-permute-start.24) | collective-permute-done | bytes 196640 | tf_op jit(solution)/shard_map/ppermute | solution.py:23
  125.6 0.6 collective-permute-start.28
  126.2 2.1 %collective-permute-start.30 = (bf16[256,128]{1,0:T(8,128)(2,1)S(1)}, bf16[256,128]{1,0:T(8,128)(2,1)S(1)}, u32[]{:S(2)}, u32[]{:S(2)}) collective-permute-start(bf16[256,128]{1,0:T(8,128)(2,1)S(1)} %weight_total.1.refs_0_), channel_id=1, source_target_pairs={{0,24},{4,28},{8,16},{12,20},{16,8},{20,12},{24,0},{28,4},{1,25},{... | collective-permute-start | bytes 196616 | tf_op jit(solution)/shard_map/ppermute | solution.py:23
  128.3 0.5 collective-permute-done.28.refs_1_
  128.8 0.5 collective-permute-done.29.refs_2_
  129.3 1.1 collective-permute-done.30.refs_3_
  130.4 3.7 %collective-permute-start.32 = (bf16[256,512]{1,0:T(8,128)(2,1)S(1)}, bf16[256,512]{1,0:T(8,128)(2,1)S(1)}, u32[]{:S(2)}, u32[]{:S(2)}) collective-permute-start(bf16[256,512]{1,0:T(8,128)(2,1)S(1)} %weight_half.1.refs_0_), channel_id=1, source_target_pairs={{0,4},{4,0},{8,12},{12,8},{16,20},{20,16},{24,28},{28,24},{1,5},{5... | collective-permute-start | bytes 786440 | tf_op jit(solution)/shard_map/ppermute | solution.py:23
  134.1 0.9 join.1
  135.0 0.2 collective-permute-done.32.refs_1_
  135.3 1.1 weight_whole.1
  (33 shorter events, 0.2 us)
Async XLA Ops:
  1.3 36.9 %copy-start.2 = (bf16[512,512]{1,0:T(8,128)(2,1)S(1)}, bf16[512,512]{1,0:T(8,128)(2,1)}, u32[]{:S(2)}) copy-start(bf16[512,512]{1,0:T(8,128)(2,1)} %refs_11_.1) | copy-start | bytes 1572868
  1.3 36.9 %copy-start.4 = (bf16[8,512]{1,0:T(8,128)(2,1)S(1)}, bf16[8,512]{1,0:T(8,128)(2,1)}, u32[]{:S(2)}) copy-start(bf16[8,512]{1,0:T(8,128)(2,1)} %refs_12_.1) | copy-start | bytes 24580
  3.6 13.1 %collective-permute-start.3 = (bf16[2048,128]{1,0:T(8,128)(2,1)}, bf16[2048,128]{1,0:T(8,128)(2,1)S(1)}, u32[]{:S(2)}, u32[]{:S(2)}) collective-permute-start(bf16[2048,128]{1,0:T(8,128)(2,1)} %get-tuple-element.43.refs_0_), channel_id=1, source_target_pairs={{0,8},{4,12},{8,0},{12,4},{16,24},{20,28},{24,16},{28,20},{1,9},{5... | collective-permute-start | bytes 1572872 | tf_op jit(solution)/shard_map/ppermute | solution.py:23
  4.9 28.1 %collective-permute-start = (bf16[2064,128]{1,0:T(8,128)(2,1)}, bf16[2064,128]{1,0:T(8,128)(2,1)S(1)}, u32[]{:S(2)}, u32[]{:S(2)}) collective-permute-start(bf16[2064,128]{1,0:T(8,128)(2,1)} %get-tuple-element.41.refs_8_.refs_0_), channel_id=1, source_target_pairs={{0,2},{1,3},{2,0},{3,1},{4,6},{5,7},{6,4},{7,5},{8,10},{9,11},{10,... | collective-permute-start | bytes 1585160 | tf_op jit(solution)/shard_map/ppermute | solution.py:23
  7.2 23.6 %collective-permute-start.4 = (bf16[2048,128]{1,0:T(8,128)(2,1)}, bf16[2048,128]{1,0:T(8,128)(2,1)S(1)}, u32[]{:S(2)}, u32[]{:S(2)}) collective-permute-start(bf16[2048,128]{1,0:T(8,128)(2,1)} %get-tuple-element.43.refs_0_), channel_id=1, source_target_pairs={{0,16},{4,20},{8,24},{12,28},{16,0},{20,4},{24,8},{28,12},{1,17},{... | collective-permute-start | bytes 1572872 | tf_op jit(solution)/shard_map/ppermute | solution.py:23
  8.4 24.5 %collective-permute-start.5 = (bf16[2048,128]{1,0:T(8,128)(2,1)}, bf16[2048,128]{1,0:T(8,128)(2,1)S(1)}, u32[]{:S(2)}, u32[]{:S(2)}) collective-permute-start(bf16[2048,128]{1,0:T(8,128)(2,1)} %get-tuple-element.43.refs_0_), channel_id=1, source_target_pairs={{0,24},{4,28},{8,16},{12,20},{16,8},{20,12},{24,0},{28,4},{1,25},{... | collective-permute-start | bytes 1572872 | tf_op jit(solution)/shard_map/ppermute | solution.py:23
  8.6 27.0 %collective-permute-start.10 = (bf16[2064,128]{1,0:T(8,128)(2,1)}, bf16[2064,128]{1,0:T(8,128)(2,1)S(1)}, u32[]{:S(2)}, u32[]{:S(2)}) collective-permute-start(bf16[2064,128]{1,0:T(8,128)(2,1)} %get-tuple-element.41.refs_8_.refs_0_), channel_id=1, source_target_pairs={{0,1},{1,0},{2,3},{3,2},{4,5},{5,4},{6,7},{7,6},{8,9},{9,8},{10,11... | collective-permute-start | bytes 1585160 | tf_op jit(solution)/shard_map/ppermute | solution.py:23
  16.7 16.8 %collective-permute-start.6 = (bf16[2048,128]{1,0:T(8,128)(2,1)}, bf16[2048,128]{1,0:T(8,128)(2,1)S(1)}, u32[]{:S(2)}, u32[]{:S(2)}) collective-permute-start(bf16[2048,128]{1,0:T(8,128)(2,1)} %get-tuple-element.43.refs_0_), channel_id=1, source_target_pairs={{0,4},{4,0},{8,12},{12,8},{16,20},{20,16},{24,28},{28,24},{1,5},{5... | collective-permute-start | bytes 1572872 | tf_op jit(solution)/shard_map/ppermute | solution.py:23
  30.8 7.4 %collective-permute-start.7 = (bf16[2048,128]{1,0:T(8,128)(2,1)S(1)}, bf16[2048,128]{1,0:T(8,128)(2,1)S(1)}, u32[]{:S(2)}, u32[]{:S(2)}) collective-permute-start(bf16[2048,128]{1,0:T(8,128)(2,1)S(1)} %collective-permute-done.3.refs_1_), channel_id=1, source_target_pairs={{0,4},{4,0},{8,12},{12,8},{16,20},{20,16},{24,28},{28,24},{1,5},{5... | collective-permute-start | bytes 1572872 | tf_op jit(solution)/shard_map/ppermute | solution.py:23
  33.0 5.2 %collective-permute-start.8 = (bf16[2048,128]{1,0:T(8,128)(2,1)S(1)}, bf16[2048,128]{1,0:T(8,128)(2,1)S(1)}, u32[]{:S(2)}, u32[]{:S(2)}) collective-permute-start(bf16[2048,128]{1,0:T(8,128)(2,1)S(1)} %collective-permute-done.4.refs_2_), channel_id=1, source_target_pairs={{0,4},{4,0},{8,12},{12,8},{16,20},{20,16},{24,28},{28,24},{1,5},{5... | collective-permute-start | bytes 1572872 | tf_op jit(solution)/shard_map/ppermute | solution.py:23
  33.0 5.2 %collective-permute-start.9 = (bf16[2048,128]{1,0:T(8,128)(2,1)S(1)}, bf16[2048,128]{1,0:T(8,128)(2,1)S(1)}, u32[]{:S(2)}, u32[]{:S(2)}) collective-permute-start(bf16[2048,128]{1,0:T(8,128)(2,1)S(1)} %collective-permute-done.5.refs_3_), channel_id=1, source_target_pairs={{0,4},{4,0},{8,12},{12,8},{16,20},{20,16},{24,28},{28,24},{1,5},{5... | collective-permute-start | bytes 1572872 | tf_op jit(solution)/shard_map/ppermute | solution.py:23
  33.5 13.4 %collective-permute-start.2 = (bf16[2064,128]{1,0:T(8,128)(2,1)S(1)}, bf16[2064,128]{1,0:T(8,128)(2,1)S(1)}, u32[]{:S(2)}, u32[]{:S(2)}) collective-permute-start(bf16[2064,128]{1,0:T(8,128)(2,1)S(1)} %collective-permute-done.refs_10_.refs_0_), channel_id=1, source_target_pairs={{2,3},{1,0},{6,7},{5,4},{10,11},{9,8},{14,15},{13,12},{18,19},{17,... | collective-permute-start | bytes 1585160 | tf_op jit(solution)/shard_map/ppermute | solution.py:382
  35.6 15.4 %collective-permute-start.1 = (bf16[2064,128]{1,0:T(8,128)(2,1)}, bf16[2064,128]{1,0:T(8,128)(2,1)S(1)}, u32[]{:S(2)}, u32[]{:S(2)}) collective-permute-start(bf16[2064,128]{1,0:T(8,128)(2,1)} %get-tuple-element.41.refs_8_.refs_0_), channel_id=1, source_target_pairs={{1,2},{2,1},{5,6},{6,5},{9,10},{10,9},{13,14},{14,13},{17,18},{18,... | collective-permute-start | bytes 1585160 | tf_op jit(solution)/shard_map/ppermute | solution.py:383
  38.2 1.0 copy-start
  39.3 1.0 copy-start.3
  51.0 4.4 %copy-start.5 = (s32[2048]{0:T(1024)S(1)}, s32[2048]{0:T(1024)}, u32[]{:S(2)}) copy-start(s32[2048]{0:T(1024)} %param.12) | copy-start | bytes 24580
  51.0 4.4 %copy-start.6 = (s32[2048]{0:T(1024)S(1)}, s32[2048]{0:T(1024)}, u32[]{:S(2)}) copy-start(s32[2048]{0:T(1024)} %param.13) | copy-start | bytes 24580
  52.6 4.1 %collective-permute-start.11 = (bf16[512,128]{1,0:T(8,128)(2,1)}, bf16[512,128]{1,0:T(8,128)(2,1)S(1)}, u32[]{:S(2)}, u32[]{:S(2)}) collective-permute-start(bf16[512,128]{1,0:T(8,128)(2,1)} %get-tuple-element.47), channel_id=1, source_target_pairs={{0,1},{1,0},{2,3},{3,2},{4,5},{5,4},{6,7},{7,6},{8,9},{9,8},{10,11... | collective-permute-start | bytes 393224 | tf_op jit(solution)/shard_map/ppermute | solution.py:23
  52.7 7.4 %collective-permute-start.12 = (bf16[512,128]{1,0:T(8,128)(2,1)S(1)}, bf16[512,128]{1,0:T(8,128)(2,1)S(1)}, u32[]{:S(2)}, u32[]{:S(2)}) collective-permute-start(bf16[512,128]{1,0:T(8,128)(2,1)S(1)} %get-tuple-element.48), channel_id=1, source_target_pairs={{0,2},{1,3},{2,0},{3,1},{4,6},{5,7},{6,4},{7,5},{8,10},{9,11},{10,... | collective-permute-start | bytes 393224 | tf_op jit(solution)/shard_map/ppermute | solution.py:23
  54.8 11.2 %collective-permute-start.13 = (bf16[512,128]{1,0:T(8,128)(2,1)S(1)}, bf16[512,128]{1,0:T(8,128)(2,1)S(1)}, u32[]{:S(2)}, u32[]{:S(2)}) collective-permute-start(bf16[512,128]{1,0:T(8,128)(2,1)S(1)} %get-tuple-element.49), channel_id=1, source_target_pairs={{0,3},{1,2},{2,1},{3,0},{4,7},{5,6},{6,5},{7,4},{8,11},{9,10},{10,... | collective-permute-start | bytes 393224 | tf_op jit(solution)/shard_map/ppermute | solution.py:23
  68.0 3.9 %collective-permute-start.14 = (bf16[512,128]{1,0:T(8,128)(2,1)S(1)}, bf16[512,128]{1,0:T(8,128)(2,1)S(1)}, u32[]{:S(2)}, u32[]{:S(2)}) collective-permute-start(bf16[512,128]{1,0:T(8,128)(2,1)S(1)} %get-tuple-element.54), channel_id=1, source_target_pairs={{0,1},{1,0},{2,3},{3,2},{4,5},{5,4},{6,7},{7,6},{8,9},{9,8},{10,11... | collective-permute-start | bytes 393224 | tf_op jit(solution)/shard_map/ppermute | solution.py:23
  68.0 10.9 %collective-permute-start.15 = (bf16[512,128]{1,0:T(8,128)(2,1)S(1)}, bf16[512,128]{1,0:T(8,128)(2,1)S(1)}, u32[]{:S(2)}, u32[]{:S(2)}) collective-permute-start(bf16[512,128]{1,0:T(8,128)(2,1)S(1)} %get-tuple-element.55), channel_id=1, source_target_pairs={{0,2},{1,3},{2,0},{3,1},{4,6},{5,7},{6,4},{7,5},{8,10},{9,11},{10,... | collective-permute-start | bytes 393224 | tf_op jit(solution)/shard_map/ppermute | solution.py:23
  71.0 10.9 %collective-permute-start.16 = (bf16[512,128]{1,0:T(8,128)(2,1)S(1)}, bf16[512,128]{1,0:T(8,128)(2,1)S(1)}, u32[]{:S(2)}, u32[]{:S(2)}) collective-permute-start(bf16[512,128]{1,0:T(8,128)(2,1)S(1)} %get-tuple-element.56), channel_id=1, source_target_pairs={{0,3},{1,2},{2,1},{3,0},{4,7},{5,6},{6,5},{7,4},{8,11},{9,10},{10,... | collective-permute-start | bytes 393224 | tf_op jit(solution)/shard_map/ppermute | solution.py:23
  81.9 5.0 %copy-start.1 = (bf16[2064,128]{1,0:T(8,128)(2,1)S(1)}, bf16[2064,128]{1,0:T(8,128)(2,1)}, u32[]{:S(2)}) copy-start(bf16[2064,128]{1,0:T(8,128)(2,1)} %get-tuple-element.41.refs_8_.refs_0_) | copy-start | bytes 1585156
  84.4 5.5 %collective-permute-start.17 = (bf16[5120,128]{1,0:T(8,128)(2,1)S(1)}, bf16[5120,128]{1,0:T(8,128)(2,1)S(1)}, u32[]{:S(2)}, u32[]{:S(2)}) collective-permute-start(bf16[5120,128]{1,0:T(8,128)(2,1)S(1)} %get-tuple-element.61), channel_id=1, source_target_pairs={{0,4},{4,0},{8,12},{12,8},{16,20},{20,16},{24,28},{28,24},{1,5},{5... | collective-permute-start | bytes 3932168 | tf_op jit(solution)/shard_map/ppermute | solution.py:23
  89.8 3.1 %collective-permute-start.21 = (bf16[4096,128]{1,0:T(8,128)(2,1)S(1)}, bf16[4096,128]{1,0:T(8,128)(2,1)S(1)}, u32[]{:S(2)}, u32[]{:S(2)}) collective-permute-start(bf16[4096,128]{1,0:T(8,128)(2,1)S(1)} %get-tuple-element.67), channel_id=1, source_target_pairs={{0,4},{4,0},{8,12},{12,8},{16,20},{20,16},{24,28},{28,24},{1,5},{5... | collective-permute-start | bytes 3145736 | tf_op jit(solution)/shard_map/ppermute | solution.py:23
  90.2 8.9 %collective-permute-start.18 = (bf16[1280,128]{1,0:T(8,128)(2,1)S(1)}, bf16[1280,128]{1,0:T(8,128)(2,1)S(1)}, u32[]{:S(2)}, u32[]{:S(2)}) collective-permute-start(bf16[1280,128]{1,0:T(8,128)(2,1)S(1)} %get-tuple-element.64), channel_id=1, source_target_pairs={{0,8},{4,12},{8,0},{12,4},{16,24},{20,28},{24,16},{28,20},{1,9},{5... | collective-permute-start | bytes 983048 | tf_op jit(solution)/shard_map/ppermute | solution.py:23
  91.2 9.0 %collective-permute-start.19 = (bf16[1280,128]{1,0:T(8,128)(2,1)S(1)}, bf16[1280,128]{1,0:T(8,128)(2,1)S(1)}, u32[]{:S(2)}, u32[]{:S(2)}) collective-permute-start(bf16[1280,128]{1,0:T(8,128)(2,1)S(1)} %get-tuple-element.65), channel_id=1, source_target_pairs={{0,16},{4,20},{8,24},{12,28},{16,0},{20,4},{24,8},{28,12},{1,17},{... | collective-permute-start | bytes 983048 | tf_op jit(solution)/shard_map/ppermute | solution.py:23
  91.8 15.5 %collective-permute-start.20 = (bf16[1280,128]{1,0:T(8,128)(2,1)S(1)}, bf16[1280,128]{1,0:T(8,128)(2,1)S(1)}, u32[]{:S(2)}, u32[]{:S(2)}) collective-permute-start(bf16[1280,128]{1,0:T(8,128)(2,1)S(1)} %get-tuple-element.66), channel_id=1, source_target_pairs={{0,24},{4,28},{8,16},{12,20},{16,8},{20,12},{24,0},{28,4},{1,25},{... | collective-permute-start | bytes 983048 | tf_op jit(solution)/shard_map/ppermute | solution.py:23
  93.1 18.6 %collective-permute-start.25 = (bf16[1024,128]{1,0:T(8,128)(2,1)S(1)}, bf16[1024,128]{1,0:T(8,128)(2,1)S(1)}, u32[]{:S(2)}, u32[]{:S(2)}) collective-permute-start(bf16[1024,128]{1,0:T(8,128)(2,1)S(1)} %get-tuple-element.72), channel_id=1, source_target_pairs={{0,8},{4,12},{8,0},{12,4},{16,24},{20,28},{24,16},{28,20},{1,9},{5... | collective-permute-start | bytes 786440 | tf_op jit(solution)/shard_map/ppermute | solution.py:23
  94.2 18.7 %collective-permute-start.26 = (bf16[1024,128]{1,0:T(8,128)(2,1)S(1)}, bf16[1024,128]{1,0:T(8,128)(2,1)S(1)}, u32[]{:S(2)}, u32[]{:S(2)}) collective-permute-start(bf16[1024,128]{1,0:T(8,128)(2,1)S(1)} %get-tuple-element.73), channel_id=1, source_target_pairs={{0,16},{4,20},{8,24},{12,28},{16,0},{20,4},{24,8},{28,12},{1,17},{... | collective-permute-start | bytes 786440 | tf_op jit(solution)/shard_map/ppermute | solution.py:23
  99.1 19.4 %collective-permute-start.27 = (bf16[1024,128]{1,0:T(8,128)(2,1)S(1)}, bf16[1024,128]{1,0:T(8,128)(2,1)S(1)}, u32[]{:S(2)}, u32[]{:S(2)}) collective-permute-start(bf16[1024,128]{1,0:T(8,128)(2,1)S(1)} %get-tuple-element.74), channel_id=1, source_target_pairs={{0,24},{4,28},{8,16},{12,20},{16,8},{20,12},{24,0},{28,4},{1,25},{... | collective-permute-start | bytes 786440 | tf_op jit(solution)/shard_map/ppermute | solution.py:23
  107.4 11.3 %collective-permute-start.23 = (bf16[768,128]{1,0:T(8,128)(2,1)S(1)}, bf16[768,128]{1,0:T(8,128)(2,1)S(1)}, u32[]{:S(2)}, u32[]{:S(2)}) collective-permute-start(bf16[768,128]{1,0:T(8,128)(2,1)S(1)} %get-tuple-element.70), channel_id=1, source_target_pairs={{0,2},{1,3},{2,0},{3,1},{4,6},{5,7},{6,4},{7,5},{8,10},{9,11},{10,... | collective-permute-start | bytes 589832 | tf_op jit(solution)/shard_map/ppermute | solution.py:23
  108.0 17.6 %collective-permute-start.24 = (bf16[768,128]{1,0:T(8,128)(2,1)S(1)}, bf16[768,128]{1,0:T(8,128)(2,1)S(1)}, u32[]{:S(2)}, u32[]{:S(2)}) collective-permute-start(bf16[768,128]{1,0:T(8,128)(2,1)S(1)} %get-tuple-element.71), channel_id=1, source_target_pairs={{0,3},{1,2},{2,1},{3,0},{4,7},{5,6},{6,5},{7,4},{8,11},{9,10},{10,... | collective-permute-start | bytes 589832 | tf_op jit(solution)/shard_map/ppermute | solution.py:23
  111.7 6.9 %collective-permute-start.22 = (bf16[256,128]{1,0:T(8,128)(2,1)S(1)}, bf16[256,128]{1,0:T(8,128)(2,1)S(1)}, u32[]{:S(2)}, u32[]{:S(2)}) collective-permute-start(bf16[256,128]{1,0:T(8,128)(2,1)S(1)} %get-tuple-element.69.refs_0_), channel_id=1, source_target_pairs={{0,1},{1,0},{2,3},{3,2},{4,5},{5,4},{6,7},{7,6},{8,9},{9,8},{10,11... | collective-permute-start | bytes 196616 | tf_op jit(solution)/shard_map/ppermute | solution.py:23
  118.6 9.7 %collective-permute-start.31 = (bf16[512,128]{1,0:T(8,128)(2,1)S(1)}, bf16[512,128]{1,0:T(8,128)(2,1)S(1)}, u32[]{:S(2)}, u32[]{:S(2)}) collective-permute-start(bf16[512,128]{1,0:T(8,128)(2,1)S(1)} %get-tuple-element.76), channel_id=1, source_target_pairs={{0,1},{1,0},{2,3},{3,2},{4,5},{5,4},{6,7},{7,6},{8,9},{9,8},{10,11... | collective-permute-start | bytes 393224 | tf_op jit(solution)/shard_map/ppermute | solution.py:23
  125.6 3.2 %collective-permute-start.28 = (bf16[256,128]{1,0:T(8,128)(2,1)S(1)}, bf16[256,128]{1,0:T(8,128)(2,1)S(1)}, u32[]{:S(2)}, u32[]{:S(2)}) collective-permute-start(bf16[256,128]{1,0:T(8,128)(2,1)S(1)} %weight_total.1.refs_0_), channel_id=1, source_target_pairs={{0,8},{4,12},{8,0},{12,4},{16,24},{20,28},{24,16},{28,20},{1,9},{5... | collective-permute-start | bytes 196616 | tf_op jit(solution)/shard_map/ppermute | solution.py:23
  126.2 3.1 %collective-permute-start.29 = (bf16[256,128]{1,0:T(8,128)(2,1)S(1)}, bf16[256,128]{1,0:T(8,128)(2,1)S(1)}, u32[]{:S(2)}, u32[]{:S(2)}) collective-permute-start(bf16[256,128]{1,0:T(8,128)(2,1)S(1)} %weight_total.1.refs_0_), channel_id=1, source_target_pairs={{0,16},{4,20},{8,24},{12,28},{16,0},{20,4},{24,8},{28,12},{1,17},{... | collective-permute-start | bytes 196616 | tf_op jit(solution)/shard_map/ppermute | solution.py:23
  126.2 4.2 %collective-permute-start.30 = (bf16[256,128]{1,0:T(8,128)(2,1)S(1)}, bf16[256,128]{1,0:T(8,128)(2,1)S(1)}, u32[]{:S(2)}, u32[]{:S(2)}) collective-permute-start(bf16[256,128]{1,0:T(8,128)(2,1)S(1)} %weight_total.1.refs_0_), channel_id=1, source_target_pairs={{0,24},{4,28},{8,16},{12,20},{16,8},{20,12},{24,0},{28,4},{1,25},{... | collective-permute-start | bytes 196616 | tf_op jit(solution)/shard_map/ppermute | solution.py:23
  130.4 4.9 %collective-permute-start.32 = (bf16[256,512]{1,0:T(8,128)(2,1)S(1)}, bf16[256,512]{1,0:T(8,128)(2,1)S(1)}, u32[]{:S(2)}, u32[]{:S(2)}) collective-permute-start(bf16[256,512]{1,0:T(8,128)(2,1)S(1)} %weight_half.1.refs_0_), channel_id=1, source_target_pairs={{0,4},{4,0},{8,12},{12,8},{16,20},{20,16},{24,28},{28,24},{1,5},{5... | collective-permute-start | bytes 786440 | tf_op jit(solution)/shard_map/ppermute | solution.py:23

commit v3 on v2

--- a/solution.py
+++ b/solution.py
@@ -23,12 +23,13 @@
     return lax.ppermute(value, axis, [(i, i ^ flip) for i in range(size)])
 
 
-def load_ids(ids_vmem, ids_smem, lists, slots, sem):
+def load_ids(ids_vmem, ids_smem, lists, slots, sem, meanwhile):
     for d in range(lists.shape[0]):
         rows = lists[d, slots * BLOCK :, :].astype(jnp.float32)
         ids_vmem[d] = rows.astype(jnp.int32)[:8]
     copy = pltpu.make_async_copy(ids_vmem, ids_smem, sem)
     copy.start()
+    meanwhile()
     copy.wait()
 
 
@@ -125,10 +126,13 @@
         copies.append(pltpu.make_async_copy(source, target, sems.at[len(copies)]))
     for copy in copies:
         copy.start()
-    totals[...] = jnp.zeros_like(totals)
+
+    def clear():
+        totals[...] = jnp.zeros_like(totals)
+
     for copy in copies[:early]:
         copy.wait()
-    load_ids(ids_vmem, ids_smem, lists, slots, id_sem)
+    load_ids(ids_vmem, ids_smem, lists, slots, id_sem, clear)
     for copy in copies[early:]:
         copy.wait()
     visit = forward_visit(panels, panel_rows, lists, ids_smem, totals)
@@ -142,9 +146,12 @@
     outs = refs[4 : 4 + teams]
     totals, lists, ids_vmem, ids_smem, sem, id_sem = refs[4 + teams :]
     fetch = fetch_late(place, teams, middle, relayed, lists.at[0], sem)
-    totals[...] = begun[...]
+
+    def take():
+        totals[...] = begun[...]
+
     fetch.wait()
-    load_ids(ids_vmem, ids_smem, lists, slots, id_sem)
+    load_ids(ids_vmem, ids_smem, lists, slots, id_sem, take)
     visit = forward_visit(panel, 0, lists, ids_smem, totals)
     each_group(ids_smem, place, [teams - 1], visit)
     share = outs[0].shape[0]
@@ -273,10 +280,13 @@
         target = rows.at[pl.ds(start, share), :]
         moves.append(pltpu.make_async_copy(backs[d], target, sems.at[count + d]))
         moves[-1].start()
-    totals[...] = jnp.zeros_like(totals)
+
+    def clear():
+        totals[...] = jnp.zeros_like(totals)
+
     for copy in copies:
         copy.wait()
-    load_ids(ids_vmem, ids_smem, lists, slots, id_sem)
+    load_ids(ids_vmem, ids_smem, lists, slots, id_sem, clear)
     for copy in moves:
         copy.wait()
 
@@ -369,17 +379,19 @@
         out_specs=[pl.BlockSpec(memory_space=pltpu.VMEM) for _ in out_shapes],
         out_shape=out_shapes,
         scratch_shapes=scratch,
-        cost_estimate=pl.CostEstimate(flops=flops, bytes_accessed=moved, transcendentals=0),
+        cost_estimate=pl.CostEstimate(
+            flops=flops, bytes_accessed=moved if flops else 0, transcendentals=0
+        ),
         compiler_params=pltpu.CompilerParams(vmem_limit_bytes=limit),
     )(*operands, *after)
 
 
-def gather_lists(mine, teams):
+def gather_lists(mine, teams, gate):
     if teams == 4:
         two = swap(mine, "team", 2)
         one = swap(mine, "team", 1)
-        held, two = lax.optimization_barrier((mine, two))
         relayed = lax.ppermute(two, "team", [(2, 3), (1, 0)])
+        held, _ = lax.optimization_barrier((mine, gate(two, one)))
         middle = lax.ppermute(held, "team", [(1, 2), (2, 1)])
         return [mine, one, two], [middle, relayed]
     early = [mine] + [swap(mine, "team", d) for d in range(1, teams - 1)]
@@ -444,9 +456,11 @@
     )
     mine = prepared[0]
     own = prepared[1] if aligned else lax.dynamic_slice_in_dim(features, team * part, part, 1)
-    early, late = gather_lists(mine, teams)
+    beside = swap(own, "row", 1)
+    own, beside = lax.optimization_barrier((own, beside))
     near = [own] + [swap(own, "row", 2 * d) for d in range(1, chips)]
-    far = [swap(value, "row", 1) for value in near]
+    early, late = gather_lists(mine, teams, lambda two, one: one)
+    far = [beside] + [swap(value, "row", 1) for value in near[1:]]
 
     ids = id_scratch(teams - 1)
     begun, late_panel, weight_here, table_here = call(
@@ -466,7 +480,7 @@
             pltpu.SemaphoreType.DMA((2 * chips + teams + 1,)),
             pltpu.SemaphoreType.DMA,
         ],
-        (teams - 1) * list_flops,
+        0,
         (nodes + panel_rows) * padded * 2 + teams * list_bytes + slab * padded * 4 + 4 * MIB,
     )
     ids = id_scratch(1)

time: 137 us -> 131 us (0.956)
  waiting for transfers between devices: 78.5 us -> 72.1 us
    ppermute x1, waiting for transfers between devices: 4.12 us -> 0.01 us  [gather_lists(): relayed = lax.ppermute(two, 'team', [(2, 3), (1, 0)])]
    ppermute x1, waiting for transfers between devices: 4.05 us -> 0.01 us  [gather_lists(): middle = lax.ppermute(held, 'team', [(1, 2), (2, 1)])]
    ppermute x31, waiting for transfers between devices: 70.4 us -> 72.1 us  [swap(): return lax.ppermute(value, axis, [(i, i ^ flip) for i in range(size)])]
where the time goes in v3:
time: 131 us; the launch traced here: 130 us
  waiting for transfers between devices  72.1 us (55%)
  starting transfers between devices  36.6 us (28%)
  Pallas kernels  18 us (14%)
  local copies, waits for them, and re-layouts  2.13 us (2%)
  between operations  1.5 us (1%)
    ppermute x31, waiting for transfers between devices, swap(): return lax.ppermute(value, axis, [(i, i ^ flip) for i in range(size)])  72.1 us
    ppermute x31, starting transfers between devices, swap(): return lax.ppermute(value, axis, [(i, i ^ flip) for i in range(size)])  31.9 us
    pallas_call x15, Pallas kernels, call(): pl.pallas_call(body, name=name, in_specs=specs, out_specs=[pl.BlockSpec(m...  18 us
    ppermute x1, starting transfers between devices, gather_lists(): middle = lax.ppermute(held, 'team', [(1, 2), (2, 1)])  3.2 us
  transfers between devices with their start and end apart: 33, of which 20 were waited for; matrix products, arithmetic and copies ran while one was open for 0% of the time, Pallas kernels for 6%

profile of v3, /device:TPU:9, one launch (start us, length us, event | category | flops | bytes accessed | tf_op | source)
XLA Modules:
  0.0 130.3 jit_solution(10615173682165876142)
XLA Ops:
  1.3 2.3 %prepare.1 = (bf16[2064,128]{1,0:T(8,128)(2,1)}, bf16[2048,128]{1,0:T(8,128)(2,1)}) custom-call(bf16[2048,128]{1,0:T(8,128)(2,1)} %bitcast.5, s32[1,16]{1,0:T(1,128)} %bitcast.6, s32[1,16]{1,0:T(1,128)} %bitcast.7, s32[1,1]{1,0:T(1,128)S(6)} %copy.12.refs_3_, bf16[2048,512]{1,0:T(8,128)(2,1)} %refs_4_.1), custom_call_target="tpu_custom_call" | custom-call | tf_op jit(solution)/shard_map/prepare/pallas_call | solution.py:375
  3.6 0.7 collective-permute-start.4
  4.3 2.5 %collective-permute-start.2 = (bf16[2064,128]{1,0:T(8,128)(2,1)}, bf16[2064,128]{1,0:T(8,128)(2,1)S(1)}, u32[]{:S(2)}, u32[]{:S(2)}) collective-permute-start(bf16[2064,128]{1,0:T(8,128)(2,1)} %get-tuple-element.42.refs_8_.refs_0_), channel_id=1, source_target_pairs={{0,2},{1,3},{2,0},{3,1},{4,6},{5,7},{6,4},{7,5},{8,10},{9,11},{10,... | collective-permute-start | bytes 1585160 | tf_op jit(solution)/shard_map/ppermute | solution.py:23
  6.8 2.2 %collective-permute-start.7 = (bf16[2048,128]{1,0:T(8,128)(2,1)}, bf16[2048,128]{1,0:T(8,128)(2,1)S(1)}, u32[]{:S(2)}, u32[]{:S(2)}) collective-permute-start(bf16[2048,128]{1,0:T(8,128)(2,1)} %get-tuple-element.44.refs_0_), channel_id=1, source_target_pairs={{0,24},{4,28},{8,16},{12,20},{16,8},{20,12},{24,0},{28,4},{1,25},{... | collective-permute-start | bytes 1572872 | tf_op jit(solution)/shard_map/ppermute | solution.py:23
  9.0 0.3 collective-permute-start.5
  9.3 0.2 collective-permute-start.6
  9.5 17.9 %collective-permute-done.refs_9_.refs_1_ = bf16[2064,128]{1,0:T(8,128)(2,1)S(1)} collective-permute-done((bf16[2064,128]{1,0:T(8,128)(2,1)}, bf16[2064,128]{1,0:T(8,128)(2,1)S(1)}, u32[]{:S(2)}, u32[]{:S(2)}) %collective-permute-start) | collective-permute-done | bytes 528416 | tf_op jit(solution)/shard_map/ppermute | solution.py:23
  27.4 3.2 %collective-permute-start.1 = (bf16[2064,128]{1,0:T(8,128)(2,1)}, bf16[2064,128]{1,0:T(8,128)(2,1)S(1)}, u32[]{:S(2)}, u32[]{:S(2)}) collective-permute-start(bf16[2064,128]{1,0:T(8,128)(2,1)} %get-tuple-element.42.refs_8_.refs_0_), channel_id=1, source_target_pairs={{1,2},{2,1},{5,6},{6,5},{9,10},{10,9},{13,14},{14,13},{17,18},{18,... | collective-permute-start | bytes 1585160 | tf_op jit(solution)/shard_map/ppermute | solution.py:395
  30.6 1.5 %collective-permute-start.3 = (bf16[2064,128]{1,0:T(8,128)(2,1)S(1)}, bf16[2064,128]{1,0:T(8,128)(2,1)S(1)}, u32[]{:S(2)}, u32[]{:S(2)}) collective-permute-start(bf16[2064,128]{1,0:T(8,128)(2,1)S(1)} %collective-permute-done.2.refs_10_.refs_0_), channel_id=1, source_target_pairs={{2,3},{1,0},{6,7},{5,4},{10,11},{9,8},{14,15},{13,12},{18,19},{17,... | collective-permute-start | bytes 1585160 | tf_op jit(solution)/shard_map/ppermute | solution.py:393
  32.2 2.9 %collective-permute-start.10 = (bf16[2048,128]{1,0:T(8,128)(2,1)S(1)}, bf16[2048,128]{1,0:T(8,128)(2,1)S(1)}, u32[]{:S(2)}, u32[]{:S(2)}) collective-permute-start(bf16[2048,128]{1,0:T(8,128)(2,1)S(1)} %collective-permute-done.7.refs_3_), channel_id=1, source_target_pairs={{0,4},{4,0},{8,12},{12,8},{16,20},{20,16},{24,28},{28,24},{1,5},{5... | collective-permute-start | bytes 1572872 | tf_op jit(solution)/shard_map/ppermute | solution.py:23
  35.0 0.1 collective-permute-start.8
  35.1 0.4 collective-permute-start.9
  35.6 1.0 collective-permute-done.10.refs_7_
  36.6 0.7 collective-permute-done.8.refs_5_
  37.3 0.7 collective-permute-done.9.refs_6_
  38.1 1.0 copy-done
  39.1 1.0 copy-done.3
  40.2 2.6 %early_products.1 = (f32[2048,128]{1,0:T(8,128)S(1)}, bf16[4096,128]{1,0:T(8,128)(2,1)S(1)}, bf16[512,512]{1,0:T(8,128)(2,1)S(1)}, bf16[8,512]{1,0:T(8,128)(2,1)S(1)}) custom-call(bf16[2048,128]{1,0:T(8,128)(2,1)S(1)} %copy-done.3, bf16[2048,128]{1,0:T(8,128)(2,1)S(1)} %collective-permute-done.5.refs_1_, ...), custom_call_target="tpu_custom_call" | custom-call | tf_op jit(solution)/shard_map/early_products/pallas_call | solution.py:375
  42.9 1.8 %late_products.1 = (bf16[512,128]{1,0:T(8,128)(2,1)S(1)}, bf16[512,128]{1,0:T(8,128)(2,1)}, bf16[512,128]{1,0:T(8,128)(2,1)S(1)}, bf16[512,128]{1,0:T(8,128)(2,1)S(1)}) custom-call(bf16[2064,128]{1,0:T(8,128)(2,1)S(1)} %collective-permute-done.1.refs_0_.refs_1_, bf16[2064,128]{1,0:T(8,128)(2,1)S(1)} %collective-permute-done.3.refs_1_.refs_2_, ...), custom_call_target="tpu_custom_call" | custom-call | flops 67108864 | bytes 3678208 | tf_op jit(solution)/shard_map/late_products/pallas_call | solution.py:375
  44.6 0.3 collective-permute-start.11
  44.9 3.8 %collective-permute-start.12 = (bf16[512,128]{1,0:T(8,128)(2,1)S(1)}, bf16[512,128]{1,0:T(8,128)(2,1)S(1)}, u32[]{:S(2)}, u32[]{:S(2)}) collective-permute-start(bf16[512,128]{1,0:T(8,128)(2,1)S(1)} %get-tuple-element.50), channel_id=1, source_target_pairs={{0,2},{1,3},{2,0},{3,1},{4,6},{5,7},{6,4},{7,5},{8,10},{9,11},{10,... | collective-permute-start | bytes 393224 | tf_op jit(solution)/shard_map/ppermute | solution.py:23
  48.7 0.2 collective-permute-start.13
  48.9 3.8 %collective-permute-done.12.refs_2_ = bf16[512,128]{1,0:T(8,128)(2,1)S(1)} collective-permute-done((bf16[512,128]{1,0:T(8,128)(2,1)S(1)}, bf16[512,128]{1,0:T(8,128)(2,1)S(1)}, u32[]{:S(2)}, u32[]{:S(2)}) %collective-permute-start.12) | collective-permute-done | bytes 131104 | tf_op jit(solution)/shard_map/ppermute | solution.py:23
  52.8 6.7 %collective-permute-done.13.refs_3_ = bf16[512,128]{1,0:T(8,128)(2,1)S(1)} collective-permute-done((bf16[512,128]{1,0:T(8,128)(2,1)S(1)}, bf16[512,128]{1,0:T(8,128)(2,1)S(1)}, u32[]{:S(2)}, u32[]{:S(2)}) %collective-permute-start.13) | collective-permute-done | bytes 131104 | tf_op jit(solution)/shard_map/ppermute | solution.py:23
  59.5 2.0 %layer.1 = (bf16[512,512]{1,0:T(8,128)(2,1)}, bf16[512,512]{1,0:T(8,128)(2,1)S(1)}, bf16[512,128]{1,0:T(8,128)(2,1)S(1)}, bf16[512,128]{1,0:T(8,128)(2,1)S(1)}, ...) custom-call(bf16[512,128]{1,0:T(8,128)(2,1)S(1)} %get-tuple-element.48.refs_0_, ...), custom_call_target="tpu_custom_call" | custom-call | flops 536870912 | bytes 2646016 | tf_op jit(solution)/shard_map/layer/pallas_call | solution.py:375
  61.5 0.1 collective-permute-start.14
  61.6 3.1 %collective-permute-start.15 = (bf16[512,128]{1,0:T(8,128)(2,1)S(1)}, bf16[512,128]{1,0:T(8,128)(2,1)S(1)}, u32[]{:S(2)}, u32[]{:S(2)}) collective-permute-start(bf16[512,128]{1,0:T(8,128)(2,1)S(1)} %get-tuple-element.57), channel_id=1, source_target_pairs={{0,2},{1,3},{2,0},{3,1},{4,6},{5,7},{6,4},{7,5},{8,10},{9,11},{10,... | collective-permute-start | bytes 393224 | tf_op jit(solution)/shard_map/ppermute | solution.py:23
  64.7 0.6 weight_term.1
  65.2 0.2 collective-permute-done.14.refs_4_.refs_3_
  65.4 7.0 %collective-permute-done.15.refs_5_.refs_4_ = bf16[512,128]{1,0:T(8,128)(2,1)S(1)} collective-permute-done((bf16[512,128]{1,0:T(8,128)(2,1)S(1)}, bf16[512,128]{1,0:T(8,128)(2,1)S(1)}, u32[]{:S(2)}, u32[]{:S(2)}) %collective-permute-start.15) | collective-permute-done | bytes 131104 | tf_op jit(solution)/shard_map/ppermute | solution.py:23
  72.4 3.0 %collective-permute-done.16.refs_6_.refs_5_ = bf16[512,128]{1,0:T(8,128)(2,1)S(1)} collective-permute-done((bf16[512,128]{1,0:T(8,128)(2,1)S(1)}, bf16[512,128]{1,0:T(8,128)(2,1)S(1)}, u32[]{:S(2)}, u32[]{:S(2)}) %collective-permute-start.16) | collective-permute-done | bytes 131104 | tf_op jit(solution)/shard_map/ppermute | solution.py:23
  75.3 2.9 %backward.2 = (bf16[5120,128]{1,0:T(8,128)(2,1)S(1)}, bf16[5120,128]{1,0:T(8,128)(2,1)S(1)}) custom-call(bf16[2064,128]{1,0:T(8,128)(2,1)S(1)} %collective-permute-done.2.refs_10_.refs_0_, bf16[2064,128]{1,0:T(8,128)(2,1)S(1)} %collective-permute-done.1.refs_0_.refs_1_, bf16[2064,128]{1,0:T(8,128)(2,1)S(1)} %collective-permute-done.3.refs_1_.refs_2_, ...), custom_call_target="tpu_custom_call" | custom-call | flops 134217728 | bytes 5255168 | tf_op jit(solution)/shard_map/backward/pallas_call | solution.py:375
  78.3 2.3 %collective-permute-start.17 = (bf16[5120,128]{1,0:T(8,128)(2,1)S(1)}, bf16[5120,128]{1,0:T(8,128)(2,1)S(1)}, u32[]{:S(2)}, u32[]{:S(2)}) collective-permute-start(bf16[5120,128]{1,0:T(8,128)(2,1)S(1)} %get-tuple-element.63), channel_id=1, source_target_pairs={{0,4},{4,0},{8,12},{12,8},{16,20},{20,16},{24,28},{28,24},{1,5},{5... | collective-permute-start | bytes 3932168 | tf_op jit(solution)/shard_map/ppermute | solution.py:23
  80.5 2.9 %backward.3 = (bf16[4096,128]{1,0:T(8,128)(2,1)S(1)}, bf16[4096,128]{1,0:T(8,128)(2,1)S(1)}) custom-call(bf16[2064,128]{1,0:T(8,128)(2,1)S(1)} %copy-done.1, bf16[2064,128]{1,0:T(8,128)(2,1)S(1)} %collective-permute-done.refs_9_.refs_1_, bf16[512,128]{1,0:T(8,128)(2,1)S(1)} %get-tuple-element.55.refs_3_.refs_2_, ...), custom_call_target="tpu_custom_call" | custom-call | flops 134217728 | bytes 3678208 | tf_op jit(solution)/shard_map/backward/pallas_call | solution.py:375
  83.4 0.3 collective-permute-start.21
  83.8 0.3 pair_sum.2
  84.1 0.8 collective-permute-start.18
  84.9 1.0 collective-permute-start.19
  85.9 0.9 collective-permute-start.20
  86.8 0.2 pair_sum.3
  87.0 0.8 collective-permute-start.25
  87.9 1.0 collective-permute-start.26
  88.9 4.3 %collective-permute-done.18.refs_1_ = bf16[1280,128]{1,0:T(8,128)(2,1)S(1)} collective-permute-done((bf16[1280,128]{1,0:T(8,128)(2,1)S(1)}, bf16[1280,128]{1,0:T(8,128)(2,1)S(1)}, u32[]{:S(2)}, u32[]{:S(2)}) %collective-permute-start.18) | collective-permute-done | bytes 327712 | tf_op jit(solution)/shard_map/ppermute | solution.py:23
  93.2 1.3 collective-permute-start.27
  94.5 7.0 %collective-permute-done.20.refs_3_ = bf16[1280,128]{1,0:T(8,128)(2,1)S(1)} collective-permute-done((bf16[1280,128]{1,0:T(8,128)(2,1)S(1)}, bf16[1280,128]{1,0:T(8,128)(2,1)S(1)}, u32[]{:S(2)}, u32[]{:S(2)}) %collective-permute-start.20) | collective-permute-done | bytes 327712 | tf_op jit(solution)/shard_map/ppermute | solution.py:23
  101.5 0.2 plane_sum.2
  101.6 0.3 collective-permute-start.23
  101.9 1.1 collective-permute-start.24
  103.0 2.8 %collective-permute-done.25.refs_1_ = bf16[1024,128]{1,0:T(8,128)(2,1)S(1)} collective-permute-done((bf16[1024,128]{1,0:T(8,128)(2,1)S(1)}, bf16[1024,128]{1,0:T(8,128)(2,1)S(1)}, u32[]{:S(2)}, u32[]{:S(2)}) %collective-permute-start.25) | collective-permute-done | bytes 262176 | tf_op jit(solution)/shard_map/ppermute | solution.py:23
  105.9 0.2 collective-permute-done.26.refs_2_
  106.0 6.7 %collective-permute-done.27.refs_3_ = bf16[1024,128]{1,0:T(8,128)(2,1)S(1)} collective-permute-done((bf16[1024,128]{1,0:T(8,128)(2,1)S(1)}, bf16[1024,128]{1,0:T(8,128)(2,1)S(1)}, u32[]{:S(2)}, u32[]{:S(2)}) %collective-permute-start.27) | collective-permute-done | bytes 262176 | tf_op jit(solution)/shard_map/ppermute | solution.py:23
  112.7 0.1 plane_sum.3
  112.9 0.2 collective-permute-done.22.refs_1_
  113.1 6.7 %collective-permute-done.24.refs_3_ = bf16[768,128]{1,0:T(8,128)(2,1)S(1)} collective-permute-done((bf16[768,128]{1,0:T(8,128)(2,1)S(1)}, bf16[768,128]{1,0:T(8,128)(2,1)S(1)}, u32[]{:S(2)}, u32[]{:S(2)}) %collective-permute-start.24) | collective-permute-done | bytes 196640 | tf_op jit(solution)/shard_map/ppermute | solution.py:23
  119.8 0.6 collective-permute-start.28
  120.4 0.2 collective-permute-start.29
  120.7 1.9 %collective-permute-start.30 = (bf16[256,128]{1,0:T(8,128)(2,1)S(1)}, bf16[256,128]{1,0:T(8,128)(2,1)S(1)}, u32[]{:S(2)}, u32[]{:S(2)}) collective-permute-start(bf16[256,128]{1,0:T(8,128)(2,1)S(1)} %weight_total.1.refs_0_), channel_id=1, source_target_pairs={{0,24},{4,28},{8,16},{12,20},{16,8},{20,12},{24,0},{28,4},{1,25},{... | collective-permute-start | bytes 196616 | tf_op jit(solution)/shard_map/ppermute | solution.py:23
  122.5 0.5 collective-permute-done.28.refs_1_
  123.0 0.5 collective-permute-done.29.refs_2_
  123.6 1.8 %collective-permute-done.30.refs_3_ = bf16[256,128]{1,0:T(8,128)(2,1)S(1)} collective-permute-done((bf16[256,128]{1,0:T(8,128)(2,1)S(1)}, bf16[256,128]{1,0:T(8,128)(2,1)S(1)}, u32[]{:S(2)}, u32[]{:S(2)}) %collective-permute-start.30) | collective-permute-done | bytes 65568 | tf_op jit(solution)/shard_map/ppermute | solution.py:23
  125.4 2.6 %collective-permute-start.32 = (bf16[256,512]{1,0:T(8,128)(2,1)S(1)}, bf16[256,512]{1,0:T(8,128)(2,1)S(1)}, u32[]{:S(2)}, u32[]{:S(2)}) collective-permute-start(bf16[256,512]{1,0:T(8,128)(2,1)S(1)} %weight_half.1.refs_0_), channel_id=1, source_target_pairs={{0,4},{4,0},{8,12},{12,8},{16,20},{20,16},{24,28},{28,24},{1,5},{5... | collective-permute-start | bytes 786440 | tf_op jit(solution)/shard_map/ppermute | solution.py:23
  128.1 0.9 join.1
  129.0 0.2 collective-permute-done.32.refs_1_
  129.2 1.1 weight_whole.1
  (33 shorter events, 0.2 us)
Async XLA Ops:
  1.3 36.8 %copy-start.2 = (bf16[512,512]{1,0:T(8,128)(2,1)S(1)}, bf16[512,512]{1,0:T(8,128)(2,1)}, u32[]{:S(2)}) copy-start(bf16[512,512]{1,0:T(8,128)(2,1)} %refs_11_.1) | copy-start | bytes 1572868
  1.3 36.8 %copy-start.4 = (bf16[8,512]{1,0:T(8,128)(2,1)S(1)}, bf16[8,512]{1,0:T(8,128)(2,1)}, u32[]{:S(2)}) copy-start(bf16[8,512]{1,0:T(8,128)(2,1)} %refs_12_.1) | copy-start | bytes 24580
  3.6 3.2 %collective-permute-start.4 = (bf16[2048,128]{1,0:T(8,128)(2,1)}, bf16[2048,128]{1,0:T(8,128)(2,1)S(1)}, u32[]{:S(2)}, u32[]{:S(2)}) collective-permute-start(bf16[2048,128]{1,0:T(8,128)(2,1)} %get-tuple-element.44.refs_0_), channel_id=1, source_target_pairs={{0,4},{4,0},{8,12},{12,8},{16,20},{20,16},{24,28},{28,24},{1,5},{5... | collective-permute-start | bytes 1572872 | tf_op jit(solution)/shard_map/ppermute | solution.py:23
  4.3 23.1 %collective-permute-start = (bf16[2064,128]{1,0:T(8,128)(2,1)}, bf16[2064,128]{1,0:T(8,128)(2,1)S(1)}, u32[]{:S(2)}, u32[]{:S(2)}) collective-permute-start(bf16[2064,128]{1,0:T(8,128)(2,1)} %get-tuple-element.42.refs_8_.refs_0_), channel_id=1, source_target_pairs={{0,1},{1,0},{2,3},{3,2},{4,5},{5,4},{6,7},{7,6},{8,9},{9,8},{10,11... | collective-permute-start | bytes 1585160 | tf_op jit(solution)/shard_map/ppermute | solution.py:23
  4.3 26.3 %collective-permute-start.2 = (bf16[2064,128]{1,0:T(8,128)(2,1)}, bf16[2064,128]{1,0:T(8,128)(2,1)S(1)}, u32[]{:S(2)}, u32[]{:S(2)}) collective-permute-start(bf16[2064,128]{1,0:T(8,128)(2,1)} %get-tuple-element.42.refs_8_.refs_0_), channel_id=1, source_target_pairs={{0,2},{1,3},{2,0},{3,1},{4,6},{5,7},{6,4},{7,5},{8,10},{9,11},{10,... | collective-permute-start | bytes 1585160 | tf_op jit(solution)/shard_map/ppermute | solution.py:23
  6.8 25.3 %collective-permute-start.7 = (bf16[2048,128]{1,0:T(8,128)(2,1)}, bf16[2048,128]{1,0:T(8,128)(2,1)S(1)}, u32[]{:S(2)}, u32[]{:S(2)}) collective-permute-start(bf16[2048,128]{1,0:T(8,128)(2,1)} %get-tuple-element.44.refs_0_), channel_id=1, source_target_pairs={{0,24},{4,28},{8,16},{12,20},{16,8},{20,12},{24,0},{28,4},{1,25},{... | collective-permute-start | bytes 1572872 | tf_op jit(solution)/shard_map/ppermute | solution.py:23
  9.0 26.0 %collective-permute-start.5 = (bf16[2048,128]{1,0:T(8,128)(2,1)}, bf16[2048,128]{1,0:T(8,128)(2,1)S(1)}, u32[]{:S(2)}, u32[]{:S(2)}) collective-permute-start(bf16[2048,128]{1,0:T(8,128)(2,1)} %get-tuple-element.44.refs_0_), channel_id=1, source_target_pairs={{0,8},{4,12},{8,0},{12,4},{16,24},{20,28},{24,16},{28,20},{1,9},{5... | collective-permute-start | bytes 1572872 | tf_op jit(solution)/shard_map/ppermute | solution.py:23
  9.3 25.9 %collective-permute-start.6 = (bf16[2048,128]{1,0:T(8,128)(2,1)}, bf16[2048,128]{1,0:T(8,128)(2,1)S(1)}, u32[]{:S(2)}, u32[]{:S(2)}) collective-permute-start(bf16[2048,128]{1,0:T(8,128)(2,1)} %get-tuple-element.44.refs_0_), channel_id=1, source_target_pairs={{0,16},{4,20},{8,24},{12,28},{16,0},{20,4},{24,8},{28,12},{1,17},{... | collective-permute-start | bytes 1572872 | tf_op jit(solution)/shard_map/ppermute | solution.py:23
  27.4 15.4 %collective-permute-start.1 = (bf16[2064,128]{1,0:T(8,128)(2,1)}, bf16[2064,128]{1,0:T(8,128)(2,1)S(1)}, u32[]{:S(2)}, u32[]{:S(2)}) collective-permute-start(bf16[2064,128]{1,0:T(8,128)(2,1)} %get-tuple-element.42.refs_8_.refs_0_), channel_id=1, source_target_pairs={{1,2},{2,1},{5,6},{6,5},{9,10},{10,9},{13,14},{14,13},{17,18},{18,... | collective-permute-start | bytes 1585160 | tf_op jit(solution)/shard_map/ppermute | solution.py:395
  30.6 12.2 %collective-permute-start.3 = (bf16[2064,128]{1,0:T(8,128)(2,1)S(1)}, bf16[2064,128]{1,0:T(8,128)(2,1)S(1)}, u32[]{:S(2)}, u32[]{:S(2)}) collective-permute-start(bf16[2064,128]{1,0:T(8,128)(2,1)S(1)} %collective-permute-done.2.refs_10_.refs_0_), channel_id=1, source_target_pairs={{2,3},{1,0},{6,7},{5,4},{10,11},{9,8},{14,15},{13,12},{18,19},{17,... | collective-permute-start | bytes 1585160 | tf_op jit(solution)/shard_map/ppermute | solution.py:393
  32.2 4.4 %collective-permute-start.10 = (bf16[2048,128]{1,0:T(8,128)(2,1)S(1)}, bf16[2048,128]{1,0:T(8,128)(2,1)S(1)}, u32[]{:S(2)}, u32[]{:S(2)}) collective-permute-start(bf16[2048,128]{1,0:T(8,128)(2,1)S(1)} %collective-permute-done.7.refs_3_), channel_id=1, source_target_pairs={{0,4},{4,0},{8,12},{12,8},{16,20},{20,16},{24,28},{28,24},{1,5},{5... | collective-permute-start | bytes 1572872 | tf_op jit(solution)/shard_map/ppermute | solution.py:23
  35.0 2.3 %collective-permute-start.8 = (bf16[2048,128]{1,0:T(8,128)(2,1)S(1)}, bf16[2048,128]{1,0:T(8,128)(2,1)S(1)}, u32[]{:S(2)}, u32[]{:S(2)}) collective-permute-start(bf16[2048,128]{1,0:T(8,128)(2,1)S(1)} %collective-permute-done.5.refs_1_), channel_id=1, source_target_pairs={{0,4},{4,0},{8,12},{12,8},{16,20},{20,16},{24,28},{28,24},{1,5},{5... | collective-permute-start | bytes 1572872 | tf_op jit(solution)/shard_map/ppermute | solution.py:23
  35.1 2.9 %collective-permute-start.9 = (bf16[2048,128]{1,0:T(8,128)(2,1)S(1)}, bf16[2048,128]{1,0:T(8,128)(2,1)S(1)}, u32[]{:S(2)}, u32[]{:S(2)}) collective-permute-start(bf16[2048,128]{1,0:T(8,128)(2,1)S(1)} %collective-permute-done.6.refs_2_), channel_id=1, source_target_pairs={{0,4},{4,0},{8,12},{12,8},{16,20},{20,16},{24,28},{28,24},{1,5},{5... | collective-permute-start | bytes 1572872 | tf_op jit(solution)/shard_map/ppermute | solution.py:23
  38.1 1.0 copy-start
  39.1 1.0 copy-start.3
  42.8 6.1 %copy-start.5 = (s32[2048]{0:T(1024)S(1)}, s32[2048]{0:T(1024)}, u32[]{:S(2)}) copy-start(s32[2048]{0:T(1024)} %param.12) | copy-start | bytes 24580
  42.9 6.1 %copy-start.6 = (s32[2048]{0:T(1024)S(1)}, s32[2048]{0:T(1024)}, u32[]{:S(2)}) copy-start(s32[2048]{0:T(1024)} %param.13) | copy-start | bytes 24580
  44.6 4.3 %collective-permute-start.11 = (bf16[512,128]{1,0:T(8,128)(2,1)}, bf16[512,128]{1,0:T(8,128)(2,1)S(1)}, u32[]{:S(2)}, u32[]{:S(2)}) collective-permute-start(bf16[512,128]{1,0:T(8,128)(2,1)} %get-tuple-element.49), channel_id=1, source_target_pairs={{0,1},{1,0},{2,3},{3,2},{4,5},{5,4},{6,7},{7,6},{8,9},{9,8},{10,11... | collective-permute-start | bytes 393224 | tf_op jit(solution)/shard_map/ppermute | solution.py:23
  44.9 7.8 %collective-permute-start.12 = (bf16[512,128]{1,0:T(8,128)(2,1)S(1)}, bf16[512,128]{1,0:T(8,128)(2,1)S(1)}, u32[]{:S(2)}, u32[]{:S(2)}) collective-permute-start(bf16[512,128]{1,0:T(8,128)(2,1)S(1)} %get-tuple-element.50), channel_id=1, source_target_pairs={{0,2},{1,3},{2,0},{3,1},{4,6},{5,7},{6,4},{7,5},{8,10},{9,11},{10,... | collective-permute-start | bytes 393224 | tf_op jit(solution)/shard_map/ppermute | solution.py:23
  48.7 10.8 %collective-permute-start.13 = (bf16[512,128]{1,0:T(8,128)(2,1)S(1)}, bf16[512,128]{1,0:T(8,128)(2,1)S(1)}, u32[]{:S(2)}, u32[]{:S(2)}) collective-permute-start(bf16[512,128]{1,0:T(8,128)(2,1)S(1)} %get-tuple-element.51), channel_id=1, source_target_pairs={{0,3},{1,2},{2,1},{3,0},{4,7},{5,6},{6,5},{7,4},{8,11},{9,10},{10,... | collective-permute-start | bytes 393224 | tf_op jit(solution)/shard_map/ppermute | solution.py:23
  61.5 3.9 %collective-permute-start.14 = (bf16[512,128]{1,0:T(8,128)(2,1)S(1)}, bf16[512,128]{1,0:T(8,128)(2,1)S(1)}, u32[]{:S(2)}, u32[]{:S(2)}) collective-permute-start(bf16[512,128]{1,0:T(8,128)(2,1)S(1)} %get-tuple-element.56), channel_id=1, source_target_pairs={{0,1},{1,0},{2,3},{3,2},{4,5},{5,4},{6,7},{7,6},{8,9},{9,8},{10,11... | collective-permute-start | bytes 393224 | tf_op jit(solution)/shard_map/ppermute | solution.py:23
  61.6 10.8 %collective-permute-start.15 = (bf16[512,128]{1,0:T(8,128)(2,1)S(1)}, bf16[512,128]{1,0:T(8,128)(2,1)S(1)}, u32[]{:S(2)}, u32[]{:S(2)}) collective-permute-start(bf16[512,128]{1,0:T(8,128)(2,1)S(1)} %get-tuple-element.57), channel_id=1, source_target_pairs={{0,2},{1,3},{2,0},{3,1},{4,6},{5,7},{6,4},{7,5},{8,10},{9,11},{10,... | collective-permute-start | bytes 393224 | tf_op jit(solution)/shard_map/ppermute | solution.py:23
  64.7 10.7 %collective-permute-start.16 = (bf16[512,128]{1,0:T(8,128)(2,1)S(1)}, bf16[512,128]{1,0:T(8,128)(2,1)S(1)}, u32[]{:S(2)}, u32[]{:S(2)}) collective-permute-start(bf16[512,128]{1,0:T(8,128)(2,1)S(1)} %get-tuple-element.58), channel_id=1, source_target_pairs={{0,3},{1,2},{2,1},{3,0},{4,7},{5,6},{6,5},{7,4},{8,11},{9,10},{10,... | collective-permute-start | bytes 393224 | tf_op jit(solution)/shard_map/ppermute | solution.py:23
  75.3 5.2 %copy-start.1 = (bf16[2064,128]{1,0:T(8,128)(2,1)S(1)}, bf16[2064,128]{1,0:T(8,128)(2,1)}, u32[]{:S(2)}) copy-start(bf16[2064,128]{1,0:T(8,128)(2,1)} %get-tuple-element.42.refs_8_.refs_0_) | copy-start | bytes 1585156
  78.3 5.5 %collective-permute-start.17 = (bf16[5120,128]{1,0:T(8,128)(2,1)S(1)}, bf16[5120,128]{1,0:T(8,128)(2,1)S(1)}, u32[]{:S(2)}, u32[]{:S(2)}) collective-permute-start(bf16[5120,128]{1,0:T(8,128)(2,1)S(1)} %get-tuple-element.63), channel_id=1, source_target_pairs={{0,4},{4,0},{8,12},{12,8},{16,20},{20,16},{24,28},{28,24},{1,5},{5... | collective-permute-start | bytes 3932168 | tf_op jit(solution)/shard_map/ppermute | solution.py:23
  83.4 3.4 %collective-permute-start.21 = (bf16[4096,128]{1,0:T(8,128)(2,1)S(1)}, bf16[4096,128]{1,0:T(8,128)(2,1)S(1)}, u32[]{:S(2)}, u32[]{:S(2)}) collective-permute-start(bf16[4096,128]{1,0:T(8,128)(2,1)S(1)} %get-tuple-element.69), channel_id=1, source_target_pairs={{0,4},{4,0},{8,12},{12,8},{16,20},{20,16},{24,28},{28,24},{1,5},{5... | collective-permute-start | bytes 3145736 | tf_op jit(solution)/shard_map/ppermute | solution.py:23
  84.1 9.1 %collective-permute-start.18 = (bf16[1280,128]{1,0:T(8,128)(2,1)S(1)}, bf16[1280,128]{1,0:T(8,128)(2,1)S(1)}, u32[]{:S(2)}, u32[]{:S(2)}) collective-permute-start(bf16[1280,128]{1,0:T(8,128)(2,1)S(1)} %get-tuple-element.66), channel_id=1, source_target_pairs={{0,8},{4,12},{8,0},{12,4},{16,24},{20,28},{24,16},{28,20},{1,9},{5... | collective-permute-start | bytes 983048 | tf_op jit(solution)/shard_map/ppermute | solution.py:23
  84.9 9.5 %collective-permute-start.19 = (bf16[1280,128]{1,0:T(8,128)(2,1)S(1)}, bf16[1280,128]{1,0:T(8,128)(2,1)S(1)}, u32[]{:S(2)}, u32[]{:S(2)}) collective-permute-start(bf16[1280,128]{1,0:T(8,128)(2,1)S(1)} %get-tuple-element.67), channel_id=1, source_target_pairs={{0,16},{4,20},{8,24},{12,28},{16,0},{20,4},{24,8},{28,12},{1,17},{... | collective-permute-start | bytes 983048 | tf_op jit(solution)/shard_map/ppermute | solution.py:23
  85.9 15.5 %collective-permute-start.20 = (bf16[1280,128]{1,0:T(8,128)(2,1)S(1)}, bf16[1280,128]{1,0:T(8,128)(2,1)S(1)}, u32[]{:S(2)}, u32[]{:S(2)}) collective-permute-start(bf16[1280,128]{1,0:T(8,128)(2,1)S(1)} %get-tuple-element.68), channel_id=1, source_target_pairs={{0,24},{4,28},{8,16},{12,20},{16,8},{20,12},{24,0},{28,4},{1,25},{... | collective-permute-start | bytes 983048 | tf_op jit(solution)/shard_map/ppermute | solution.py:23
  87.0 18.9 %collective-permute-start.25 = (bf16[1024,128]{1,0:T(8,128)(2,1)S(1)}, bf16[1024,128]{1,0:T(8,128)(2,1)S(1)}, u32[]{:S(2)}, u32[]{:S(2)}) collective-permute-start(bf16[1024,128]{1,0:T(8,128)(2,1)S(1)} %get-tuple-element.74), channel_id=1, source_target_pairs={{0,8},{4,12},{8,0},{12,4},{16,24},{20,28},{24,16},{28,20},{1,9},{5... | collective-permute-start | bytes 786440 | tf_op jit(solution)/shard_map/ppermute | solution.py:23
  87.9 18.2 %collective-permute-start.26 = (bf16[1024,128]{1,0:T(8,128)(2,1)S(1)}, bf16[1024,128]{1,0:T(8,128)(2,1)S(1)}, u32[]{:S(2)}, u32[]{:S(2)}) collective-permute-start(bf16[1024,128]{1,0:T(8,128)(2,1)S(1)} %get-tuple-element.75), channel_id=1, source_target_pairs={{0,16},{4,20},{8,24},{12,28},{16,0},{20,4},{24,8},{28,12},{1,17},{... | collective-permute-start | bytes 786440 | tf_op jit(solution)/shard_map/ppermute | solution.py:23
  93.2 19.5 %collective-permute-start.27 = (bf16[1024,128]{1,0:T(8,128)(2,1)S(1)}, bf16[1024,128]{1,0:T(8,128)(2,1)S(1)}, u32[]{:S(2)}, u32[]{:S(2)}) collective-permute-start(bf16[1024,128]{1,0:T(8,128)(2,1)S(1)} %get-tuple-element.76), channel_id=1, source_target_pairs={{0,24},{4,28},{8,16},{12,20},{16,8},{20,12},{24,0},{28,4},{1,25},{... | collective-permute-start | bytes 786440 | tf_op jit(solution)/shard_map/ppermute | solution.py:23
  101.6 11.5 %collective-permute-start.23 = (bf16[768,128]{1,0:T(8,128)(2,1)S(1)}, bf16[768,128]{1,0:T(8,128)(2,1)S(1)}, u32[]{:S(2)}, u32[]{:S(2)}) collective-permute-start(bf16[768,128]{1,0:T(8,128)(2,1)S(1)} %get-tuple-element.72), channel_id=1, source_target_pairs={{0,2},{1,3},{2,0},{3,1},{4,6},{5,7},{6,4},{7,5},{8,10},{9,11},{10,... | collective-permute-start | bytes 589832 | tf_op jit(solution)/shard_map/ppermute | solution.py:23
  101.9 17.9 %collective-permute-start.24 = (bf16[768,128]{1,0:T(8,128)(2,1)S(1)}, bf16[768,128]{1,0:T(8,128)(2,1)S(1)}, u32[]{:S(2)}, u32[]{:S(2)}) collective-permute-start(bf16[768,128]{1,0:T(8,128)(2,1)S(1)} %get-tuple-element.73), channel_id=1, source_target_pairs={{0,3},{1,2},{2,1},{3,0},{4,7},{5,6},{6,5},{7,4},{8,11},{9,10},{10,... | collective-permute-start | bytes 589832 | tf_op jit(solution)/shard_map/ppermute | solution.py:23
  105.9 7.3 %collective-permute-start.22 = (bf16[256,128]{1,0:T(8,128)(2,1)S(1)}, bf16[256,128]{1,0:T(8,128)(2,1)S(1)}, u32[]{:S(2)}, u32[]{:S(2)}) collective-permute-start(bf16[256,128]{1,0:T(8,128)(2,1)S(1)} %get-tuple-element.71.refs_0_), channel_id=1, source_target_pairs={{0,1},{1,0},{2,3},{3,2},{4,5},{5,4},{6,7},{7,6},{8,9},{9,8},{10,11... | collective-permute-start | bytes 196616 | tf_op jit(solution)/shard_map/ppermute | solution.py:23
  112.8 9.7 %collective-permute-start.31 = (bf16[512,128]{1,0:T(8,128)(2,1)S(1)}, bf16[512,128]{1,0:T(8,128)(2,1)S(1)}, u32[]{:S(2)}, u32[]{:S(2)}) collective-permute-start(bf16[512,128]{1,0:T(8,128)(2,1)S(1)} %get-tuple-element.78), channel_id=1, source_target_pairs={{0,1},{1,0},{2,3},{3,2},{4,5},{5,4},{6,7},{7,6},{8,9},{9,8},{10,11... | collective-permute-start | bytes 393224 | tf_op jit(solution)/shard_map/ppermute | solution.py:23
  119.8 3.2 %collective-permute-start.28 = (bf16[256,128]{1,0:T(8,128)(2,1)S(1)}, bf16[256,128]{1,0:T(8,128)(2,1)S(1)}, u32[]{:S(2)}, u32[]{:S(2)}) collective-permute-start(bf16[256,128]{1,0:T(8,128)(2,1)S(1)} %weight_total.1.refs_0_), channel_id=1, source_target_pairs={{0,8},{4,12},{8,0},{12,4},{16,24},{20,28},{24,16},{28,20},{1,9},{5... | collective-permute-start | bytes 196616 | tf_op jit(solution)/shard_map/ppermute | solution.py:23
  120.4 3.1 %collective-permute-start.29 = (bf16[256,128]{1,0:T(8,128)(2,1)S(1)}, bf16[256,128]{1,0:T(8,128)(2,1)S(1)}, u32[]{:S(2)}, u32[]{:S(2)}) collective-permute-start(bf16[256,128]{1,0:T(8,128)(2,1)S(1)} %weight_total.1.refs_0_), channel_id=1, source_target_pairs={{0,16},{4,20},{8,24},{12,28},{16,0},{20,4},{24,8},{28,12},{1,17},{... | collective-permute-start | bytes 196616 | tf_op jit(solution)/shard_map/ppermute | solution.py:23
  120.7 4.7 %collective-permute-start.30 = (bf16[256,128]{1,0:T(8,128)(2,1)S(1)}, bf16[256,128]{1,0:T(8,128)(2,1)S(1)}, u32[]{:S(2)}, u32[]{:S(2)}) collective-permute-start(bf16[256,128]{1,0:T(8,128)(2,1)S(1)} %weight_total.1.refs_0_), channel_id=1, source_target_pairs={{0,24},{4,28},{8,16},{12,20},{16,8},{20,12},{24,0},{28,4},{1,25},{... | collective-permute-start | bytes 196616 | tf_op jit(solution)/shard_map/ppermute | solution.py:23
  125.4 3.8 %collective-permute-start.32 = (bf16[256,512]{1,0:T(8,128)(2,1)S(1)}, bf16[256,512]{1,0:T(8,128)(2,1)S(1)}, u32[]{:S(2)}, u32[]{:S(2)}) collective-permute-start(bf16[256,512]{1,0:T(8,128)(2,1)S(1)} %weight_half.1.refs_0_), channel_id=1, source_target_pairs={{0,4},{4,0},{8,12},{12,8},{16,20},{20,16},{24,28},{28,24},{1,5},{5... | collective-permute-start | bytes 786440 | tf_op jit(solution)/shard_map/ppermute | solution.py:23

commit v4 on v3

--- a/solution.py
+++ b/solution.py
@@ -261,34 +261,28 @@
     given = refs[: count + last]
     backs = refs[count + last : count + last + teams]
     refs = refs[count + last + teams :]
+    at_end = (place[0] == 0) | (place[0] == teams - 1)
+
+    def held(i, here):
+        if last and i == count - 1:
+            return jnp.where(at_end, given[i + 1][here, :], given[i][here, :])
+        return given[i][here, :]
+
     rider_refs, refs = refs[:riders], refs[riders:]
-    keep, send, lists, rows, totals, ids_vmem, ids_smem, sems, id_sem = refs
+    keep, send, rows, totals, ids_vmem, ids_smem, id_sem = refs
     team, core = place[0], place[2]
     share = backs[0].shape[0]
     per_piece = piece // BLOCK
-    plain = count - last
-    copies = []
-    for i in range(plain):
-        copies.append(pltpu.make_async_copy(given[i], lists.at[i], sems.at[i]))
-        copies[-1].start()
-    if last:
-        target = lists.at[plain]
-        copies.append(fetch_late(place, teams, *given[plain:], target, sems.at[plain]))
-    moves = []
+    for i in range(count):
+        tail = held(i, pl.ds(slots * BLOCK, ID_ROWS)).astype(jnp.float32)
+        ids_vmem[i] = tail.astype(jnp.int32)[:8]
+    copy = pltpu.make_async_copy(ids_vmem, ids_smem, id_sem)
+    copy.start()
+    totals[...] = jnp.zeros_like(totals)
     for d in range(teams):
         start = pl.multiple_of((team ^ d) * share, share)
-        target = rows.at[pl.ds(start, share), :]
-        moves.append(pltpu.make_async_copy(backs[d], target, sems.at[count + d]))
-        moves[-1].start()
-
-    def clear():
-        totals[...] = jnp.zeros_like(totals)
-
-    for copy in copies:
-        copy.wait()
-    load_ids(ids_vmem, ids_smem, lists, slots, id_sem, clear)
-    for copy in moves:
-        copy.wait()
+        rows[pl.ds(start, share), :] = backs[d][...]
+    copy.wait()
 
     def visit(i, panel, first, live):
         products = []
@@ -296,7 +290,7 @@
             slot = first + u
             start = pl.multiple_of(ids_smem[i, 0, slot] * BLOCK, BLOCK)
             source = rows[pl.ds(start, BLOCK), :]
-            block = lists[i, pl.ds(pl.multiple_of(slot * BLOCK, BLOCK), BLOCK), :]
+            block = held(i, pl.ds(pl.multiple_of(slot * BLOCK, BLOCK), BLOCK))
             product = lax.dot_general(
                 block, source, (((0,), (0,)), ((), ())), preferred_element_type=jnp.float32
             )
@@ -457,7 +451,6 @@
     mine = prepared[0]
     own = prepared[1] if aligned else lax.dynamic_slice_in_dim(features, team * part, part, 1)
     beside = swap(own, "row", 1)
-    own, beside = lax.optimization_barrier((own, beside))
     near = [own] + [swap(own, "row", 2 * d) for d in range(1, chips)]
     early, late = gather_lists(mine, teams, lambda two, one: one)
     far = [beside] + [swap(value, "row", 1) for value in near[1:]]
@@ -557,18 +550,16 @@
                 ),
                 "backward",
                 [*given, *backs, *riders],
-                [any_space] * (len(given) + teams) + [vmem] * len(riders),
+                [vmem] * (len(given) + teams + len(riders)),
                 [shaped(moved, part)] * 2,
                 [
-                    id_scratch(count)[0],
                     pltpu.VMEM((slab, part), bf16),
                     pltpu.VMEM((2 * rows, part), f32),
                     *id_scratch(count)[1:],
-                    pltpu.SemaphoreType.DMA((count + teams,)),
                     pltpu.SemaphoreType.DMA,
                 ],
                 count * list_flops,
-                rows * padded * 14 + count * list_bytes + slab * padded * 2 + 4 * MIB,
+                rows * padded * 14 + (count + 1) * list_bytes + slab * padded * 4 + 4 * MIB,
                 after=[value[0] for value in held],
             )
         )

time: 131 us -> 129 us (0.985)
  Pallas kernels: 18 us -> 14.7 us
  waiting for transfers between devices: 72.1 us -> 73.7 us
    pallas_call x15, Pallas kernels: 18 us -> 14.7 us  [call(): pl.pallas_call(body, name=name, in_specs=specs, out_specs=[pl.BlockSpec(m...]
    ppermute x1, waiting for transfers between devices: 0.01 us -> 1.64 us  [gather_lists(): middle = lax.ppermute(held, 'team', [(1, 2), (2, 1)])]
  transfers between devices with their start and end apart: 33 -> 33, of which waited for: 20 -> 22; matrix products, arithmetic and copies ran while one was open for 0% -> 0% of each run, Pallas kernels for 6% -> 5%
where the time goes in v4:
time: 129 us
  waiting for transfers between devices  73.7 us (57%)
  starting transfers between devices  36.4 us (28%)
  Pallas kernels  14.7 us (11%)
  local copies, waits for them, and re-layouts  2.12 us (2%)
  between operations  1.48 us (1%)
    ppermute x31, waiting for transfers between devices, swap(): return lax.ppermute(value, axis, [(i, i ^ flip) for i in range(size)])  72.1 us
    ppermute x31, starting transfers between devices, swap(): return lax.ppermute(value, axis, [(i, i ^ flip) for i in range(size)])  31.7 us
    pallas_call x15, Pallas kernels, call(): pl.pallas_call(body, name=name, in_specs=specs, out_specs=[pl.BlockSpec(m...  14.7 us
    ppermute x1, starting transfers between devices, gather_lists(): middle = lax.ppermute(held, 'team', [(1, 2), (2, 1)])  3.38 us
  transfers between devices with their start and end apart: 33, of which 22 were waited for; matrix products, arithmetic and copies ran while one was open for 0% of the time, Pallas kernels for 5%

profile of v4, /device:TPU:9, one launch (start us, length us, event | category | flops | bytes accessed | tf_op | source)
XLA Modules:
  0.0 128.5 jit_solution(18098218635976747343)
XLA Ops:
  1.3 2.3 %prepare.1 = (bf16[2064,128]{1,0:T(8,128)(2,1)}, bf16[2048,128]{1,0:T(8,128)(2,1)}) custom-call(bf16[2048,128]{1,0:T(8,128)(2,1)} %bitcast.5, s32[1,16]{1,0:T(1,128)} %bitcast.6, s32[1,16]{1,0:T(1,128)} %bitcast.7, s32[1,1]{1,0:T(1,128)S(6)} %copy.12.refs_3_, bf16[2048,512]{1,0:T(8,128)(2,1)} %refs_4_.1), custom_call_target="tpu_custom_call" | custom-call | tf_op jit(solution)/shard_map/prepare/pallas_call | solution.py:369
  3.7 2.5 %collective-permute-start.2 = (bf16[2064,128]{1,0:T(8,128)(2,1)}, bf16[2064,128]{1,0:T(8,128)(2,1)S(1)}, u32[]{:S(2)}, u32[]{:S(2)}) collective-permute-start(bf16[2064,128]{1,0:T(8,128)(2,1)} %get-tuple-element.40.refs_8_.refs_0_), channel_id=1, source_target_pairs={{0,2},{1,3},{2,0},{3,1},{4,6},{5,7},{6,4},{7,5},{8,10},{9,11},{10,... | collective-permute-start | bytes 1585160 | tf_op jit(solution)/shard_map/ppermute | solution.py:23
  6.1 2.2 %collective-permute-start.6 = (bf16[2048,128]{1,0:T(8,128)(2,1)}, bf16[2048,128]{1,0:T(8,128)(2,1)S(1)}, u32[]{:S(2)}, u32[]{:S(2)}) collective-permute-start(bf16[2048,128]{1,0:T(8,128)(2,1)} %get-tuple-element.41.refs_0_), channel_id=1, source_target_pairs={{0,24},{4,28},{8,16},{12,20},{16,8},{20,12},{24,0},{28,4},{1,25},{... | collective-permute-start | bytes 1572872 | tf_op jit(solution)/shard_map/ppermute | solution.py:23
  8.3 0.3 collective-permute-start.4
  8.6 0.2 collective-permute-start.5
  8.8 17.4 %collective-permute-done.refs_9_.refs_1_ = bf16[2064,128]{1,0:T(8,128)(2,1)S(1)} collective-permute-done((bf16[2064,128]{1,0:T(8,128)(2,1)}, bf16[2064,128]{1,0:T(8,128)(2,1)S(1)}, u32[]{:S(2)}, u32[]{:S(2)}) %collective-permute-start) | collective-permute-done | bytes 528416 | tf_op jit(solution)/shard_map/ppermute | solution.py:23
  26.2 1.2 collective-permute-start.7
  27.4 3.4 %collective-permute-start.1 = (bf16[2064,128]{1,0:T(8,128)(2,1)}, bf16[2064,128]{1,0:T(8,128)(2,1)S(1)}, u32[]{:S(2)}, u32[]{:S(2)}) collective-permute-start(bf16[2064,128]{1,0:T(8,128)(2,1)} %get-tuple-element.40.refs_8_.refs_0_), channel_id=1, source_target_pairs={{1,2},{2,1},{5,6},{6,5},{9,10},{10,9},{13,14},{14,13},{17,18},{18,... | collective-permute-start | bytes 1585160 | tf_op jit(solution)/shard_map/ppermute | solution.py:389
  30.8 1.3 %collective-permute-start.3 = (bf16[2064,128]{1,0:T(8,128)(2,1)S(1)}, bf16[2064,128]{1,0:T(8,128)(2,1)S(1)}, u32[]{:S(2)}, u32[]{:S(2)}) collective-permute-start(bf16[2064,128]{1,0:T(8,128)(2,1)S(1)} %collective-permute-done.2.refs_10_.refs_0_), channel_id=1, source_target_pairs={{2,3},{1,0},{6,7},{5,4},{10,11},{9,8},{14,15},{13,12},{18,19},{17,... | collective-permute-start | bytes 1585160 | tf_op jit(solution)/shard_map/ppermute | solution.py:387
  32.2 2.2 %collective-permute-start.10 = (bf16[2048,128]{1,0:T(8,128)(2,1)S(1)}, bf16[2048,128]{1,0:T(8,128)(2,1)S(1)}, u32[]{:S(2)}, u32[]{:S(2)}) collective-permute-start(bf16[2048,128]{1,0:T(8,128)(2,1)S(1)} %collective-permute-done.6.refs_3_), channel_id=1, source_target_pairs={{0,4},{4,0},{8,12},{12,8},{16,20},{20,16},{24,28},{28,24},{1,5},{5... | collective-permute-start | bytes 1572872 | tf_op jit(solution)/shard_map/ppermute | solution.py:23
  34.4 0.1 collective-permute-start.8
  34.4 0.4 collective-permute-start.9
  34.9 1.0 collective-permute-done.10.refs_7_
  35.9 0.7 collective-permute-done.8.refs_5_
  36.6 0.7 collective-permute-done.9.refs_6_
  37.4 1.0 copy-done
  38.4 1.0 copy-done.3
  39.5 2.1 %early_products.1 = (f32[2048,128]{1,0:T(8,128)S(1)}, bf16[4096,128]{1,0:T(8,128)(2,1)S(1)}, bf16[512,512]{1,0:T(8,128)(2,1)S(1)}, bf16[8,512]{1,0:T(8,128)(2,1)S(1)}) custom-call(bf16[2048,128]{1,0:T(8,128)(2,1)S(1)} %copy-done.3, bf16[2048,128]{1,0:T(8,128)(2,1)S(1)} %collective-permute-done.4.refs_1_, ...), custom_call_target="tpu_custom_call" | custom-call | tf_op jit(solution)/shard_map/early_products/pallas_call | solution.py:369
  41.6 1.6 %collective-permute-done.1.refs_0_.refs_1_ = bf16[2064,128]{1,0:T(8,128)(2,1)S(1)} collective-permute-done((bf16[2064,128]{1,0:T(8,128)(2,1)}, bf16[2064,128]{1,0:T(8,128)(2,1)S(1)}, u32[]{:S(2)}, u32[]{:S(2)}) %collective-permute-start.1) | collective-permute-done | bytes 528416 | tf_op jit(solution)/shard_map/ppermute | solution.py:389
  43.2 1.6 %late_products.1 = (bf16[512,128]{1,0:T(8,128)(2,1)S(1)}, bf16[512,128]{1,0:T(8,128)(2,1)}, bf16[512,128]{1,0:T(8,128)(2,1)S(1)}, bf16[512,128]{1,0:T(8,128)(2,1)S(1)}) custom-call(bf16[2064,128]{1,0:T(8,128)(2,1)S(1)} %collective-permute-done.1.refs_0_.refs_1_, bf16[2064,128]{1,0:T(8,128)(2,1)S(1)} %collective-permute-done.3.refs_1_.refs_2_, ...), custom_call_target="tpu_custom_call" | custom-call | flops 67108864 | bytes 3678208 | tf_op jit(solution)/shard_map/late_products/pallas_call | solution.py:369
  44.8 0.6 collective-permute-start.11
  45.4 2.1 %collective-permute-start.12 = (bf16[512,128]{1,0:T(8,128)(2,1)S(1)}, bf16[512,128]{1,0:T(8,128)(2,1)S(1)}, u32[]{:S(2)}, u32[]{:S(2)}) collective-permute-start(bf16[512,128]{1,0:T(8,128)(2,1)S(1)} %get-tuple-element.46), channel_id=1, source_target_pairs={{0,2},{1,3},{2,0},{3,1},{4,6},{5,7},{6,4},{7,5},{8,10},{9,11},{10,... | collective-permute-start | bytes 393224 | tf_op jit(solution)/shard_map/ppermute | solution.py:23
  47.5 1.4 %collective-permute-done.11.refs_1_ = bf16[512,128]{1,0:T(8,128)(2,1)S(1)} collective-permute-done((bf16[512,128]{1,0:T(8,128)(2,1)}, bf16[512,128]{1,0:T(8,128)(2,1)S(1)}, u32[]{:S(2)}, u32[]{:S(2)}) %collective-permute-start.11) | collective-permute-done | bytes 131104 | tf_op jit(solution)/shard_map/ppermute | solution.py:23
  48.9 3.0 %collective-permute-done.12.refs_2_ = bf16[512,128]{1,0:T(8,128)(2,1)S(1)} collective-permute-done((bf16[512,128]{1,0:T(8,128)(2,1)S(1)}, bf16[512,128]{1,0:T(8,128)(2,1)S(1)}, u32[]{:S(2)}, u32[]{:S(2)}) %collective-permute-start.12) | collective-permute-done | bytes 131104 | tf_op jit(solution)/shard_map/ppermute | solution.py:23
  51.9 6.1 %collective-permute-done.13.refs_3_ = bf16[512,128]{1,0:T(8,128)(2,1)S(1)} collective-permute-done((bf16[512,128]{1,0:T(8,128)(2,1)S(1)}, bf16[512,128]{1,0:T(8,128)(2,1)S(1)}, u32[]{:S(2)}, u32[]{:S(2)}) %collective-permute-start.13) | collective-permute-done | bytes 131104 | tf_op jit(solution)/shard_map/ppermute | solution.py:23
  58.0 2.0 %layer.1 = (bf16[512,512]{1,0:T(8,128)(2,1)}, bf16[512,512]{1,0:T(8,128)(2,1)S(1)}, bf16[512,128]{1,0:T(8,128)(2,1)S(1)}, bf16[512,128]{1,0:T(8,128)(2,1)S(1)}, ...) custom-call(bf16[512,128]{1,0:T(8,128)(2,1)S(1)} %get-tuple-element.44.refs_0_, ...), custom_call_target="tpu_custom_call" | custom-call | flops 536870912 | bytes 2646016 | tf_op jit(solution)/shard_map/layer/pallas_call | solution.py:369
  60.1 2.8 %collective-permute-start.15 = (bf16[512,128]{1,0:T(8,128)(2,1)S(1)}, bf16[512,128]{1,0:T(8,128)(2,1)S(1)}, u32[]{:S(2)}, u32[]{:S(2)}) collective-permute-start(bf16[512,128]{1,0:T(8,128)(2,1)S(1)} %get-tuple-element.53), channel_id=1, source_target_pairs={{0,2},{1,3},{2,0},{3,1},{4,6},{5,7},{6,4},{7,5},{8,10},{9,11},{10,... | collective-permute-start | bytes 393224 | tf_op jit(solution)/shard_map/ppermute | solution.py:23
  62.9 0.6 weight_term.1
  63.5 0.4 collective-permute-done.14.refs_4_.refs_3_
  63.9 6.8 %collective-permute-done.15.refs_5_.refs_4_ = bf16[512,128]{1,0:T(8,128)(2,1)S(1)} collective-permute-done((bf16[512,128]{1,0:T(8,128)(2,1)S(1)}, bf16[512,128]{1,0:T(8,128)(2,1)S(1)}, u32[]{:S(2)}, u32[]{:S(2)}) %collective-permute-start.15) | collective-permute-done | bytes 131104 | tf_op jit(solution)/shard_map/ppermute | solution.py:23
  70.7 3.0 %collective-permute-done.16.refs_6_.refs_5_ = bf16[512,128]{1,0:T(8,128)(2,1)S(1)} collective-permute-done((bf16[512,128]{1,0:T(8,128)(2,1)S(1)}, bf16[512,128]{1,0:T(8,128)(2,1)S(1)}, u32[]{:S(2)}, u32[]{:S(2)}) %collective-permute-start.16) | collective-permute-done | bytes 131104 | tf_op jit(solution)/shard_map/ppermute | solution.py:23
  73.7 1.7 %backward.2 = (bf16[5120,128]{1,0:T(8,128)(2,1)S(1)}, bf16[5120,128]{1,0:T(8,128)(2,1)S(1)}) custom-call(bf16[2064,128]{1,0:T(8,128)(2,1)S(1)} %collective-permute-done.2.refs_10_.refs_0_, bf16[2064,128]{1,0:T(8,128)(2,1)S(1)} %collective-permute-done.1.refs_0_.refs_1_, bf16[2064,128]{1,0:T(8,128)(2,1)S(1)} %collective-permute-done.3.refs_1_.refs_2_, ...), custom_call_target="tpu_custom_call" | custom-call | flops 134217728 | bytes 5255168 | tf_op jit(solution)/shard_map/backward/pallas_call | solution.py:369
  75.4 2.7 %collective-permute-start.17 = (bf16[5120,128]{1,0:T(8,128)(2,1)S(1)}, bf16[5120,128]{1,0:T(8,128)(2,1)S(1)}, u32[]{:S(2)}, u32[]{:S(2)}) collective-permute-start(bf16[5120,128]{1,0:T(8,128)(2,1)S(1)} %get-tuple-element.59), channel_id=1, source_target_pairs={{0,4},{4,0},{8,12},{12,8},{16,20},{20,16},{24,28},{28,24},{1,5},{5... | collective-permute-start | bytes 3932168 | tf_op jit(solution)/shard_map/ppermute | solution.py:23
  78.0 1.6 %backward.3 = (bf16[4096,128]{1,0:T(8,128)(2,1)S(1)}, bf16[4096,128]{1,0:T(8,128)(2,1)S(1)}) custom-call(bf16[2064,128]{1,0:T(8,128)(2,1)S(1)} %copy-done.1, bf16[2064,128]{1,0:T(8,128)(2,1)S(1)} %collective-permute-done.refs_9_.refs_1_, bf16[512,128]{1,0:T(8,128)(2,1)S(1)} %get-tuple-element.51.refs_3_.refs_2_, ...), custom_call_target="tpu_custom_call" | custom-call | flops 134217728 | bytes 3678208 | tf_op jit(solution)/shard_map/backward/pallas_call | solution.py:369
  79.7 0.5 collective-permute-start.21
  80.2 0.5 collective-permute-done.17.refs_1_
  80.7 0.3 pair_sum.2
  81.0 1.7 %collective-permute-start.18 = (bf16[1280,128]{1,0:T(8,128)(2,1)S(1)}, bf16[1280,128]{1,0:T(8,128)(2,1)S(1)}, u32[]{:S(2)}, u32[]{:S(2)}) collective-permute-start(bf16[1280,128]{1,0:T(8,128)(2,1)S(1)} %get-tuple-element.62), channel_id=1, source_target_pairs={{0,8},{4,12},{8,0},{12,4},{16,24},{20,28},{24,16},{28,20},{1,9},{5... | collective-permute-start | bytes 983048 | tf_op jit(solution)/shard_map/ppermute | solution.py:23
  82.7 0.5 collective-permute-start.19
  83.2 0.7 collective-permute-start.20
  84.0 0.2 pair_sum.3
  84.2 1.5 %collective-permute-start.25 = (bf16[1024,128]{1,0:T(8,128)(2,1)S(1)}, bf16[1024,128]{1,0:T(8,128)(2,1)S(1)}, u32[]{:S(2)}, u32[]{:S(2)}) collective-permute-start(bf16[1024,128]{1,0:T(8,128)(2,1)S(1)} %get-tuple-element.70), channel_id=1, source_target_pairs={{0,8},{4,12},{8,0},{12,4},{16,24},{20,28},{24,16},{28,20},{1,9},{5... | collective-permute-start | bytes 786440 | tf_op jit(solution)/shard_map/ppermute | solution.py:23
  85.7 0.5 collective-permute-start.26
  86.2 4.2 %collective-permute-done.18.refs_1_ = bf16[1280,128]{1,0:T(8,128)(2,1)S(1)} collective-permute-done((bf16[1280,128]{1,0:T(8,128)(2,1)S(1)}, bf16[1280,128]{1,0:T(8,128)(2,1)S(1)}, u32[]{:S(2)}, u32[]{:S(2)}) %collective-permute-start.18) | collective-permute-done | bytes 327712 | tf_op jit(solution)/shard_map/ppermute | solution.py:23
  90.3 1.5 %collective-permute-start.27 = (bf16[1024,128]{1,0:T(8,128)(2,1)S(1)}, bf16[1024,128]{1,0:T(8,128)(2,1)S(1)}, u32[]{:S(2)}, u32[]{:S(2)}) collective-permute-start(bf16[1024,128]{1,0:T(8,128)(2,1)S(1)} %get-tuple-element.72), channel_id=1, source_target_pairs={{0,24},{4,28},{8,16},{12,20},{16,8},{20,12},{24,0},{28,4},{1,25},{... | collective-permute-start | bytes 786440 | tf_op jit(solution)/shard_map/ppermute | solution.py:23
  91.9 6.3 %collective-permute-done.20.refs_3_ = bf16[1280,128]{1,0:T(8,128)(2,1)S(1)} collective-permute-done((bf16[1280,128]{1,0:T(8,128)(2,1)S(1)}, bf16[1280,128]{1,0:T(8,128)(2,1)S(1)}, u32[]{:S(2)}, u32[]{:S(2)}) %collective-permute-start.20) | collective-permute-done | bytes 327712 | tf_op jit(solution)/shard_map/ppermute | solution.py:23
  98.2 0.2 plane_sum.2
  98.3 0.4 collective-permute-start.23
  98.8 1.2 collective-permute-start.24
  100.0 3.0 %collective-permute-done.25.refs_1_ = bf16[1024,128]{1,0:T(8,128)(2,1)S(1)} collective-permute-done((bf16[1024,128]{1,0:T(8,128)(2,1)S(1)}, bf16[1024,128]{1,0:T(8,128)(2,1)S(1)}, u32[]{:S(2)}, u32[]{:S(2)}) %collective-permute-start.25) | collective-permute-done | bytes 262176 | tf_op jit(solution)/shard_map/ppermute | solution.py:23
  103.0 1.1 collective-permute-done.26.refs_2_
  104.1 5.3 %collective-permute-done.27.refs_3_ = bf16[1024,128]{1,0:T(8,128)(2,1)S(1)} collective-permute-done((bf16[1024,128]{1,0:T(8,128)(2,1)S(1)}, bf16[1024,128]{1,0:T(8,128)(2,1)S(1)}, u32[]{:S(2)}, u32[]{:S(2)}) %collective-permute-start.27) | collective-permute-done | bytes 262176 | tf_op jit(solution)/shard_map/ppermute | solution.py:23
  109.4 0.1 plane_sum.3
  109.7 7.2 %collective-permute-done.24.refs_3_ = bf16[768,128]{1,0:T(8,128)(2,1)S(1)} collective-permute-done((bf16[768,128]{1,0:T(8,128)(2,1)S(1)}, bf16[768,128]{1,0:T(8,128)(2,1)S(1)}, u32[]{:S(2)}, u32[]{:S(2)}) %collective-permute-start.24) | collective-permute-done | bytes 196640 | tf_op jit(solution)/shard_map/ppermute | solution.py:23
  116.9 0.5 collective-permute-start.28
  117.4 1.8 %collective-permute-start.29 = (bf16[256,128]{1,0:T(8,128)(2,1)S(1)}, bf16[256,128]{1,0:T(8,128)(2,1)S(1)}, u32[]{:S(2)}, u32[]{:S(2)}) collective-permute-start(bf16[256,128]{1,0:T(8,128)(2,1)S(1)} %weight_total.1.refs_0_), channel_id=1, source_target_pairs={{0,16},{4,20},{8,24},{12,28},{16,0},{20,4},{24,8},{28,12},{1,17},{... | collective-permute-start | bytes 196616 | tf_op jit(solution)/shard_map/ppermute | solution.py:23
  119.3 0.4 collective-permute-start.30
  119.6 0.5 collective-permute-done.28.refs_1_
  120.1 0.8 collective-permute-done.29.refs_2_
  120.9 2.5 %collective-permute-done.30.refs_3_ = bf16[256,128]{1,0:T(8,128)(2,1)S(1)} collective-permute-done((bf16[256,128]{1,0:T(8,128)(2,1)S(1)}, bf16[256,128]{1,0:T(8,128)(2,1)S(1)}, u32[]{:S(2)}, u32[]{:S(2)}) %collective-permute-start.30) | collective-permute-done | bytes 65568 | tf_op jit(solution)/shard_map/ppermute | solution.py:23
  123.5 2.8 %collective-permute-start.32 = (bf16[256,512]{1,0:T(8,128)(2,1)S(1)}, bf16[256,512]{1,0:T(8,128)(2,1)S(1)}, u32[]{:S(2)}, u32[]{:S(2)}) collective-permute-start(bf16[256,512]{1,0:T(8,128)(2,1)S(1)} %weight_half.1.refs_0_), channel_id=1, source_target_pairs={{0,4},{4,0},{8,12},{12,8},{16,20},{20,16},{24,28},{28,24},{1,5},{5... | collective-permute-start | bytes 786440 | tf_op jit(solution)/shard_map/ppermute | solution.py:23
  126.3 0.9 join.1
  127.2 0.2 collective-permute-done.32.refs_1_
  127.5 1.1 weight_whole.1
  (33 shorter events, 0.4 us)
Async XLA Ops:
  1.3 36.1 %copy-start.2 = (bf16[512,512]{1,0:T(8,128)(2,1)S(1)}, bf16[512,512]{1,0:T(8,128)(2,1)}, u32[]{:S(2)}) copy-start(bf16[512,512]{1,0:T(8,128)(2,1)} %refs_11_.1) | copy-start | bytes 1572868
  1.3 36.1 %copy-start.4 = (bf16[8,512]{1,0:T(8,128)(2,1)S(1)}, bf16[8,512]{1,0:T(8,128)(2,1)}, u32[]{:S(2)}) copy-start(bf16[8,512]{1,0:T(8,128)(2,1)} %refs_12_.1) | copy-start | bytes 24580
  3.6 22.6 %collective-permute-start = (bf16[2064,128]{1,0:T(8,128)(2,1)}, bf16[2064,128]{1,0:T(8,128)(2,1)S(1)}, u32[]{:S(2)}, u32[]{:S(2)}) collective-permute-start(bf16[2064,128]{1,0:T(8,128)(2,1)} %get-tuple-element.40.refs_8_.refs_0_), channel_id=1, source_target_pairs={{0,1},{1,0},{2,3},{3,2},{4,5},{5,4},{6,7},{7,6},{8,9},{9,8},{10,11... | collective-permute-start | bytes 1585160 | tf_op jit(solution)/shard_map/ppermute | solution.py:23
  3.7 27.1 %collective-permute-start.2 = (bf16[2064,128]{1,0:T(8,128)(2,1)}, bf16[2064,128]{1,0:T(8,128)(2,1)S(1)}, u32[]{:S(2)}, u32[]{:S(2)}) collective-permute-start(bf16[2064,128]{1,0:T(8,128)(2,1)} %get-tuple-element.40.refs_8_.refs_0_), channel_id=1, source_target_pairs={{0,2},{1,3},{2,0},{3,1},{4,6},{5,7},{6,4},{7,5},{8,10},{9,11},{10,... | collective-permute-start | bytes 1585160 | tf_op jit(solution)/shard_map/ppermute | solution.py:23
  6.1 21.3 %collective-permute-start.6 = (bf16[2048,128]{1,0:T(8,128)(2,1)}, bf16[2048,128]{1,0:T(8,128)(2,1)S(1)}, u32[]{:S(2)}, u32[]{:S(2)}) collective-permute-start(bf16[2048,128]{1,0:T(8,128)(2,1)} %get-tuple-element.41.refs_0_), channel_id=1, source_target_pairs={{0,24},{4,28},{8,16},{12,20},{16,8},{20,12},{24,0},{28,4},{1,25},{... | collective-permute-start | bytes 1572872 | tf_op jit(solution)/shard_map/ppermute | solution.py:23
  8.3 23.8 %collective-permute-start.4 = (bf16[2048,128]{1,0:T(8,128)(2,1)}, bf16[2048,128]{1,0:T(8,128)(2,1)S(1)}, u32[]{:S(2)}, u32[]{:S(2)}) collective-permute-start(bf16[2048,128]{1,0:T(8,128)(2,1)} %get-tuple-element.41.refs_0_), channel_id=1, source_target_pairs={{0,8},{4,12},{8,0},{12,4},{16,24},{20,28},{24,16},{28,20},{1,9},{5... | collective-permute-start | bytes 1572872 | tf_op jit(solution)/shard_map/ppermute | solution.py:23
  8.6 25.8 %collective-permute-start.5 = (bf16[2048,128]{1,0:T(8,128)(2,1)}, bf16[2048,128]{1,0:T(8,128)(2,1)S(1)}, u32[]{:S(2)}, u32[]{:S(2)}) collective-permute-start(bf16[2048,128]{1,0:T(8,128)(2,1)} %get-tuple-element.41.refs_0_), channel_id=1, source_target_pairs={{0,16},{4,20},{8,24},{12,28},{16,0},{20,4},{24,8},{28,12},{1,17},{... | collective-permute-start | bytes 1572872 | tf_op jit(solution)/shard_map/ppermute | solution.py:23
  26.2 8.3 %collective-permute-start.7 = (bf16[2048,128]{1,0:T(8,128)(2,1)}, bf16[2048,128]{1,0:T(8,128)(2,1)S(1)}, u32[]{:S(2)}, u32[]{:S(2)}) collective-permute-start(bf16[2048,128]{1,0:T(8,128)(2,1)} %get-tuple-element.41.refs_0_), channel_id=1, source_target_pairs={{0,4},{4,0},{8,12},{12,8},{16,20},{20,16},{24,28},{28,24},{1,5},{5... | collective-permute-start | bytes 1572872 | tf_op jit(solution)/shard_map/ppermute | solution.py:23
  27.4 15.8 %collective-permute-start.1 = (bf16[2064,128]{1,0:T(8,128)(2,1)}, bf16[2064,128]{1,0:T(8,128)(2,1)S(1)}, u32[]{:S(2)}, u32[]{:S(2)}) collective-permute-start(bf16[2064,128]{1,0:T(8,128)(2,1)} %get-tuple-element.40.refs_8_.refs_0_), channel_id=1, source_target_pairs={{1,2},{2,1},{5,6},{6,5},{9,10},{10,9},{13,14},{14,13},{17,18},{18,... | collective-permute-start | bytes 1585160 | tf_op jit(solution)/shard_map/ppermute | solution.py:389
  30.8 12.4 %collective-permute-start.3 = (bf16[2064,128]{1,0:T(8,128)(2,1)S(1)}, bf16[2064,128]{1,0:T(8,128)(2,1)S(1)}, u32[]{:S(2)}, u32[]{:S(2)}) collective-permute-start(bf16[2064,128]{1,0:T(8,128)(2,1)S(1)} %collective-permute-done.2.refs_10_.refs_0_), channel_id=1, source_target_pairs={{2,3},{1,0},{6,7},{5,4},{10,11},{9,8},{14,15},{13,12},{18,19},{17,... | collective-permute-start | bytes 1585160 | tf_op jit(solution)/shard_map/ppermute | solution.py:387
  32.2 3.7 %collective-permute-start.10 = (bf16[2048,128]{1,0:T(8,128)(2,1)S(1)}, bf16[2048,128]{1,0:T(8,128)(2,1)S(1)}, u32[]{:S(2)}, u32[]{:S(2)}) collective-permute-start(bf16[2048,128]{1,0:T(8,128)(2,1)S(1)} %collective-permute-done.6.refs_3_), channel_id=1, source_target_pairs={{0,4},{4,0},{8,12},{12,8},{16,20},{20,16},{24,28},{28,24},{1,5},{5... | collective-permute-start | bytes 1572872 | tf_op jit(solution)/shard_map/ppermute | solution.py:23
  34.4 2.3 %collective-permute-start.8 = (bf16[2048,128]{1,0:T(8,128)(2,1)S(1)}, bf16[2048,128]{1,0:T(8,128)(2,1)S(1)}, u32[]{:S(2)}, u32[]{:S(2)}) collective-permute-start(bf16[2048,128]{1,0:T(8,128)(2,1)S(1)} %collective-permute-done.4.refs_1_), channel_id=1, source_target_pairs={{0,4},{4,0},{8,12},{12,8},{16,20},{20,16},{24,28},{28,24},{1,5},{5... | collective-permute-start | bytes 1572872 | tf_op jit(solution)/shard_map/ppermute | solution.py:23
  34.4 2.9 %collective-permute-start.9 = (bf16[2048,128]{1,0:T(8,128)(2,1)S(1)}, bf16[2048,128]{1,0:T(8,128)(2,1)S(1)}, u32[]{:S(2)}, u32[]{:S(2)}) collective-permute-start(bf16[2048,128]{1,0:T(8,128)(2,1)S(1)} %collective-permute-done.5.refs_2_), channel_id=1, source_target_pairs={{0,4},{4,0},{8,12},{12,8},{16,20},{20,16},{24,28},{28,24},{1,5},{5... | collective-permute-start | bytes 1572872 | tf_op jit(solution)/shard_map/ppermute | solution.py:23
  37.4 1.0 copy-start
  38.4 1.0 copy-start.3
  43.2 4.3 %copy-start.5 = (s32[2048]{0:T(1024)S(1)}, s32[2048]{0:T(1024)}, u32[]{:S(2)}) copy-start(s32[2048]{0:T(1024)} %param.12) | copy-start | bytes 24580
  43.2 4.3 %copy-start.6 = (s32[2048]{0:T(1024)S(1)}, s32[2048]{0:T(1024)}, u32[]{:S(2)}) copy-start(s32[2048]{0:T(1024)} %param.13) | copy-start | bytes 24580
  44.8 4.1 %collective-permute-start.11 = (bf16[512,128]{1,0:T(8,128)(2,1)}, bf16[512,128]{1,0:T(8,128)(2,1)S(1)}, u32[]{:S(2)}, u32[]{:S(2)}) collective-permute-start(bf16[512,128]{1,0:T(8,128)(2,1)} %get-tuple-element.45), channel_id=1, source_target_pairs={{0,1},{1,0},{2,3},{3,2},{4,5},{5,4},{6,7},{7,6},{8,9},{9,8},{10,11... | collective-permute-start | bytes 393224 | tf_op jit(solution)/shard_map/ppermute | solution.py:23
  45.4 6.5 %collective-permute-start.12 = (bf16[512,128]{1,0:T(8,128)(2,1)S(1)}, bf16[512,128]{1,0:T(8,128)(2,1)S(1)}, u32[]{:S(2)}, u32[]{:S(2)}) collective-permute-start(bf16[512,128]{1,0:T(8,128)(2,1)S(1)} %get-tuple-element.46), channel_id=1, source_target_pairs={{0,2},{1,3},{2,0},{3,1},{4,6},{5,7},{6,4},{7,5},{8,10},{9,11},{10,... | collective-permute-start | bytes 393224 | tf_op jit(solution)/shard_map/ppermute | solution.py:23
  47.5 10.5 %collective-permute-start.13 = (bf16[512,128]{1,0:T(8,128)(2,1)S(1)}, bf16[512,128]{1,0:T(8,128)(2,1)S(1)}, u32[]{:S(2)}, u32[]{:S(2)}) collective-permute-start(bf16[512,128]{1,0:T(8,128)(2,1)S(1)} %get-tuple-element.47), channel_id=1, source_target_pairs={{0,3},{1,2},{2,1},{3,0},{4,7},{5,6},{6,5},{7,4},{8,11},{9,10},{10,... | collective-permute-start | bytes 393224 | tf_op jit(solution)/shard_map/ppermute | solution.py:23
  60.0 3.9 %collective-permute-start.14 = (bf16[512,128]{1,0:T(8,128)(2,1)S(1)}, bf16[512,128]{1,0:T(8,128)(2,1)S(1)}, u32[]{:S(2)}, u32[]{:S(2)}) collective-permute-start(bf16[512,128]{1,0:T(8,128)(2,1)S(1)} %get-tuple-element.52), channel_id=1, source_target_pairs={{0,1},{1,0},{2,3},{3,2},{4,5},{5,4},{6,7},{7,6},{8,9},{9,8},{10,11... | collective-permute-start | bytes 393224 | tf_op jit(solution)/shard_map/ppermute | solution.py:23
  60.1 10.6 %collective-permute-start.15 = (bf16[512,128]{1,0:T(8,128)(2,1)S(1)}, bf16[512,128]{1,0:T(8,128)(2,1)S(1)}, u32[]{:S(2)}, u32[]{:S(2)}) collective-permute-start(bf16[512,128]{1,0:T(8,128)(2,1)S(1)} %get-tuple-element.53), channel_id=1, source_target_pairs={{0,2},{1,3},{2,0},{3,1},{4,6},{5,7},{6,4},{7,5},{8,10},{9,11},{10,... | collective-permute-start | bytes 393224 | tf_op jit(solution)/shard_map/ppermute | solution.py:23
  62.9 10.7 %collective-permute-start.16 = (bf16[512,128]{1,0:T(8,128)(2,1)S(1)}, bf16[512,128]{1,0:T(8,128)(2,1)S(1)}, u32[]{:S(2)}, u32[]{:S(2)}) collective-permute-start(bf16[512,128]{1,0:T(8,128)(2,1)S(1)} %get-tuple-element.54), channel_id=1, source_target_pairs={{0,3},{1,2},{2,1},{3,0},{4,7},{5,6},{6,5},{7,4},{8,11},{9,10},{10,... | collective-permute-start | bytes 393224 | tf_op jit(solution)/shard_map/ppermute | solution.py:23
  73.7 4.4 %copy-start.1 = (bf16[2064,128]{1,0:T(8,128)(2,1)S(1)}, bf16[2064,128]{1,0:T(8,128)(2,1)}, u32[]{:S(2)}) copy-start(bf16[2064,128]{1,0:T(8,128)(2,1)} %get-tuple-element.40.refs_8_.refs_0_) | copy-start | bytes 1585156
  75.4 5.3 %collective-permute-start.17 = (bf16[5120,128]{1,0:T(8,128)(2,1)S(1)}, bf16[5120,128]{1,0:T(8,128)(2,1)S(1)}, u32[]{:S(2)}, u32[]{:S(2)}) collective-permute-start(bf16[5120,128]{1,0:T(8,128)(2,1)S(1)} %get-tuple-element.59), channel_id=1, source_target_pairs={{0,4},{4,0},{8,12},{12,8},{16,20},{20,16},{24,28},{28,24},{1,5},{5... | collective-permute-start | bytes 3932168 | tf_op jit(solution)/shard_map/ppermute | solution.py:23
  79.7 4.3 %collective-permute-start.21 = (bf16[4096,128]{1,0:T(8,128)(2,1)S(1)}, bf16[4096,128]{1,0:T(8,128)(2,1)S(1)}, u32[]{:S(2)}, u32[]{:S(2)}) collective-permute-start(bf16[4096,128]{1,0:T(8,128)(2,1)S(1)} %get-tuple-element.65), channel_id=1, source_target_pairs={{0,4},{4,0},{8,12},{12,8},{16,20},{20,16},{24,28},{28,24},{1,5},{5... | collective-permute-start | bytes 3145736 | tf_op jit(solution)/shard_map/ppermute | solution.py:23
  81.0 9.4 %collective-permute-start.18 = (bf16[1280,128]{1,0:T(8,128)(2,1)S(1)}, bf16[1280,128]{1,0:T(8,128)(2,1)S(1)}, u32[]{:S(2)}, u32[]{:S(2)}) collective-permute-start(bf16[1280,128]{1,0:T(8,128)(2,1)S(1)} %get-tuple-element.62), channel_id=1, source_target_pairs={{0,8},{4,12},{8,0},{12,4},{16,24},{20,28},{24,16},{28,20},{1,9},{5... | collective-permute-start | bytes 983048 | tf_op jit(solution)/shard_map/ppermute | solution.py:23
  82.7 9.2 %collective-permute-start.19 = (bf16[1280,128]{1,0:T(8,128)(2,1)S(1)}, bf16[1280,128]{1,0:T(8,128)(2,1)S(1)}, u32[]{:S(2)}, u32[]{:S(2)}) collective-permute-start(bf16[1280,128]{1,0:T(8,128)(2,1)S(1)} %get-tuple-element.63), channel_id=1, source_target_pairs={{0,16},{4,20},{8,24},{12,28},{16,0},{20,4},{24,8},{28,12},{1,17},{... | collective-permute-start | bytes 983048 | tf_op jit(solution)/shard_map/ppermute | solution.py:23
  83.2 14.9 %collective-permute-start.20 = (bf16[1280,128]{1,0:T(8,128)(2,1)S(1)}, bf16[1280,128]{1,0:T(8,128)(2,1)S(1)}, u32[]{:S(2)}, u32[]{:S(2)}) collective-permute-start(bf16[1280,128]{1,0:T(8,128)(2,1)S(1)} %get-tuple-element.64), channel_id=1, source_target_pairs={{0,24},{4,28},{8,16},{12,20},{16,8},{20,12},{24,0},{28,4},{1,25},{... | collective-permute-start | bytes 983048 | tf_op jit(solution)/shard_map/ppermute | solution.py:23
  84.2 18.8 %collective-permute-start.25 = (bf16[1024,128]{1,0:T(8,128)(2,1)S(1)}, bf16[1024,128]{1,0:T(8,128)(2,1)S(1)}, u32[]{:S(2)}, u32[]{:S(2)}) collective-permute-start(bf16[1024,128]{1,0:T(8,128)(2,1)S(1)} %get-tuple-element.70), channel_id=1, source_target_pairs={{0,8},{4,12},{8,0},{12,4},{16,24},{20,28},{24,16},{28,20},{1,9},{5... | collective-permute-start | bytes 786440 | tf_op jit(solution)/shard_map/ppermute | solution.py:23
  85.7 18.4 %collective-permute-start.26 = (bf16[1024,128]{1,0:T(8,128)(2,1)S(1)}, bf16[1024,128]{1,0:T(8,128)(2,1)S(1)}, u32[]{:S(2)}, u32[]{:S(2)}) collective-permute-start(bf16[1024,128]{1,0:T(8,128)(2,1)S(1)} %get-tuple-element.71), channel_id=1, source_target_pairs={{0,16},{4,20},{8,24},{12,28},{16,0},{20,4},{24,8},{28,12},{1,17},{... | collective-permute-start | bytes 786440 | tf_op jit(solution)/shard_map/ppermute | solution.py:23
  90.3 19.1 %collective-permute-start.27 = (bf16[1024,128]{1,0:T(8,128)(2,1)S(1)}, bf16[1024,128]{1,0:T(8,128)(2,1)S(1)}, u32[]{:S(2)}, u32[]{:S(2)}) collective-permute-start(bf16[1024,128]{1,0:T(8,128)(2,1)S(1)} %get-tuple-element.72), channel_id=1, source_target_pairs={{0,24},{4,28},{8,16},{12,20},{16,8},{20,12},{24,0},{28,4},{1,25},{... | collective-permute-start | bytes 786440 | tf_op jit(solution)/shard_map/ppermute | solution.py:23
  98.3 11.3 %collective-permute-start.23 = (bf16[768,128]{1,0:T(8,128)(2,1)S(1)}, bf16[768,128]{1,0:T(8,128)(2,1)S(1)}, u32[]{:S(2)}, u32[]{:S(2)}) collective-permute-start(bf16[768,128]{1,0:T(8,128)(2,1)S(1)} %get-tuple-element.68), channel_id=1, source_target_pairs={{0,2},{1,3},{2,0},{3,1},{4,6},{5,7},{6,4},{7,5},{8,10},{9,11},{10,... | collective-permute-start | bytes 589832 | tf_op jit(solution)/shard_map/ppermute | solution.py:23
  98.8 18.1 %collective-permute-start.24 = (bf16[768,128]{1,0:T(8,128)(2,1)S(1)}, bf16[768,128]{1,0:T(8,128)(2,1)S(1)}, u32[]{:S(2)}, u32[]{:S(2)}) collective-permute-start(bf16[768,128]{1,0:T(8,128)(2,1)S(1)} %get-tuple-element.69), channel_id=1, source_target_pairs={{0,3},{1,2},{2,1},{3,0},{4,7},{5,6},{6,5},{7,4},{8,11},{9,10},{10,... | collective-permute-start | bytes 589832 | tf_op jit(solution)/shard_map/ppermute | solution.py:23
  103.0 6.6 %collective-permute-start.22 = (bf16[256,128]{1,0:T(8,128)(2,1)S(1)}, bf16[256,128]{1,0:T(8,128)(2,1)S(1)}, u32[]{:S(2)}, u32[]{:S(2)}) collective-permute-start(bf16[256,128]{1,0:T(8,128)(2,1)S(1)} %get-tuple-element.67.refs_0_), channel_id=1, source_target_pairs={{0,1},{1,0},{2,3},{3,2},{4,5},{5,4},{6,7},{7,6},{8,9},{9,8},{10,11... | collective-permute-start | bytes 196616 | tf_op jit(solution)/shard_map/ppermute | solution.py:23
  109.6 10.1 %collective-permute-start.31 = (bf16[512,128]{1,0:T(8,128)(2,1)S(1)}, bf16[512,128]{1,0:T(8,128)(2,1)S(1)}, u32[]{:S(2)}, u32[]{:S(2)}) collective-permute-start(bf16[512,128]{1,0:T(8,128)(2,1)S(1)} %get-tuple-element.74), channel_id=1, source_target_pairs={{0,1},{1,0},{2,3},{3,2},{4,5},{5,4},{6,7},{7,6},{8,9},{9,8},{10,11... | collective-permute-start | bytes 393224 | tf_op jit(solution)/shard_map/ppermute | solution.py:23
  116.9 3.2 %collective-permute-start.28 = (bf16[256,128]{1,0:T(8,128)(2,1)S(1)}, bf16[256,128]{1,0:T(8,128)(2,1)S(1)}, u32[]{:S(2)}, u32[]{:S(2)}) collective-permute-start(bf16[256,128]{1,0:T(8,128)(2,1)S(1)} %weight_total.1.refs_0_), channel_id=1, source_target_pairs={{0,8},{4,12},{8,0},{12,4},{16,24},{20,28},{24,16},{28,20},{1,9},{5... | collective-permute-start | bytes 196616 | tf_op jit(solution)/shard_map/ppermute | solution.py:23
  117.4 3.5 %collective-permute-start.29 = (bf16[256,128]{1,0:T(8,128)(2,1)S(1)}, bf16[256,128]{1,0:T(8,128)(2,1)S(1)}, u32[]{:S(2)}, u32[]{:S(2)}) collective-permute-start(bf16[256,128]{1,0:T(8,128)(2,1)S(1)} %weight_total.1.refs_0_), channel_id=1, source_target_pairs={{0,16},{4,20},{8,24},{12,28},{16,0},{20,4},{24,8},{28,12},{1,17},{... | collective-permute-start | bytes 196616 | tf_op jit(solution)/shard_map/ppermute | solution.py:23
  119.3 4.1 %collective-permute-start.30 = (bf16[256,128]{1,0:T(8,128)(2,1)S(1)}, bf16[256,128]{1,0:T(8,128)(2,1)S(1)}, u32[]{:S(2)}, u32[]{:S(2)}) collective-permute-start(bf16[256,128]{1,0:T(8,128)(2,1)S(1)} %weight_total.1.refs_0_), channel_id=1, source_target_pairs={{0,24},{4,28},{8,16},{12,20},{16,8},{20,12},{24,0},{28,4},{1,25},{... | collective-permute-start | bytes 196616 | tf_op jit(solution)/shard_map/ppermute | solution.py:23
  123.5 4.0 %collective-permute-start.32 = (bf16[256,512]{1,0:T(8,128)(2,1)S(1)}, bf16[256,512]{1,0:T(8,128)(2,1)S(1)}, u32[]{:S(2)}, u32[]{:S(2)}) collective-permute-start(bf16[256,512]{1,0:T(8,128)(2,1)S(1)} %weight_half.1.refs_0_), channel_id=1, source_target_pairs={{0,4},{4,0},{8,12},{12,8},{16,20},{20,16},{24,28},{28,24},{1,5},{5... | collective-permute-start | bytes 786440 | tf_op jit(solution)/shard_map/ppermute | solution.py:23

commit v5 on v4

--- a/solution.py
+++ b/solution.py
@@ -42,20 +42,6 @@
             return carry
 
         lax.fori_loop(0, (live + GROUP - 1) // GROUP, step, 0)
-
-
-def fetch_late(place, teams, middle, relayed, target, sem):
-    at_end = (place[0] == 0) | (place[0] == teams - 1)
-
-    @pl.when(at_end)
-    def _():
-        pltpu.make_async_copy(relayed, target, sem).start()
-
-    @pl.when(jnp.logical_not(at_end))
-    def _():
-        pltpu.make_async_copy(middle, target, sem).start()
-
-    return pltpu.make_async_copy(middle, target, sem)
 
 
 def forward_visit(panels, panel_rows, lists, ids, totals):
@@ -141,17 +127,22 @@
     late_panel[...] = panels[pl.ds(start, panel_rows), :]
 
 
+def pick(place, teams, middle, relayed, here):
+    at_end = (place[0] == 0) | (place[0] == teams - 1)
+    return jnp.where(at_end, relayed[here, :], middle[here, :])
+
+
 def late_kernel(teams, slots, place, *refs):
     middle, relayed, begun, panel = refs[:4]
     outs = refs[4 : 4 + teams]
-    totals, lists, ids_vmem, ids_smem, sem, id_sem = refs[4 + teams :]
-    fetch = fetch_late(place, teams, middle, relayed, lists.at[0], sem)
-
-    def take():
-        totals[...] = begun[...]
-
-    fetch.wait()
-    load_ids(ids_vmem, ids_smem, lists, slots, id_sem, take)
+    totals, lists, ids_vmem, ids_smem, id_sem = refs[4 + teams :]
+    tail = pick(place, teams, middle, relayed, pl.ds(slots * BLOCK, ID_ROWS))
+    ids_vmem[0] = tail.astype(jnp.float32).astype(jnp.int32)[:8]
+    copy = pltpu.make_async_copy(ids_vmem, ids_smem, id_sem)
+    copy.start()
+    totals[...] = begun[...]
+    lists[0] = pick(place, teams, middle, relayed, slice(None))
+    copy.wait()
     visit = forward_visit(panel, 0, lists, ids_smem, totals)
     each_group(ids_smem, place, [teams - 1], visit)
     share = outs[0].shape[0]
@@ -165,7 +156,7 @@
     weight, table, *fixed = refs[teams : teams + 4]
     output, grad_pre = refs[teams + 4 : teams + 6]
     backs = refs[teams + 6 : 2 * teams + 6]
-    labels, mask, sems = refs[2 * teams + 6 :]
+    labels, mask, cols, sems = refs[2 * teams + 6 :]
     team = place[0]
     width = parts[0].shape[1]
     copies = [
@@ -175,12 +166,10 @@
     for copy in copies:
         copy.start()
 
-    def weight_rows(d):
-        return weight[pl.ds(pl.multiple_of((team ^ d) * width, width), width), :]
-
-    preact = jnp.dot(parts[0][...], weight_rows(0), preferred_element_type=jnp.float32)
-    for d in range(1, teams):
-        preact += jnp.dot(parts[d][...], weight_rows(d), preferred_element_type=jnp.float32)
+    for d in range(teams):
+        cols[team ^ d] = parts[d][...]
+    agg = jnp.concatenate([cols[t] for t in range(teams)], axis=1)
+    preact = jnp.dot(agg, weight[...], preferred_element_type=jnp.float32)
     sigma = 1.0 / (1.0 + jnp.exp(-preact))
     active = preact * sigma
     output[...] = active.astype(jnp.bfloat16)
@@ -200,10 +189,13 @@
     slope = sigma * (1.0 + preact * (1.0 - sigma))
     grad = ((masked * active - target) * slope).astype(jnp.bfloat16)
     grad_pre[...] = grad
+    back = lax.dot_general(
+        grad, weight[...], (((1,), (1,)), ((), ())), preferred_element_type=jnp.float32
+    ).astype(jnp.bfloat16)
+    for t in range(teams):
+        cols[t] = back[:, t * width : (t + 1) * width]
     for d in range(teams):
-        backs[d][...] = lax.dot_general(
-            grad, weight_rows(d), (((1,), (1,)), ((), ())), preferred_element_type=jnp.float32
-        ).astype(jnp.bfloat16)
+        backs[d][...] = cols[team ^ d]
 
 
 def weight_kernel(teams, chips, place, *refs):
@@ -261,11 +253,10 @@
     given = refs[: count + last]
     backs = refs[count + last : count + last + teams]
     refs = refs[count + last + teams :]
-    at_end = (place[0] == 0) | (place[0] == teams - 1)
 
     def held(i, here):
         if last and i == count - 1:
-            return jnp.where(at_end, given[i + 1][here, :], given[i][here, :])
+            return pick(place, teams, given[i], given[i + 1], here)
         return given[i][here, :]
 
     rider_refs, refs = refs[:riders], refs[riders:]
@@ -481,16 +472,15 @@
         functools.partial(late_kernel, teams, slots),
         "late_products",
         [*late, begun, late_panel],
-        [any_space, any_space, vmem, vmem],
+        [vmem] * 4,
         [shaped(share, part)] * teams,
         [
             pltpu.VMEM((slab, part), f32),
             *ids,
             pltpu.SemaphoreType.DMA,
-            pltpu.SemaphoreType.DMA,
         ],
         list_flops,
-        (panel_rows + 5 * slab) * padded * 2 + list_bytes + 3 * MIB,
+        (panel_rows + 5 * slab) * padded * 2 + 3 * list_bytes + 3 * MIB,
     )
     aggs = [sent[0]] + [swap(sent[d], "team", d) for d in range(1, teams)]
 
@@ -509,6 +499,7 @@
         [
             pltpu.VMEM((teams, share), jnp.int32),
             pltpu.VMEM((teams, share), jnp.int32),
+            pltpu.VMEM((teams, share, part), bf16),
             pltpu.SemaphoreType.DMA((2,)),
         ],
         4 * share * width * width,

time: 129 us -> 128 us (level)
  waiting for transfers between devices: 73.7 us -> 72.1 us
    ppermute x31, waiting for transfers between devices: 72.1 us -> 70.7 us  [swap(): return lax.ppermute(value, axis, [(i, i ^ flip) for i in range(size)])]
where the time goes in v5:
time: 128 us; the launch traced here: 127 us
  waiting for transfers between devices  72.1 us (56%)
  starting transfers between devices  36.7 us (29%)
  Pallas kernels  15 us (12%)
  local copies, waits for them, and re-layouts  2.12 us (2%)
  between operations  1.49 us (1%)
    ppermute x31, waiting for transfers between devices, swap(): return lax.ppermute(value, axis, [(i, i ^ flip) for i in range(size)])  70.7 us
    ppermute x31, starting transfers between devices, swap(): return lax.ppermute(value, axis, [(i, i ^ flip) for i in range(size)])  32 us
    pallas_call x15, Pallas kernels, call(): pl.pallas_call(body, name=name, in_specs=specs, out_specs=[pl.BlockSpec(m...  15 us
    ppermute x1, starting transfers between devices, gather_lists(): middle = lax.ppermute(held, 'team', [(1, 2), (2, 1)])  3.38 us
  transfers between devices with their start and end apart: 33, of which 22 were waited for; matrix products, arithmetic and copies ran while one was open for 0% of the time, Pallas kernels for 5%

profile of v5, /device:TPU:9, one launch (start us, length us, event | category | flops | bytes accessed | tf_op | source)
XLA Modules:
  0.0 127.4 jit_solution(4050619742758717271)
XLA Ops:
  1.3 2.3 %prepare.1 = (bf16[2064,128]{1,0:T(8,128)(2,1)}, bf16[2048,128]{1,0:T(8,128)(2,1)}) custom-call(bf16[2048,128]{1,0:T(8,128)(2,1)} %bitcast.5, s32[1,16]{1,0:T(1,128)} %bitcast.6, s32[1,16]{1,0:T(1,128)} %bitcast.7, s32[1,1]{1,0:T(1,128)S(6)} %copy.12.refs_3_, bf16[2048,512]{1,0:T(8,128)(2,1)} %refs_4_.1), custom_call_target="tpu_custom_call" | custom-call | tf_op jit(solution)/shard_map/prepare/pallas_call | solution.py:360
  3.7 2.5 %collective-permute-start.2 = (bf16[2064,128]{1,0:T(8,128)(2,1)}, bf16[2064,128]{1,0:T(8,128)(2,1)S(1)}, u32[]{:S(2)}, u32[]{:S(2)}) collective-permute-start(bf16[2064,128]{1,0:T(8,128)(2,1)} %get-tuple-element.40.refs_8_.refs_0_), channel_id=1, source_target_pairs={{0,2},{1,3},{2,0},{3,1},{4,6},{5,7},{6,4},{7,5},{8,10},{9,11},{10,... | collective-permute-start | bytes 1585160 | tf_op jit(solution)/shard_map/ppermute | solution.py:23
  6.1 2.2 %collective-permute-start.6 = (bf16[2048,128]{1,0:T(8,128)(2,1)}, bf16[2048,128]{1,0:T(8,128)(2,1)S(1)}, u32[]{:S(2)}, u32[]{:S(2)}) collective-permute-start(bf16[2048,128]{1,0:T(8,128)(2,1)} %get-tuple-element.41.refs_0_), channel_id=1, source_target_pairs={{0,24},{4,28},{8,16},{12,20},{16,8},{20,12},{24,0},{28,4},{1,25},{... | collective-permute-start | bytes 1572872 | tf_op jit(solution)/shard_map/ppermute | solution.py:23
  8.3 0.3 collective-permute-start.4
  8.6 0.2 collective-permute-start.5
  8.8 17.4 %collective-permute-done.refs_9_.refs_1_ = bf16[2064,128]{1,0:T(8,128)(2,1)S(1)} collective-permute-done((bf16[2064,128]{1,0:T(8,128)(2,1)}, bf16[2064,128]{1,0:T(8,128)(2,1)S(1)}, u32[]{:S(2)}, u32[]{:S(2)}) %collective-permute-start) | collective-permute-done | bytes 528416 | tf_op jit(solution)/shard_map/ppermute | solution.py:23
  26.2 1.2 collective-permute-start.7
  27.4 3.4 %collective-permute-start.1 = (bf16[2064,128]{1,0:T(8,128)(2,1)}, bf16[2064,128]{1,0:T(8,128)(2,1)S(1)}, u32[]{:S(2)}, u32[]{:S(2)}) collective-permute-start(bf16[2064,128]{1,0:T(8,128)(2,1)} %get-tuple-element.40.refs_8_.refs_0_), channel_id=1, source_target_pairs={{1,2},{2,1},{5,6},{6,5},{9,10},{10,9},{13,14},{14,13},{17,18},{18,... | collective-permute-start | bytes 1585160 | tf_op jit(solution)/shard_map/ppermute | solution.py:380
  30.8 1.3 %collective-permute-start.3 = (bf16[2064,128]{1,0:T(8,128)(2,1)S(1)}, bf16[2064,128]{1,0:T(8,128)(2,1)S(1)}, u32[]{:S(2)}, u32[]{:S(2)}) collective-permute-start(bf16[2064,128]{1,0:T(8,128)(2,1)S(1)} %collective-permute-done.2.refs_10_.refs_0_), channel_id=1, source_target_pairs={{2,3},{1,0},{6,7},{5,4},{10,11},{9,8},{14,15},{13,12},{18,19},{17,... | collective-permute-start | bytes 1585160 | tf_op jit(solution)/shard_map/ppermute | solution.py:378
  32.2 2.2 %collective-permute-start.10 = (bf16[2048,128]{1,0:T(8,128)(2,1)S(1)}, bf16[2048,128]{1,0:T(8,128)(2,1)S(1)}, u32[]{:S(2)}, u32[]{:S(2)}) collective-permute-start(bf16[2048,128]{1,0:T(8,128)(2,1)S(1)} %collective-permute-done.6.refs_3_), channel_id=1, source_target_pairs={{0,4},{4,0},{8,12},{12,8},{16,20},{20,16},{24,28},{28,24},{1,5},{5... | collective-permute-start | bytes 1572872 | tf_op jit(solution)/shard_map/ppermute | solution.py:23
  34.4 0.1 collective-permute-start.8
  34.4 0.4 collective-permute-start.9
  34.9 1.0 collective-permute-done.10.refs_7_
  35.9 0.7 collective-permute-done.8.refs_5_
  36.6 0.7 collective-permute-done.9.refs_6_
  37.4 1.0 copy-done
  38.4 1.0 copy-done.3
  39.5 2.3 %early_products.1 = (f32[2048,128]{1,0:T(8,128)S(1)}, bf16[4096,128]{1,0:T(8,128)(2,1)S(1)}, bf16[512,512]{1,0:T(8,128)(2,1)S(1)}, bf16[8,512]{1,0:T(8,128)(2,1)S(1)}) custom-call(bf16[2048,128]{1,0:T(8,128)(2,1)S(1)} %copy-done.3, bf16[2048,128]{1,0:T(8,128)(2,1)S(1)} %collective-permute-done.4.refs_1_, ...), custom_call_target="tpu_custom_call" | custom-call | tf_op jit(solution)/shard_map/early_products/pallas_call | solution.py:360
  41.8 1.5 %collective-permute-done.1.refs_0_.refs_1_ = bf16[2064,128]{1,0:T(8,128)(2,1)S(1)} collective-permute-done((bf16[2064,128]{1,0:T(8,128)(2,1)}, bf16[2064,128]{1,0:T(8,128)(2,1)S(1)}, u32[]{:S(2)}, u32[]{:S(2)}) %collective-permute-start.1) | collective-permute-done | bytes 528416 | tf_op jit(solution)/shard_map/ppermute | solution.py:380
  43.2 1.7 %late_products.1 = (bf16[512,128]{1,0:T(8,128)(2,1)S(1)}, bf16[512,128]{1,0:T(8,128)(2,1)}, bf16[512,128]{1,0:T(8,128)(2,1)S(1)}, bf16[512,128]{1,0:T(8,128)(2,1)S(1)}) custom-call(bf16[2064,128]{1,0:T(8,128)(2,1)S(1)} %collective-permute-done.1.refs_0_.refs_1_, bf16[2064,128]{1,0:T(8,128)(2,1)S(1)} %collective-permute-done.3.refs_1_.refs_2_, ...), custom_call_target="tpu_custom_call" | custom-call | flops 67108864 | bytes 3678208 | tf_op jit(solution)/shard_map/late_products/pallas_call | solution.py:360
  44.9 0.4 collective-permute-start.11
  45.4 2.2 %collective-permute-start.12 = (bf16[512,128]{1,0:T(8,128)(2,1)S(1)}, bf16[512,128]{1,0:T(8,128)(2,1)S(1)}, u32[]{:S(2)}, u32[]{:S(2)}) collective-permute-start(bf16[512,128]{1,0:T(8,128)(2,1)S(1)} %get-tuple-element.46), channel_id=1, source_target_pairs={{0,2},{1,3},{2,0},{3,1},{4,6},{5,7},{6,4},{7,5},{8,10},{9,11},{10,... | collective-permute-start | bytes 393224 | tf_op jit(solution)/shard_map/ppermute | solution.py:23
  47.7 1.4 %collective-permute-done.11.refs_1_ = bf16[512,128]{1,0:T(8,128)(2,1)S(1)} collective-permute-done((bf16[512,128]{1,0:T(8,128)(2,1)}, bf16[512,128]{1,0:T(8,128)(2,1)S(1)}, u32[]{:S(2)}, u32[]{:S(2)}) %collective-permute-start.11) | collective-permute-done | bytes 131104 | tf_op jit(solution)/shard_map/ppermute | solution.py:23
  49.0 3.2 %collective-permute-done.12.refs_2_ = bf16[512,128]{1,0:T(8,128)(2,1)S(1)} collective-permute-done((bf16[512,128]{1,0:T(8,128)(2,1)S(1)}, bf16[512,128]{1,0:T(8,128)(2,1)S(1)}, u32[]{:S(2)}, u32[]{:S(2)}) %collective-permute-start.12) | collective-permute-done | bytes 131104 | tf_op jit(solution)/shard_map/ppermute | solution.py:23
  52.2 5.9 %collective-permute-done.13.refs_3_ = bf16[512,128]{1,0:T(8,128)(2,1)S(1)} collective-permute-done((bf16[512,128]{1,0:T(8,128)(2,1)S(1)}, bf16[512,128]{1,0:T(8,128)(2,1)S(1)}, u32[]{:S(2)}, u32[]{:S(2)}) %collective-permute-start.13) | collective-permute-done | bytes 131104 | tf_op jit(solution)/shard_map/ppermute | solution.py:23
  58.2 1.4 %layer.1 = (bf16[512,512]{1,0:T(8,128)(2,1)}, bf16[512,512]{1,0:T(8,128)(2,1)S(1)}, bf16[512,128]{1,0:T(8,128)(2,1)S(1)}, bf16[512,128]{1,0:T(8,128)(2,1)S(1)}, ...) custom-call(bf16[512,128]{1,0:T(8,128)(2,1)S(1)} %get-tuple-element.44.refs_0_, ...), custom_call_target="tpu_custom_call" | custom-call | flops 536870912 | bytes 2646016 | tf_op jit(solution)/shard_map/layer/pallas_call | solution.py:360
  59.7 3.3 %collective-permute-start.15 = (bf16[512,128]{1,0:T(8,128)(2,1)S(1)}, bf16[512,128]{1,0:T(8,128)(2,1)S(1)}, u32[]{:S(2)}, u32[]{:S(2)}) collective-permute-start(bf16[512,128]{1,0:T(8,128)(2,1)S(1)} %get-tuple-element.53), channel_id=1, source_target_pairs={{0,2},{1,3},{2,0},{3,1},{4,6},{5,7},{6,4},{7,5},{8,10},{9,11},{10,... | collective-permute-start | bytes 393224 | tf_op jit(solution)/shard_map/ppermute | solution.py:23
  63.0 0.6 weight_term.1
  63.6 7.1 %collective-permute-done.15.refs_5_.refs_4_ = bf16[512,128]{1,0:T(8,128)(2,1)S(1)} collective-permute-done((bf16[512,128]{1,0:T(8,128)(2,1)S(1)}, bf16[512,128]{1,0:T(8,128)(2,1)S(1)}, u32[]{:S(2)}, u32[]{:S(2)}) %collective-permute-start.15) | collective-permute-done | bytes 131104 | tf_op jit(solution)/shard_map/ppermute | solution.py:23
  70.7 3.0 %collective-permute-done.16.refs_6_.refs_5_ = bf16[512,128]{1,0:T(8,128)(2,1)S(1)} collective-permute-done((bf16[512,128]{1,0:T(8,128)(2,1)S(1)}, bf16[512,128]{1,0:T(8,128)(2,1)S(1)}, u32[]{:S(2)}, u32[]{:S(2)}) %collective-permute-start.16) | collective-permute-done | bytes 131104 | tf_op jit(solution)/shard_map/ppermute | solution.py:23
  73.7 1.9 %backward.2 = (bf16[5120,128]{1,0:T(8,128)(2,1)S(1)}, bf16[5120,128]{1,0:T(8,128)(2,1)S(1)}) custom-call(bf16[2064,128]{1,0:T(8,128)(2,1)S(1)} %collective-permute-done.2.refs_10_.refs_0_, bf16[2064,128]{1,0:T(8,128)(2,1)S(1)} %collective-permute-done.1.refs_0_.refs_1_, bf16[2064,128]{1,0:T(8,128)(2,1)S(1)} %collective-permute-done.3.refs_1_.refs_2_, ...), custom_call_target="tpu_custom_call" | custom-call | flops 134217728 | bytes 5255168 | tf_op jit(solution)/shard_map/backward/pallas_call | solution.py:360
  75.6 2.5 %collective-permute-start.17 = (bf16[5120,128]{1,0:T(8,128)(2,1)S(1)}, bf16[5120,128]{1,0:T(8,128)(2,1)S(1)}, u32[]{:S(2)}, u32[]{:S(2)}) collective-permute-start(bf16[5120,128]{1,0:T(8,128)(2,1)S(1)} %get-tuple-element.59), channel_id=1, source_target_pairs={{0,4},{4,0},{8,12},{12,8},{16,20},{20,16},{24,28},{28,24},{1,5},{5... | collective-permute-start | bytes 3932168 | tf_op jit(solution)/shard_map/ppermute | solution.py:23
  78.1 1.9 %backward.3 = (bf16[4096,128]{1,0:T(8,128)(2,1)S(1)}, bf16[4096,128]{1,0:T(8,128)(2,1)S(1)}) custom-call(bf16[2064,128]{1,0:T(8,128)(2,1)S(1)} %copy-done.1, bf16[2064,128]{1,0:T(8,128)(2,1)S(1)} %collective-permute-done.refs_9_.refs_1_, bf16[512,128]{1,0:T(8,128)(2,1)S(1)} %get-tuple-element.51.refs_3_.refs_2_, ...), custom_call_target="tpu_custom_call" | custom-call | flops 134217728 | bytes 3678208 | tf_op jit(solution)/shard_map/backward/pallas_call | solution.py:360
  80.0 0.1 collective-permute-start.21
  80.1 0.7 collective-permute-done.17.refs_1_
  80.8 0.3 pair_sum.2
  81.1 1.0 collective-permute-start.18
  82.0 1.5 %collective-permute-start.19 = (bf16[1280,128]{1,0:T(8,128)(2,1)S(1)}, bf16[1280,128]{1,0:T(8,128)(2,1)S(1)}, u32[]{:S(2)}, u32[]{:S(2)}) collective-permute-start(bf16[1280,128]{1,0:T(8,128)(2,1)S(1)} %get-tuple-element.63), channel_id=1, source_target_pairs={{0,16},{4,20},{8,24},{12,28},{16,0},{20,4},{24,8},{28,12},{1,17},{... | collective-permute-start | bytes 983048 | tf_op jit(solution)/shard_map/ppermute | solution.py:23
  83.6 0.9 collective-permute-start.20
  84.5 0.2 pair_sum.3
  84.7 0.3 collective-permute-start.25
  85.1 1.4 %collective-permute-start.26 = (bf16[1024,128]{1,0:T(8,128)(2,1)S(1)}, bf16[1024,128]{1,0:T(8,128)(2,1)S(1)}, u32[]{:S(2)}, u32[]{:S(2)}) collective-permute-start(bf16[1024,128]{1,0:T(8,128)(2,1)S(1)} %get-tuple-element.71), channel_id=1, source_target_pairs={{0,16},{4,20},{8,24},{12,28},{16,0},{20,4},{24,8},{28,12},{1,17},{... | collective-permute-start | bytes 786440 | tf_op jit(solution)/shard_map/ppermute | solution.py:23
  86.5 3.5 %collective-permute-done.18.refs_1_ = bf16[1280,128]{1,0:T(8,128)(2,1)S(1)} collective-permute-done((bf16[1280,128]{1,0:T(8,128)(2,1)S(1)}, bf16[1280,128]{1,0:T(8,128)(2,1)S(1)}, u32[]{:S(2)}, u32[]{:S(2)}) %collective-permute-start.18) | collective-permute-done | bytes 327712 | tf_op jit(solution)/shard_map/ppermute | solution.py:23
  90.1 2.1 %collective-permute-start.27 = (bf16[1024,128]{1,0:T(8,128)(2,1)S(1)}, bf16[1024,128]{1,0:T(8,128)(2,1)S(1)}, u32[]{:S(2)}, u32[]{:S(2)}) collective-permute-start(bf16[1024,128]{1,0:T(8,128)(2,1)S(1)} %get-tuple-element.72), channel_id=1, source_target_pairs={{0,24},{4,28},{8,16},{12,20},{16,8},{20,12},{24,0},{28,4},{1,25},{... | collective-permute-start | bytes 786440 | tf_op jit(solution)/shard_map/ppermute | solution.py:23
  92.2 6.8 %collective-permute-done.20.refs_3_ = bf16[1280,128]{1,0:T(8,128)(2,1)S(1)} collective-permute-done((bf16[1280,128]{1,0:T(8,128)(2,1)S(1)}, bf16[1280,128]{1,0:T(8,128)(2,1)S(1)}, u32[]{:S(2)}, u32[]{:S(2)}) %collective-permute-start.20) | collective-permute-done | bytes 327712 | tf_op jit(solution)/shard_map/ppermute | solution.py:23
  99.0 0.2 plane_sum.2
  99.2 0.1 collective-permute-start.23
  99.3 0.5 collective-permute-start.24
  99.7 3.0 %collective-permute-done.25.refs_1_ = bf16[1024,128]{1,0:T(8,128)(2,1)S(1)} collective-permute-done((bf16[1024,128]{1,0:T(8,128)(2,1)S(1)}, bf16[1024,128]{1,0:T(8,128)(2,1)S(1)}, u32[]{:S(2)}, u32[]{:S(2)}) %collective-permute-start.25) | collective-permute-done | bytes 262176 | tf_op jit(solution)/shard_map/ppermute | solution.py:23
  102.8 0.6 collective-permute-done.26.refs_2_
  103.4 6.9 %collective-permute-done.27.refs_3_ = bf16[1024,128]{1,0:T(8,128)(2,1)S(1)} collective-permute-done((bf16[1024,128]{1,0:T(8,128)(2,1)S(1)}, bf16[1024,128]{1,0:T(8,128)(2,1)S(1)}, u32[]{:S(2)}, u32[]{:S(2)}) %collective-permute-start.27) | collective-permute-done | bytes 262176 | tf_op jit(solution)/shard_map/ppermute | solution.py:23
  110.3 0.1 plane_sum.3
  110.4 0.1 collective-permute-start.31
  110.5 0.8 collective-permute-done.23.refs_2_
  111.3 4.5 %collective-permute-done.24.refs_3_ = bf16[768,128]{1,0:T(8,128)(2,1)S(1)} collective-permute-done((bf16[768,128]{1,0:T(8,128)(2,1)S(1)}, bf16[768,128]{1,0:T(8,128)(2,1)S(1)}, u32[]{:S(2)}, u32[]{:S(2)}) %collective-permute-start.24) | collective-permute-done | bytes 196640 | tf_op jit(solution)/shard_map/ppermute | solution.py:23
  115.8 1.5 %collective-permute-start.28 = (bf16[256,128]{1,0:T(8,128)(2,1)S(1)}, bf16[256,128]{1,0:T(8,128)(2,1)S(1)}, u32[]{:S(2)}, u32[]{:S(2)}) collective-permute-start(bf16[256,128]{1,0:T(8,128)(2,1)S(1)} %weight_total.1.refs_0_), channel_id=1, source_target_pairs={{0,8},{4,12},{8,0},{12,4},{16,24},{20,28},{24,16},{28,20},{1,9},{5... | collective-permute-start | bytes 196616 | tf_op jit(solution)/shard_map/ppermute | solution.py:23
  117.3 1.3 collective-permute-start.30
  118.5 0.5 collective-permute-done.28.refs_1_
  119.0 1.4 %collective-permute-done.29.refs_2_ = bf16[256,128]{1,0:T(8,128)(2,1)S(1)} collective-permute-done((bf16[256,128]{1,0:T(8,128)(2,1)S(1)}, bf16[256,128]{1,0:T(8,128)(2,1)S(1)}, u32[]{:S(2)}, u32[]{:S(2)}) %collective-permute-start.29) | collective-permute-done | bytes 65568 | tf_op jit(solution)/shard_map/ppermute | solution.py:23
  120.4 1.3 %collective-permute-done.30.refs_3_ = bf16[256,128]{1,0:T(8,128)(2,1)S(1)} collective-permute-done((bf16[256,128]{1,0:T(8,128)(2,1)S(1)}, bf16[256,128]{1,0:T(8,128)(2,1)S(1)}, u32[]{:S(2)}, u32[]{:S(2)}) %collective-permute-start.30) | collective-permute-done | bytes 65568 | tf_op jit(solution)/shard_map/ppermute | solution.py:23
  121.7 3.4 %collective-permute-start.32 = (bf16[256,512]{1,0:T(8,128)(2,1)S(1)}, bf16[256,512]{1,0:T(8,128)(2,1)S(1)}, u32[]{:S(2)}, u32[]{:S(2)}) collective-permute-start(bf16[256,512]{1,0:T(8,128)(2,1)S(1)} %weight_half.1.refs_0_), channel_id=1, source_target_pairs={{0,4},{4,0},{8,12},{12,8},{16,20},{20,16},{24,28},{28,24},{1,5},{5... | collective-permute-start | bytes 786440 | tf_op jit(solution)/shard_map/ppermute | solution.py:23
  125.2 0.9 join.1
  126.1 0.2 collective-permute-done.32.refs_1_
  126.3 1.1 weight_whole.1
  (33 shorter events, 0.4 us)
Async XLA Ops:
  1.3 36.1 %copy-start.2 = (bf16[512,512]{1,0:T(8,128)(2,1)S(1)}, bf16[512,512]{1,0:T(8,128)(2,1)}, u32[]{:S(2)}) copy-start(bf16[512,512]{1,0:T(8,128)(2,1)} %refs_11_.1) | copy-start | bytes 1572868
  1.3 36.1 %copy-start.4 = (bf16[8,512]{1,0:T(8,128)(2,1)S(1)}, bf16[8,512]{1,0:T(8,128)(2,1)}, u32[]{:S(2)}) copy-start(bf16[8,512]{1,0:T(8,128)(2,1)} %refs_12_.1) | copy-start | bytes 24580
  3.6 22.6 %collective-permute-start = (bf16[2064,128]{1,0:T(8,128)(2,1)}, bf16[2064,128]{1,0:T(8,128)(2,1)S(1)}, u32[]{:S(2)}, u32[]{:S(2)}) collective-permute-start(bf16[2064,128]{1,0:T(8,128)(2,1)} %get-tuple-element.40.refs_8_.refs_0_), channel_id=1, source_target_pairs={{0,1},{1,0},{2,3},{3,2},{4,5},{5,4},{6,7},{7,6},{8,9},{9,8},{10,11... | collective-permute-start | bytes 1585160 | tf_op jit(solution)/shard_map/ppermute | solution.py:23
  3.7 27.1 %collective-permute-start.2 = (bf16[2064,128]{1,0:T(8,128)(2,1)}, bf16[2064,128]{1,0:T(8,128)(2,1)S(1)}, u32[]{:S(2)}, u32[]{:S(2)}) collective-permute-start(bf16[2064,128]{1,0:T(8,128)(2,1)} %get-tuple-element.40.refs_8_.refs_0_), channel_id=1, source_target_pairs={{0,2},{1,3},{2,0},{3,1},{4,6},{5,7},{6,4},{7,5},{8,10},{9,11},{10,... | collective-permute-start | bytes 1585160 | tf_op jit(solution)/shard_map/ppermute | solution.py:23
  6.1 21.3 %collective-permute-start.6 = (bf16[2048,128]{1,0:T(8,128)(2,1)}, bf16[2048,128]{1,0:T(8,128)(2,1)S(1)}, u32[]{:S(2)}, u32[]{:S(2)}) collective-permute-start(bf16[2048,128]{1,0:T(8,128)(2,1)} %get-tuple-element.41.refs_0_), channel_id=1, source_target_pairs={{0,24},{4,28},{8,16},{12,20},{16,8},{20,12},{24,0},{28,4},{1,25},{... | collective-permute-start | bytes 1572872 | tf_op jit(solution)/shard_map/ppermute | solution.py:23
  8.3 23.8 %collective-permute-start.4 = (bf16[2048,128]{1,0:T(8,128)(2,1)}, bf16[2048,128]{1,0:T(8,128)(2,1)S(1)}, u32[]{:S(2)}, u32[]{:S(2)}) collective-permute-start(bf16[2048,128]{1,0:T(8,128)(2,1)} %get-tuple-element.41.refs_0_), channel_id=1, source_target_pairs={{0,8},{4,12},{8,0},{12,4},{16,24},{20,28},{24,16},{28,20},{1,9},{5... | collective-permute-start | bytes 1572872 | tf_op jit(solution)/shard_map/ppermute | solution.py:23
  8.6 25.8 %collective-permute-start.5 = (bf16[2048,128]{1,0:T(8,128)(2,1)}, bf16[2048,128]{1,0:T(8,128)(2,1)S(1)}, u32[]{:S(2)}, u32[]{:S(2)}) collective-permute-start(bf16[2048,128]{1,0:T(8,128)(2,1)} %get-tuple-element.41.refs_0_), channel_id=1, source_target_pairs={{0,16},{4,20},{8,24},{12,28},{16,0},{20,4},{24,8},{28,12},{1,17},{... | collective-permute-start | bytes 1572872 | tf_op jit(solution)/shard_map/ppermute | solution.py:23
  26.2 8.3 %collective-permute-start.7 = (bf16[2048,128]{1,0:T(8,128)(2,1)}, bf16[2048,128]{1,0:T(8,128)(2,1)S(1)}, u32[]{:S(2)}, u32[]{:S(2)}) collective-permute-start(bf16[2048,128]{1,0:T(8,128)(2,1)} %get-tuple-element.41.refs_0_), channel_id=1, source_target_pairs={{0,4},{4,0},{8,12},{12,8},{16,20},{20,16},{24,28},{28,24},{1,5},{5... | collective-permute-start | bytes 1572872 | tf_op jit(solution)/shard_map/ppermute | solution.py:23
  27.4 15.8 %collective-permute-start.1 = (bf16[2064,128]{1,0:T(8,128)(2,1)}, bf16[2064,128]{1,0:T(8,128)(2,1)S(1)}, u32[]{:S(2)}, u32[]{:S(2)}) collective-permute-start(bf16[2064,128]{1,0:T(8,128)(2,1)} %get-tuple-element.40.refs_8_.refs_0_), channel_id=1, source_target_pairs={{1,2},{2,1},{5,6},{6,5},{9,10},{10,9},{13,14},{14,13},{17,18},{18,... | collective-permute-start | bytes 1585160 | tf_op jit(solution)/shard_map/ppermute | solution.py:380
  30.8 12.4 %collective-permute-start.3 = (bf16[2064,128]{1,0:T(8,128)(2,1)S(1)}, bf16[2064,128]{1,0:T(8,128)(2,1)S(1)}, u32[]{:S(2)}, u32[]{:S(2)}) collective-permute-start(bf16[2064,128]{1,0:T(8,128)(2,1)S(1)} %collective-permute-done.2.refs_10_.refs_0_), channel_id=1, source_target_pairs={{2,3},{1,0},{6,7},{5,4},{10,11},{9,8},{14,15},{13,12},{18,19},{17,... | collective-permute-start | bytes 1585160 | tf_op jit(solution)/shard_map/ppermute | solution.py:378
  32.2 3.7 %collective-permute-start.10 = (bf16[2048,128]{1,0:T(8,128)(2,1)S(1)}, bf16[2048,128]{1,0:T(8,128)(2,1)S(1)}, u32[]{:S(2)}, u32[]{:S(2)}) collective-permute-start(bf16[2048,128]{1,0:T(8,128)(2,1)S(1)} %collective-permute-done.6.refs_3_), channel_id=1, source_target_pairs={{0,4},{4,0},{8,12},{12,8},{16,20},{20,16},{24,28},{28,24},{1,5},{5... | collective-permute-start | bytes 1572872 | tf_op jit(solution)/shard_map/ppermute | solution.py:23
  34.4 2.3 %collective-permute-start.8 = (bf16[2048,128]{1,0:T(8,128)(2,1)S(1)}, bf16[2048,128]{1,0:T(8,128)(2,1)S(1)}, u32[]{:S(2)}, u32[]{:S(2)}) collective-permute-start(bf16[2048,128]{1,0:T(8,128)(2,1)S(1)} %collective-permute-done.4.refs_1_), channel_id=1, source_target_pairs={{0,4},{4,0},{8,12},{12,8},{16,20},{20,16},{24,28},{28,24},{1,5},{5... | collective-permute-start | bytes 1572872 | tf_op jit(solution)/shard_map/ppermute | solution.py:23
  34.4 2.9 %collective-permute-start.9 = (bf16[2048,128]{1,0:T(8,128)(2,1)S(1)}, bf16[2048,128]{1,0:T(8,128)(2,1)S(1)}, u32[]{:S(2)}, u32[]{:S(2)}) collective-permute-start(bf16[2048,128]{1,0:T(8,128)(2,1)S(1)} %collective-permute-done.5.refs_2_), channel_id=1, source_target_pairs={{0,4},{4,0},{8,12},{12,8},{16,20},{20,16},{24,28},{28,24},{1,5},{5... | collective-permute-start | bytes 1572872 | tf_op jit(solution)/shard_map/ppermute | solution.py:23
  37.4 1.0 copy-start
  38.4 1.0 copy-start.3
  43.2 4.5 %copy-start.5 = (s32[2048]{0:T(1024)S(1)}, s32[2048]{0:T(1024)}, u32[]{:S(2)}) copy-start(s32[2048]{0:T(1024)} %param.12) | copy-start | bytes 24580
  43.2 4.5 %copy-start.6 = (s32[2048]{0:T(1024)S(1)}, s32[2048]{0:T(1024)}, u32[]{:S(2)}) copy-start(s32[2048]{0:T(1024)} %param.13) | copy-start | bytes 24580
  44.9 4.1 %collective-permute-start.11 = (bf16[512,128]{1,0:T(8,128)(2,1)}, bf16[512,128]{1,0:T(8,128)(2,1)S(1)}, u32[]{:S(2)}, u32[]{:S(2)}) collective-permute-start(bf16[512,128]{1,0:T(8,128)(2,1)} %get-tuple-element.45), channel_id=1, source_target_pairs={{0,1},{1,0},{2,3},{3,2},{4,5},{5,4},{6,7},{7,6},{8,9},{9,8},{10,11... | collective-permute-start | bytes 393224 | tf_op jit(solution)/shard_map/ppermute | solution.py:23
  45.4 6.8 %collective-permute-start.12 = (bf16[512,128]{1,0:T(8,128)(2,1)S(1)}, bf16[512,128]{1,0:T(8,128)(2,1)S(1)}, u32[]{:S(2)}, u32[]{:S(2)}) collective-permute-start(bf16[512,128]{1,0:T(8,128)(2,1)S(1)} %get-tuple-element.46), channel_id=1, source_target_pairs={{0,2},{1,3},{2,0},{3,1},{4,6},{5,7},{6,4},{7,5},{8,10},{9,11},{10,... | collective-permute-start | bytes 393224 | tf_op jit(solution)/shard_map/ppermute | solution.py:23
  47.6 10.5 %collective-permute-start.13 = (bf16[512,128]{1,0:T(8,128)(2,1)S(1)}, bf16[512,128]{1,0:T(8,128)(2,1)S(1)}, u32[]{:S(2)}, u32[]{:S(2)}) collective-permute-start(bf16[512,128]{1,0:T(8,128)(2,1)S(1)} %get-tuple-element.47), channel_id=1, source_target_pairs={{0,3},{1,2},{2,1},{3,0},{4,7},{5,6},{6,5},{7,4},{8,11},{9,10},{10,... | collective-permute-start | bytes 393224 | tf_op jit(solution)/shard_map/ppermute | solution.py:23
  59.6 4.0 %collective-permute-start.14 = (bf16[512,128]{1,0:T(8,128)(2,1)S(1)}, bf16[512,128]{1,0:T(8,128)(2,1)S(1)}, u32[]{:S(2)}, u32[]{:S(2)}) collective-permute-start(bf16[512,128]{1,0:T(8,128)(2,1)S(1)} %get-tuple-element.52), channel_id=1, source_target_pairs={{0,1},{1,0},{2,3},{3,2},{4,5},{5,4},{6,7},{7,6},{8,9},{9,8},{10,11... | collective-permute-start | bytes 393224 | tf_op jit(solution)/shard_map/ppermute | solution.py:23
  59.7 11.0 %collective-permute-start.15 = (bf16[512,128]{1,0:T(8,128)(2,1)S(1)}, bf16[512,128]{1,0:T(8,128)(2,1)S(1)}, u32[]{:S(2)}, u32[]{:S(2)}) collective-permute-start(bf16[512,128]{1,0:T(8,128)(2,1)S(1)} %get-tuple-element.53), channel_id=1, source_target_pairs={{0,2},{1,3},{2,0},{3,1},{4,6},{5,7},{6,4},{7,5},{8,10},{9,11},{10,... | collective-permute-start | bytes 393224 | tf_op jit(solution)/shard_map/ppermute | solution.py:23
  63.0 10.7 %collective-permute-start.16 = (bf16[512,128]{1,0:T(8,128)(2,1)S(1)}, bf16[512,128]{1,0:T(8,128)(2,1)S(1)}, u32[]{:S(2)}, u32[]{:S(2)}) collective-permute-start(bf16[512,128]{1,0:T(8,128)(2,1)S(1)} %get-tuple-element.54), channel_id=1, source_target_pairs={{0,3},{1,2},{2,1},{3,0},{4,7},{5,6},{6,5},{7,4},{8,11},{9,10},{10,... | collective-permute-start | bytes 393224 | tf_op jit(solution)/shard_map/ppermute | solution.py:23
  73.7 4.5 %copy-start.1 = (bf16[2064,128]{1,0:T(8,128)(2,1)S(1)}, bf16[2064,128]{1,0:T(8,128)(2,1)}, u32[]{:S(2)}) copy-start(bf16[2064,128]{1,0:T(8,128)(2,1)} %get-tuple-element.40.refs_8_.refs_0_) | copy-start | bytes 1585156
  75.6 5.2 %collective-permute-start.17 = (bf16[5120,128]{1,0:T(8,128)(2,1)S(1)}, bf16[5120,128]{1,0:T(8,128)(2,1)S(1)}, u32[]{:S(2)}, u32[]{:S(2)}) collective-permute-start(bf16[5120,128]{1,0:T(8,128)(2,1)S(1)} %get-tuple-element.59), channel_id=1, source_target_pairs={{0,4},{4,0},{8,12},{12,8},{16,20},{20,16},{24,28},{28,24},{1,5},{5... | collective-permute-start | bytes 3932168 | tf_op jit(solution)/shard_map/ppermute | solution.py:23
  80.0 4.5 %collective-permute-start.21 = (bf16[4096,128]{1,0:T(8,128)(2,1)S(1)}, bf16[4096,128]{1,0:T(8,128)(2,1)S(1)}, u32[]{:S(2)}, u32[]{:S(2)}) collective-permute-start(bf16[4096,128]{1,0:T(8,128)(2,1)S(1)} %get-tuple-element.65), channel_id=1, source_target_pairs={{0,4},{4,0},{8,12},{12,8},{16,20},{20,16},{24,28},{28,24},{1,5},{5... | collective-permute-start | bytes 3145736 | tf_op jit(solution)/shard_map/ppermute | solution.py:23
  81.1 9.0 %collective-permute-start.18 = (bf16[1280,128]{1,0:T(8,128)(2,1)S(1)}, bf16[1280,128]{1,0:T(8,128)(2,1)S(1)}, u32[]{:S(2)}, u32[]{:S(2)}) collective-permute-start(bf16[1280,128]{1,0:T(8,128)(2,1)S(1)} %get-tuple-element.62), channel_id=1, source_target_pairs={{0,8},{4,12},{8,0},{12,4},{16,24},{20,28},{24,16},{28,20},{1,9},{5... | collective-permute-start | bytes 983048 | tf_op jit(solution)/shard_map/ppermute | solution.py:23
  82.0 10.2 %collective-permute-start.19 = (bf16[1280,128]{1,0:T(8,128)(2,1)S(1)}, bf16[1280,128]{1,0:T(8,128)(2,1)S(1)}, u32[]{:S(2)}, u32[]{:S(2)}) collective-permute-start(bf16[1280,128]{1,0:T(8,128)(2,1)S(1)} %get-tuple-element.63), channel_id=1, source_target_pairs={{0,16},{4,20},{8,24},{12,28},{16,0},{20,4},{24,8},{28,12},{1,17},{... | collective-permute-start | bytes 983048 | tf_op jit(solution)/shard_map/ppermute | solution.py:23
  83.6 15.5 %collective-permute-start.20 = (bf16[1280,128]{1,0:T(8,128)(2,1)S(1)}, bf16[1280,128]{1,0:T(8,128)(2,1)S(1)}, u32[]{:S(2)}, u32[]{:S(2)}) collective-permute-start(bf16[1280,128]{1,0:T(8,128)(2,1)S(1)} %get-tuple-element.64), channel_id=1, source_target_pairs={{0,24},{4,28},{8,16},{12,20},{16,8},{20,12},{24,0},{28,4},{1,25},{... | collective-permute-start | bytes 983048 | tf_op jit(solution)/shard_map/ppermute | solution.py:23
  84.7 18.0 %collective-permute-start.25 = (bf16[1024,128]{1,0:T(8,128)(2,1)S(1)}, bf16[1024,128]{1,0:T(8,128)(2,1)S(1)}, u32[]{:S(2)}, u32[]{:S(2)}) collective-permute-start(bf16[1024,128]{1,0:T(8,128)(2,1)S(1)} %get-tuple-element.70), channel_id=1, source_target_pairs={{0,8},{4,12},{8,0},{12,4},{16,24},{20,28},{24,16},{28,20},{1,9},{5... | collective-permute-start | bytes 786440 | tf_op jit(solution)/shard_map/ppermute | solution.py:23
  85.1 18.3 %collective-permute-start.26 = (bf16[1024,128]{1,0:T(8,128)(2,1)S(1)}, bf16[1024,128]{1,0:T(8,128)(2,1)S(1)}, u32[]{:S(2)}, u32[]{:S(2)}) collective-permute-start(bf16[1024,128]{1,0:T(8,128)(2,1)S(1)} %get-tuple-element.71), channel_id=1, source_target_pairs={{0,16},{4,20},{8,24},{12,28},{16,0},{20,4},{24,8},{28,12},{1,17},{... | collective-permute-start | bytes 786440 | tf_op jit(solution)/shard_map/ppermute | solution.py:23
  90.1 20.2 %collective-permute-start.27 = (bf16[1024,128]{1,0:T(8,128)(2,1)S(1)}, bf16[1024,128]{1,0:T(8,128)(2,1)S(1)}, u32[]{:S(2)}, u32[]{:S(2)}) collective-permute-start(bf16[1024,128]{1,0:T(8,128)(2,1)S(1)} %get-tuple-element.72), channel_id=1, source_target_pairs={{0,24},{4,28},{8,16},{12,20},{16,8},{20,12},{24,0},{28,4},{1,25},{... | collective-permute-start | bytes 786440 | tf_op jit(solution)/shard_map/ppermute | solution.py:23
  99.2 12.1 %collective-permute-start.23 = (bf16[768,128]{1,0:T(8,128)(2,1)S(1)}, bf16[768,128]{1,0:T(8,128)(2,1)S(1)}, u32[]{:S(2)}, u32[]{:S(2)}) collective-permute-start(bf16[768,128]{1,0:T(8,128)(2,1)S(1)} %get-tuple-element.68), channel_id=1, source_target_pairs={{0,2},{1,3},{2,0},{3,1},{4,6},{5,7},{6,4},{7,5},{8,10},{9,11},{10,... | collective-permute-start | bytes 589832 | tf_op jit(solution)/shard_map/ppermute | solution.py:23
  99.3 16.5 %collective-permute-start.24 = (bf16[768,128]{1,0:T(8,128)(2,1)S(1)}, bf16[768,128]{1,0:T(8,128)(2,1)S(1)}, u32[]{:S(2)}, u32[]{:S(2)}) collective-permute-start(bf16[768,128]{1,0:T(8,128)(2,1)S(1)} %get-tuple-element.69), channel_id=1, source_target_pairs={{0,3},{1,2},{2,1},{3,0},{4,7},{5,6},{6,5},{7,4},{8,11},{9,10},{10,... | collective-permute-start | bytes 589832 | tf_op jit(solution)/shard_map/ppermute | solution.py:23
  102.7 7.7 %collective-permute-start.22 = (bf16[256,128]{1,0:T(8,128)(2,1)S(1)}, bf16[256,128]{1,0:T(8,128)(2,1)S(1)}, u32[]{:S(2)}, u32[]{:S(2)}) collective-permute-start(bf16[256,128]{1,0:T(8,128)(2,1)S(1)} %get-tuple-element.67.refs_0_), channel_id=1, source_target_pairs={{0,1},{1,0},{2,3},{3,2},{4,5},{5,4},{6,7},{7,6},{8,9},{9,8},{10,11... | collective-permute-start | bytes 196616 | tf_op jit(solution)/shard_map/ppermute | solution.py:23
  110.4 8.1 %collective-permute-start.31 = (bf16[512,128]{1,0:T(8,128)(2,1)S(1)}, bf16[512,128]{1,0:T(8,128)(2,1)S(1)}, u32[]{:S(2)}, u32[]{:S(2)}) collective-permute-start(bf16[512,128]{1,0:T(8,128)(2,1)S(1)} %get-tuple-element.74), channel_id=1, source_target_pairs={{0,1},{1,0},{2,3},{3,2},{4,5},{5,4},{6,7},{7,6},{8,9},{9,8},{10,11... | collective-permute-start | bytes 393224 | tf_op jit(solution)/shard_map/ppermute | solution.py:23
  115.8 3.2 %collective-permute-start.28 = (bf16[256,128]{1,0:T(8,128)(2,1)S(1)}, bf16[256,128]{1,0:T(8,128)(2,1)S(1)}, u32[]{:S(2)}, u32[]{:S(2)}) collective-permute-start(bf16[256,128]{1,0:T(8,128)(2,1)S(1)} %weight_total.1.refs_0_), channel_id=1, source_target_pairs={{0,8},{4,12},{8,0},{12,4},{16,24},{20,28},{24,16},{28,20},{1,9},{5... | collective-permute-start | bytes 196616 | tf_op jit(solution)/shard_map/ppermute | solution.py:23
  117.3 3.1 %collective-permute-start.29 = (bf16[256,128]{1,0:T(8,128)(2,1)S(1)}, bf16[256,128]{1,0:T(8,128)(2,1)S(1)}, u32[]{:S(2)}, u32[]{:S(2)}) collective-permute-start(bf16[256,128]{1,0:T(8,128)(2,1)S(1)} %weight_total.1.refs_0_), channel_id=1, source_target_pairs={{0,16},{4,20},{8,24},{12,28},{16,0},{20,4},{24,8},{28,12},{1,17},{... | collective-permute-start | bytes 196616 | tf_op jit(solution)/shard_map/ppermute | solution.py:23
  117.3 4.4 %collective-permute-start.30 = (bf16[256,128]{1,0:T(8,128)(2,1)S(1)}, bf16[256,128]{1,0:T(8,128)(2,1)S(1)}, u32[]{:S(2)}, u32[]{:S(2)}) collective-permute-start(bf16[256,128]{1,0:T(8,128)(2,1)S(1)} %weight_total.1.refs_0_), channel_id=1, source_target_pairs={{0,24},{4,28},{8,16},{12,20},{16,8},{20,12},{24,0},{28,4},{1,25},{... | collective-permute-start | bytes 196616 | tf_op jit(solution)/shard_map/ppermute | solution.py:23
  121.7 4.6 %collective-permute-start.32 = (bf16[256,512]{1,0:T(8,128)(2,1)S(1)}, bf16[256,512]{1,0:T(8,128)(2,1)S(1)}, u32[]{:S(2)}, u32[]{:S(2)}) collective-permute-start(bf16[256,512]{1,0:T(8,128)(2,1)S(1)} %weight_half.1.refs_0_), channel_id=1, source_target_pairs={{0,4},{4,0},{8,12},{12,8},{16,20},{20,16},{24,28},{28,24},{1,5},{5... | collective-permute-start | bytes 786440 | tf_op jit(solution)/shard_map/ppermute | solution.py:23

commit v6 on v5

--- a/solution.py
+++ b/solution.py
@@ -230,21 +230,17 @@
     out[...] = tree(values).astype(out.dtype)
 
 
-def weight_half_kernel(chips, teams, place, *refs):
-    out = refs[chips]
+def whole_kernel(chips, teams, scale, place, *refs):
+    out = refs[2 * chips]
     rows = refs[0].shape[0] // teams
     width = refs[0].shape[1]
-    for d in range(chips):
-        held = pl.ds(pl.multiple_of((place[1] ^ d) * rows, rows), rows)
-        for t in range(teams):
-            out[held, t * width : (t + 1) * width] = refs[d][t * rows : (t + 1) * rows, :]
-
-
-def whole_kernel(scale, place, mine, taken, out):
-    rows = mine.shape[0]
-    for value, here in ((mine, place[2]), (taken, 1 - place[2])):
-        held = pl.ds(pl.multiple_of(here * rows, rows), rows)
-        out[held, :] = value[...].astype(jnp.float32) * scale
+    for side, pieces in ((place[2], refs[:chips]), (1 - place[2], refs[chips : 2 * chips])):
+        for d in range(chips):
+            start = (side * chips + (place[1] ^ d)) * rows
+            held = pl.ds(pl.multiple_of(start, rows), rows)
+            for t in range(teams):
+                value = pieces[d][t * rows : (t + 1) * rows, :].astype(jnp.float32)
+                out[held, t * width : (t + 1) * width] = value * scale
 
 
 def backward_kernel(chips, teams, slots, piece, chunk, riders, place, *refs):
@@ -606,26 +602,18 @@
         6 * MIB,
         after=sums[:1],
     )
-    (w_half,) = call(
-        functools.partial(weight_half_kernel, chips, teams),
-        "weight_half",
-        plane_total([w_total] * chips),
-        [vmem] * chips,
-        [shaped(half, width)],
+    w_near = plane_total([w_total] * chips)
+    w_far = [swap(value, "row", 1) for value in w_near]
+    (grad_weight,) = call(
+        functools.partial(whole_kernel, chips, teams, 1.0 / math.sqrt(nodes)),
+        "weight_whole",
+        [*w_near, *w_far],
+        [vmem] * (2 * chips),
+        [shaped(width, width, kind=f32)],
         [],
         half * width,
         6 * MIB,
         after=[slices[d] for d in chunks[1][1:]],
-    )
-    (grad_weight,) = call(
-        functools.partial(whole_kernel, 1.0 / math.sqrt(nodes)),
-        "weight_whole",
-        [w_half, swap(w_half, "row", 1)],
-        [vmem] * 2,
-        [shaped(width, width, kind=f32)],
-        [],
-        half * width,
-        6 * MIB,
     )
     (grad_features,) = call(
         functools.partial(join_kernel, teams),

time: 128 us -> 127 us (level)
  waiting for transfers between devices: 72.1 us -> 69.3 us
  starting transfers between devices: 36.7 us -> 38.9 us
    ppermute x31 -> x34, waiting for transfers between devices: 70.7 us -> 68 us  [swap(): return lax.ppermute(value, axis, [(i, i ^ flip) for i in range(size)])]
    ppermute x31 -> x34, starting transfers between devices: 32 us -> 34.1 us  [swap(): return lax.ppermute(value, axis, [(i, i ^ flip) for i in range(size)])]
    pallas_call x15 -> x14, Pallas kernels: 15 us -> 15.3 us  [call(): pl.pallas_call(body, name=name, in_specs=specs, out_specs=[pl.BlockSpec(m...]
  transfers between devices with their start and end apart: 33 -> 36, of which waited for: 22 -> 18; matrix products, arithmetic and copies ran while one was open for 0% -> 0% of each run, Pallas kernels for 5% -> 5%
where the time goes in v6:
time: 127 us
  waiting for transfers between devices  69.3 us (55%)
  starting transfers between devices  38.9 us (31%)
  Pallas kernels  15.3 us (12%)
  local copies, waits for them, and re-layouts  2.12 us (2%)
  between operations  1.49 us (1%)
    ppermute x34, waiting for transfers between devices, swap(): return lax.ppermute(value, axis, [(i, i ^ flip) for i in range(size)])  68 us
    ppermute x34, starting transfers between devices, swap(): return lax.ppermute(value, axis, [(i, i ^ flip) for i in range(size)])  34.1 us
    pallas_call x14, Pallas kernels, call(): pl.pallas_call(body, name=name, in_specs=specs, out_specs=[pl.BlockSpec(m...  15.3 us
    ppermute x1, starting transfers between devices, gather_lists(): middle = lax.ppermute(held, 'team', [(1, 2), (2, 1)])  3.38 us
  transfers between devices with their start and end apart: 36, of which 18 were waited for; matrix products, arithmetic and copies ran while one was open for 0% of the time, Pallas kernels for 5%

profile of v6, /device:TPU:9, one launch (start us, length us, event | category | flops | bytes accessed | tf_op | source)
XLA Modules:
  0.0 127.1 jit_solution(10350281951427655474)
XLA Ops:
  1.3 2.3 %prepare.1 = (bf16[2064,128]{1,0:T(8,128)(2,1)}, bf16[2048,128]{1,0:T(8,128)(2,1)}) custom-call(bf16[2048,128]{1,0:T(8,128)(2,1)} %bitcast.5, s32[1,16]{1,0:T(1,128)} %bitcast.6, s32[1,16]{1,0:T(1,128)} %bitcast.7, s32[1,1]{1,0:T(1,128)S(6)} %copy.12.refs_3_, bf16[2048,512]{1,0:T(8,128)(2,1)} %refs_4_.1), custom_call_target="tpu_custom_call" | custom-call | tf_op jit(solution)/shard_map/prepare/pallas_call | solution.py:356
  3.7 2.5 %collective-permute-start.2 = (bf16[2064,128]{1,0:T(8,128)(2,1)}, bf16[2064,128]{1,0:T(8,128)(2,1)S(1)}, u32[]{:S(2)}, u32[]{:S(2)}) collective-permute-start(bf16[2064,128]{1,0:T(8,128)(2,1)} %get-tuple-element.40.refs_8_.refs_0_), channel_id=1, source_target_pairs={{0,2},{1,3},{2,0},{3,1},{4,6},{5,7},{6,4},{7,5},{8,10},{9,11},{10,... | collective-permute-start | bytes 1585160 | tf_op jit(solution)/shard_map/ppermute | solution.py:23
  6.1 2.2 %collective-permute-start.6 = (bf16[2048,128]{1,0:T(8,128)(2,1)}, bf16[2048,128]{1,0:T(8,128)(2,1)S(1)}, u32[]{:S(2)}, u32[]{:S(2)}) collective-permute-start(bf16[2048,128]{1,0:T(8,128)(2,1)} %get-tuple-element.41.refs_0_), channel_id=1, source_target_pairs={{0,24},{4,28},{8,16},{12,20},{16,8},{20,12},{24,0},{28,4},{1,25},{... | collective-permute-start | bytes 1572872 | tf_op jit(solution)/shard_map/ppermute | solution.py:23
  8.3 0.3 collective-permute-start.4
  8.6 0.2 collective-permute-start.5
  8.8 17.4 %collective-permute-done.refs_9_.refs_1_ = bf16[2064,128]{1,0:T(8,128)(2,1)S(1)} collective-permute-done((bf16[2064,128]{1,0:T(8,128)(2,1)}, bf16[2064,128]{1,0:T(8,128)(2,1)S(1)}, u32[]{:S(2)}, u32[]{:S(2)}) %collective-permute-start) | collective-permute-done | bytes 528416 | tf_op jit(solution)/shard_map/ppermute | solution.py:23
  26.2 1.2 collective-permute-start.7
  27.4 3.4 %collective-permute-start.1 = (bf16[2064,128]{1,0:T(8,128)(2,1)}, bf16[2064,128]{1,0:T(8,128)(2,1)S(1)}, u32[]{:S(2)}, u32[]{:S(2)}) collective-permute-start(bf16[2064,128]{1,0:T(8,128)(2,1)} %get-tuple-element.40.refs_8_.refs_0_), channel_id=1, source_target_pairs={{1,2},{2,1},{5,6},{6,5},{9,10},{10,9},{13,14},{14,13},{17,18},{18,... | collective-permute-start | bytes 1585160 | tf_op jit(solution)/shard_map/ppermute | solution.py:376
  30.8 1.3 %collective-permute-start.3 = (bf16[2064,128]{1,0:T(8,128)(2,1)S(1)}, bf16[2064,128]{1,0:T(8,128)(2,1)S(1)}, u32[]{:S(2)}, u32[]{:S(2)}) collective-permute-start(bf16[2064,128]{1,0:T(8,128)(2,1)S(1)} %collective-permute-done.2.refs_10_.refs_0_), channel_id=1, source_target_pairs={{2,3},{1,0},{6,7},{5,4},{10,11},{9,8},{14,15},{13,12},{18,19},{17,... | collective-permute-start | bytes 1585160 | tf_op jit(solution)/shard_map/ppermute | solution.py:374
  32.2 2.2 %collective-permute-start.10 = (bf16[2048,128]{1,0:T(8,128)(2,1)S(1)}, bf16[2048,128]{1,0:T(8,128)(2,1)S(1)}, u32[]{:S(2)}, u32[]{:S(2)}) collective-permute-start(bf16[2048,128]{1,0:T(8,128)(2,1)S(1)} %collective-permute-done.6.refs_3_), channel_id=1, source_target_pairs={{0,4},{4,0},{8,12},{12,8},{16,20},{20,16},{24,28},{28,24},{1,5},{5... | collective-permute-start | bytes 1572872 | tf_op jit(solution)/shard_map/ppermute | solution.py:23
  34.4 0.1 collective-permute-start.8
  34.4 0.4 collective-permute-start.9
  34.9 1.0 collective-permute-done.10.refs_7_
  35.9 0.7 collective-permute-done.8.refs_5_
  36.6 0.7 collective-permute-done.9.refs_6_
  37.4 1.0 copy-done
  38.4 1.0 copy-done.3
  39.5 2.5 %early_products.1 = (f32[2048,128]{1,0:T(8,128)S(1)}, bf16[4096,128]{1,0:T(8,128)(2,1)S(1)}, bf16[512,512]{1,0:T(8,128)(2,1)S(1)}, bf16[8,512]{1,0:T(8,128)(2,1)S(1)}) custom-call(bf16[2048,128]{1,0:T(8,128)(2,1)S(1)} %copy-done.3, bf16[2048,128]{1,0:T(8,128)(2,1)S(1)} %collective-permute-done.4.refs_1_, ...), custom_call_target="tpu_custom_call" | custom-call | tf_op jit(solution)/shard_map/early_products/pallas_call | solution.py:356
  41.9 1.3 collective-permute-done.1.refs_0_.refs_1_
  43.2 1.7 %late_products.1 = (bf16[512,128]{1,0:T(8,128)(2,1)S(1)}, bf16[512,128]{1,0:T(8,128)(2,1)}, bf16[512,128]{1,0:T(8,128)(2,1)S(1)}, bf16[512,128]{1,0:T(8,128)(2,1)S(1)}) custom-call(bf16[2064,128]{1,0:T(8,128)(2,1)S(1)} %collective-permute-done.1.refs_0_.refs_1_, bf16[2064,128]{1,0:T(8,128)(2,1)S(1)} %collective-permute-done.3.refs_1_.refs_2_, ...), custom_call_target="tpu_custom_call" | custom-call | flops 67108864 | bytes 3678208 | tf_op jit(solution)/shard_map/late_products/pallas_call | solution.py:356
  44.9 0.6 collective-permute-start.11
  45.6 1.9 %collective-permute-start.12 = (bf16[512,128]{1,0:T(8,128)(2,1)S(1)}, bf16[512,128]{1,0:T(8,128)(2,1)S(1)}, u32[]{:S(2)}, u32[]{:S(2)}) collective-permute-start(bf16[512,128]{1,0:T(8,128)(2,1)S(1)} %get-tuple-element.46), channel_id=1, source_target_pairs={{0,2},{1,3},{2,0},{3,1},{4,6},{5,7},{6,4},{7,5},{8,10},{9,11},{10,... | collective-permute-start | bytes 393224 | tf_op jit(solution)/shard_map/ppermute | solution.py:23
  47.4 0.2 collective-permute-start.13
  47.7 1.4 %collective-permute-done.11.refs_1_ = bf16[512,128]{1,0:T(8,128)(2,1)S(1)} collective-permute-done((bf16[512,128]{1,0:T(8,128)(2,1)}, bf16[512,128]{1,0:T(8,128)(2,1)S(1)}, u32[]{:S(2)}, u32[]{:S(2)}) %collective-permute-start.11) | collective-permute-done | bytes 131104 | tf_op jit(solution)/shard_map/ppermute | solution.py:23
  49.0 2.5 %collective-permute-done.12.refs_2_ = bf16[512,128]{1,0:T(8,128)(2,1)S(1)} collective-permute-done((bf16[512,128]{1,0:T(8,128)(2,1)S(1)}, bf16[512,128]{1,0:T(8,128)(2,1)S(1)}, u32[]{:S(2)}, u32[]{:S(2)}) %collective-permute-start.12) | collective-permute-done | bytes 131104 | tf_op jit(solution)/shard_map/ppermute | solution.py:23
  51.6 6.6 %collective-permute-done.13.refs_3_ = bf16[512,128]{1,0:T(8,128)(2,1)S(1)} collective-permute-done((bf16[512,128]{1,0:T(8,128)(2,1)S(1)}, bf16[512,128]{1,0:T(8,128)(2,1)S(1)}, u32[]{:S(2)}, u32[]{:S(2)}) %collective-permute-start.13) | collective-permute-done | bytes 131104 | tf_op jit(solution)/shard_map/ppermute | solution.py:23
  58.2 1.4 %layer.1 = (bf16[512,512]{1,0:T(8,128)(2,1)}, bf16[512,512]{1,0:T(8,128)(2,1)S(1)}, bf16[512,128]{1,0:T(8,128)(2,1)S(1)}, bf16[512,128]{1,0:T(8,128)(2,1)S(1)}, ...) custom-call(bf16[512,128]{1,0:T(8,128)(2,1)S(1)} %get-tuple-element.44.refs_0_, ...), custom_call_target="tpu_custom_call" | custom-call | flops 536870912 | bytes 2646016 | tf_op jit(solution)/shard_map/layer/pallas_call | solution.py:356
  59.7 2.2 %collective-permute-start.15 = (bf16[512,128]{1,0:T(8,128)(2,1)S(1)}, bf16[512,128]{1,0:T(8,128)(2,1)S(1)}, u32[]{:S(2)}, u32[]{:S(2)}) collective-permute-start(bf16[512,128]{1,0:T(8,128)(2,1)S(1)} %get-tuple-element.53), channel_id=1, source_target_pairs={{0,2},{1,3},{2,0},{3,1},{4,6},{5,7},{6,4},{7,5},{8,10},{9,11},{10,... | collective-permute-start | bytes 393224 | tf_op jit(solution)/shard_map/ppermute | solution.py:23
  61.9 0.5 collective-permute-start.16
  62.4 0.6 weight_term.1
  62.9 0.6 collective-permute-done.14.refs_4_.refs_3_
  63.5 2.5 %collective-permute-done.15.refs_5_.refs_4_ = bf16[512,128]{1,0:T(8,128)(2,1)S(1)} collective-permute-done((bf16[512,128]{1,0:T(8,128)(2,1)S(1)}, bf16[512,128]{1,0:T(8,128)(2,1)S(1)}, u32[]{:S(2)}, u32[]{:S(2)}) %collective-permute-start.15) | collective-permute-done | bytes 131104 | tf_op jit(solution)/shard_map/ppermute | solution.py:23
  66.0 7.5 %collective-permute-done.16.refs_6_.refs_5_ = bf16[512,128]{1,0:T(8,128)(2,1)S(1)} collective-permute-done((bf16[512,128]{1,0:T(8,128)(2,1)S(1)}, bf16[512,128]{1,0:T(8,128)(2,1)S(1)}, u32[]{:S(2)}, u32[]{:S(2)}) %collective-permute-start.16) | collective-permute-done | bytes 131104 | tf_op jit(solution)/shard_map/ppermute | solution.py:23
  73.6 2.2 %backward.2 = (bf16[5120,128]{1,0:T(8,128)(2,1)S(1)}, bf16[5120,128]{1,0:T(8,128)(2,1)S(1)}) custom-call(bf16[2064,128]{1,0:T(8,128)(2,1)S(1)} %collective-permute-done.2.refs_10_.refs_0_, bf16[2064,128]{1,0:T(8,128)(2,1)S(1)} %collective-permute-done.1.refs_0_.refs_1_, bf16[2064,128]{1,0:T(8,128)(2,1)S(1)} %collective-permute-done.3.refs_1_.refs_2_, ...), custom_call_target="tpu_custom_call" | custom-call | flops 134217728 | bytes 5255168 | tf_op jit(solution)/shard_map/backward/pallas_call | solution.py:356
  75.7 1.3 collective-permute-start.17
  77.0 1.9 %backward.3 = (bf16[4096,128]{1,0:T(8,128)(2,1)S(1)}, bf16[4096,128]{1,0:T(8,128)(2,1)S(1)}) custom-call(bf16[2064,128]{1,0:T(8,128)(2,1)S(1)} %copy-done.1, bf16[2064,128]{1,0:T(8,128)(2,1)S(1)} %collective-permute-done.refs_9_.refs_1_, bf16[512,128]{1,0:T(8,128)(2,1)S(1)} %get-tuple-element.51.refs_3_.refs_2_, ...), custom_call_target="tpu_custom_call" | custom-call | flops 134217728 | bytes 3678208 | tf_op jit(solution)/shard_map/backward/pallas_call | solution.py:356
  78.9 0.8 collective-permute-start.21
  79.7 0.3 pair_sum.2
  80.0 2.1 %collective-permute-start.18 = (bf16[1280,128]{1,0:T(8,128)(2,1)S(1)}, bf16[1280,128]{1,0:T(8,128)(2,1)S(1)}, u32[]{:S(2)}, u32[]{:S(2)}) collective-permute-start(bf16[1280,128]{1,0:T(8,128)(2,1)S(1)} %get-tuple-element.62), channel_id=1, source_target_pairs={{0,8},{4,12},{8,0},{12,4},{16,24},{20,28},{24,16},{28,20},{1,9},{5... | collective-permute-start | bytes 983048 | tf_op jit(solution)/shard_map/ppermute | solution.py:23
  82.1 0.6 collective-permute-start.19
  82.7 1.1 collective-permute-start.20
  83.8 0.2 pair_sum.3
  84.0 1.0 collective-permute-start.25
  85.0 0.6 collective-permute-start.26
  85.6 4.2 %collective-permute-done.18.refs_1_ = bf16[1280,128]{1,0:T(8,128)(2,1)S(1)} collective-permute-done((bf16[1280,128]{1,0:T(8,128)(2,1)S(1)}, bf16[1280,128]{1,0:T(8,128)(2,1)S(1)}, u32[]{:S(2)}, u32[]{:S(2)}) %collective-permute-start.18) | collective-permute-done | bytes 327712 | tf_op jit(solution)/shard_map/ppermute | solution.py:23
  89.8 1.6 %collective-permute-start.27 = (bf16[1024,128]{1,0:T(8,128)(2,1)S(1)}, bf16[1024,128]{1,0:T(8,128)(2,1)S(1)}, u32[]{:S(2)}, u32[]{:S(2)}) collective-permute-start(bf16[1024,128]{1,0:T(8,128)(2,1)S(1)} %get-tuple-element.72), channel_id=1, source_target_pairs={{0,24},{4,28},{8,16},{12,20},{16,8},{20,12},{24,0},{28,4},{1,25},{... | collective-permute-start | bytes 786440 | tf_op jit(solution)/shard_map/ppermute | solution.py:23
  91.4 6.9 %collective-permute-done.20.refs_3_ = bf16[1280,128]{1,0:T(8,128)(2,1)S(1)} collective-permute-done((bf16[1280,128]{1,0:T(8,128)(2,1)S(1)}, bf16[1280,128]{1,0:T(8,128)(2,1)S(1)}, u32[]{:S(2)}, u32[]{:S(2)}) %collective-permute-start.20) | collective-permute-done | bytes 327712 | tf_op jit(solution)/shard_map/ppermute | solution.py:23
  98.3 0.2 plane_sum.2
  98.6 0.5 collective-permute-start.24
  99.1 3.5 %collective-permute-done.25.refs_1_ = bf16[1024,128]{1,0:T(8,128)(2,1)S(1)} collective-permute-done((bf16[1024,128]{1,0:T(8,128)(2,1)S(1)}, bf16[1024,128]{1,0:T(8,128)(2,1)S(1)}, u32[]{:S(2)}, u32[]{:S(2)}) %collective-permute-start.25) | collective-permute-done | bytes 262176 | tf_op jit(solution)/shard_map/ppermute | solution.py:23
  102.5 0.8 collective-permute-done.26.refs_2_
  103.3 6.3 %collective-permute-done.27.refs_3_ = bf16[1024,128]{1,0:T(8,128)(2,1)S(1)} collective-permute-done((bf16[1024,128]{1,0:T(8,128)(2,1)S(1)}, bf16[1024,128]{1,0:T(8,128)(2,1)S(1)}, u32[]{:S(2)}, u32[]{:S(2)}) %collective-permute-start.27) | collective-permute-done | bytes 262176 | tf_op jit(solution)/shard_map/ppermute | solution.py:23
  109.6 0.1 plane_sum.3
  109.8 0.3 collective-permute-done.23.refs_2_
  110.1 5.0 %collective-permute-done.24.refs_3_ = bf16[768,128]{1,0:T(8,128)(2,1)S(1)} collective-permute-done((bf16[768,128]{1,0:T(8,128)(2,1)S(1)}, bf16[768,128]{1,0:T(8,128)(2,1)S(1)}, u32[]{:S(2)}, u32[]{:S(2)}) %collective-permute-start.24) | collective-permute-done | bytes 196640 | tf_op jit(solution)/shard_map/ppermute | solution.py:23
  115.1 1.4 %collective-permute-start.28 = (bf16[256,128]{1,0:T(8,128)(2,1)S(1)}, bf16[256,128]{1,0:T(8,128)(2,1)S(1)}, u32[]{:S(2)}, u32[]{:S(2)}) collective-permute-start(bf16[256,128]{1,0:T(8,128)(2,1)S(1)} %weight_total.1.refs_0_), channel_id=1, source_target_pairs={{0,8},{4,12},{8,0},{12,4},{16,24},{20,28},{24,16},{28,20},{1,9},{5... | collective-permute-start | bytes 196616 | tf_op jit(solution)/shard_map/ppermute | solution.py:23
  116.5 1.2 collective-permute-start.29
  117.7 0.2 collective-permute-start.30
  117.9 3.3 %collective-permute-start.31 = (bf16[256,128]{1,0:T(8,128)(2,1)S(1)}, bf16[256,128]{1,0:T(8,128)(2,1)S(1)}, u32[]{:S(2)}, u32[]{:S(2)}) collective-permute-start(bf16[256,128]{1,0:T(8,128)(2,1)S(1)} %weight_total.1.refs_0_), channel_id=1, source_target_pairs={{0,4},{4,0},{8,12},{12,8},{16,20},{20,16},{24,28},{28,24},{1,5},{5... | collective-permute-start | bytes 196616 | tf_op jit(solution)/shard_map/ppermute | solution.py:23
  121.1 1.1 collective-permute-start.32
  122.2 1.1 collective-permute-start.33
  123.3 1.7 %collective-permute-start.34 = (bf16[256,128]{1,0:T(8,128)(2,1)S(1)}, bf16[256,128]{1,0:T(8,128)(2,1)S(1)}, u32[]{:S(2)}, u32[]{:S(2)}) collective-permute-start(bf16[256,128]{1,0:T(8,128)(2,1)S(1)} %collective-permute-done.30.refs_3_), channel_id=1, source_target_pairs={{0,4},{4,0},{8,12},{12,8},{16,20},{20,16},{24,28},{28,24},{1,5},{5... | collective-permute-start | bytes 196616 | tf_op jit(solution)/shard_map/ppermute | solution.py:23
  125.1 0.9 join.1
  126.0 1.1 weight_whole.1
  (38 shorter events, 0.4 us)
Async XLA Ops:
  1.3 36.1 %copy-start.2 = (bf16[512,512]{1,0:T(8,128)(2,1)S(1)}, bf16[512,512]{1,0:T(8,128)(2,1)}, u32[]{:S(2)}) copy-start(bf16[512,512]{1,0:T(8,128)(2,1)} %refs_11_.1) | copy-start | bytes 1572868
  1.3 36.1 %copy-start.4 = (bf16[8,512]{1,0:T(8,128)(2,1)S(1)}, bf16[8,512]{1,0:T(8,128)(2,1)}, u32[]{:S(2)}) copy-start(bf16[8,512]{1,0:T(8,128)(2,1)} %refs_12_.1) | copy-start | bytes 24580
  3.6 22.6 %collective-permute-start = (bf16[2064,128]{1,0:T(8,128)(2,1)}, bf16[2064,128]{1,0:T(8,128)(2,1)S(1)}, u32[]{:S(2)}, u32[]{:S(2)}) collective-permute-start(bf16[2064,128]{1,0:T(8,128)(2,1)} %get-tuple-element.40.refs_8_.refs_0_), channel_id=1, source_target_pairs={{0,1},{1,0},{2,3},{3,2},{4,5},{5,4},{6,7},{7,6},{8,9},{9,8},{10,11... | collective-permute-start | bytes 1585160 | tf_op jit(solution)/shard_map/ppermute | solution.py:23
  3.7 27.1 %collective-permute-start.2 = (bf16[2064,128]{1,0:T(8,128)(2,1)}, bf16[2064,128]{1,0:T(8,128)(2,1)S(1)}, u32[]{:S(2)}, u32[]{:S(2)}) collective-permute-start(bf16[2064,128]{1,0:T(8,128)(2,1)} %get-tuple-element.40.refs_8_.refs_0_), channel_id=1, source_target_pairs={{0,2},{1,3},{2,0},{3,1},{4,6},{5,7},{6,4},{7,5},{8,10},{9,11},{10,... | collective-permute-start | bytes 1585160 | tf_op jit(solution)/shard_map/ppermute | solution.py:23
  6.1 21.3 %collective-permute-start.6 = (bf16[2048,128]{1,0:T(8,128)(2,1)}, bf16[2048,128]{1,0:T(8,128)(2,1)S(1)}, u32[]{:S(2)}, u32[]{:S(2)}) collective-permute-start(bf16[2048,128]{1,0:T(8,128)(2,1)} %get-tuple-element.41.refs_0_), channel_id=1, source_target_pairs={{0,24},{4,28},{8,16},{12,20},{16,8},{20,12},{24,0},{28,4},{1,25},{... | collective-permute-start | bytes 1572872 | tf_op jit(solution)/shard_map/ppermute | solution.py:23
  8.3 23.8 %collective-permute-start.4 = (bf16[2048,128]{1,0:T(8,128)(2,1)}, bf16[2048,128]{1,0:T(8,128)(2,1)S(1)}, u32[]{:S(2)}, u32[]{:S(2)}) collective-permute-start(bf16[2048,128]{1,0:T(8,128)(2,1)} %get-tuple-element.41.refs_0_), channel_id=1, source_target_pairs={{0,8},{4,12},{8,0},{12,4},{16,24},{20,28},{24,16},{28,20},{1,9},{5... | collective-permute-start | bytes 1572872 | tf_op jit(solution)/shard_map/ppermute | solution.py:23
  8.6 25.8 %collective-permute-start.5 = (bf16[2048,128]{1,0:T(8,128)(2,1)}, bf16[2048,128]{1,0:T(8,128)(2,1)S(1)}, u32[]{:S(2)}, u32[]{:S(2)}) collective-permute-start(bf16[2048,128]{1,0:T(8,128)(2,1)} %get-tuple-element.41.refs_0_), channel_id=1, source_target_pairs={{0,16},{4,20},{8,24},{12,28},{16,0},{20,4},{24,8},{28,12},{1,17},{... | collective-permute-start | bytes 1572872 | tf_op jit(solution)/shard_map/ppermute | solution.py:23
  26.2 8.3 %collective-permute-start.7 = (bf16[2048,128]{1,0:T(8,128)(2,1)}, bf16[2048,128]{1,0:T(8,128)(2,1)S(1)}, u32[]{:S(2)}, u32[]{:S(2)}) collective-permute-start(bf16[2048,128]{1,0:T(8,128)(2,1)} %get-tuple-element.41.refs_0_), channel_id=1, source_target_pairs={{0,4},{4,0},{8,12},{12,8},{16,20},{20,16},{24,28},{28,24},{1,5},{5... | collective-permute-start | bytes 1572872 | tf_op jit(solution)/shard_map/ppermute | solution.py:23
  27.4 15.8 %collective-permute-start.1 = (bf16[2064,128]{1,0:T(8,128)(2,1)}, bf16[2064,128]{1,0:T(8,128)(2,1)S(1)}, u32[]{:S(2)}, u32[]{:S(2)}) collective-permute-start(bf16[2064,128]{1,0:T(8,128)(2,1)} %get-tuple-element.40.refs_8_.refs_0_), channel_id=1, source_target_pairs={{1,2},{2,1},{5,6},{6,5},{9,10},{10,9},{13,14},{14,13},{17,18},{18,... | collective-permute-start | bytes 1585160 | tf_op jit(solution)/shard_map/ppermute | solution.py:376
  30.8 12.4 %collective-permute-start.3 = (bf16[2064,128]{1,0:T(8,128)(2,1)S(1)}, bf16[2064,128]{1,0:T(8,128)(2,1)S(1)}, u32[]{:S(2)}, u32[]{:S(2)}) collective-permute-start(bf16[2064,128]{1,0:T(8,128)(2,1)S(1)} %collective-permute-done.2.refs_10_.refs_0_), channel_id=1, source_target_pairs={{2,3},{1,0},{6,7},{5,4},{10,11},{9,8},{14,15},{13,12},{18,19},{17,... | collective-permute-start | bytes 1585160 | tf_op jit(solution)/shard_map/ppermute | solution.py:374
  32.2 3.7 %collective-permute-start.10 = (bf16[2048,128]{1,0:T(8,128)(2,1)S(1)}, bf16[2048,128]{1,0:T(8,128)(2,1)S(1)}, u32[]{:S(2)}, u32[]{:S(2)}) collective-permute-start(bf16[2048,128]{1,0:T(8,128)(2,1)S(1)} %collective-permute-done.6.refs_3_), channel_id=1, source_target_pairs={{0,4},{4,0},{8,12},{12,8},{16,20},{20,16},{24,28},{28,24},{1,5},{5... | collective-permute-start | bytes 1572872 | tf_op jit(solution)/shard_map/ppermute | solution.py:23
  34.4 2.3 %collective-permute-start.8 = (bf16[2048,128]{1,0:T(8,128)(2,1)S(1)}, bf16[2048,128]{1,0:T(8,128)(2,1)S(1)}, u32[]{:S(2)}, u32[]{:S(2)}) collective-permute-start(bf16[2048,128]{1,0:T(8,128)(2,1)S(1)} %collective-permute-done.4.refs_1_), channel_id=1, source_target_pairs={{0,4},{4,0},{8,12},{12,8},{16,20},{20,16},{24,28},{28,24},{1,5},{5... | collective-permute-start | bytes 1572872 | tf_op jit(solution)/shard_map/ppermute | solution.py:23
  34.4 2.9 %collective-permute-start.9 = (bf16[2048,128]{1,0:T(8,128)(2,1)S(1)}, bf16[2048,128]{1,0:T(8,128)(2,1)S(1)}, u32[]{:S(2)}, u32[]{:S(2)}) collective-permute-start(bf16[2048,128]{1,0:T(8,128)(2,1)S(1)} %collective-permute-done.5.refs_2_), channel_id=1, source_target_pairs={{0,4},{4,0},{8,12},{12,8},{16,20},{20,16},{24,28},{28,24},{1,5},{5... | collective-permute-start | bytes 1572872 | tf_op jit(solution)/shard_map/ppermute | solution.py:23
  37.4 1.0 copy-start
  38.4 1.0 copy-start.3
  43.2 4.5 %copy-start.5 = (s32[2048]{0:T(1024)S(1)}, s32[2048]{0:T(1024)}, u32[]{:S(2)}) copy-start(s32[2048]{0:T(1024)} %param.12) | copy-start | bytes 24580
  43.2 4.5 %copy-start.6 = (s32[2048]{0:T(1024)S(1)}, s32[2048]{0:T(1024)}, u32[]{:S(2)}) copy-start(s32[2048]{0:T(1024)} %param.13) | copy-start | bytes 24580
  44.9 4.1 %collective-permute-start.11 = (bf16[512,128]{1,0:T(8,128)(2,1)}, bf16[512,128]{1,0:T(8,128)(2,1)S(1)}, u32[]{:S(2)}, u32[]{:S(2)}) collective-permute-start(bf16[512,128]{1,0:T(8,128)(2,1)} %get-tuple-element.45), channel_id=1, source_target_pairs={{0,1},{1,0},{2,3},{3,2},{4,5},{5,4},{6,7},{7,6},{8,9},{9,8},{10,11... | collective-permute-start | bytes 393224 | tf_op jit(solution)/shard_map/ppermute | solution.py:23
  45.6 6.0 %collective-permute-start.12 = (bf16[512,128]{1,0:T(8,128)(2,1)S(1)}, bf16[512,128]{1,0:T(8,128)(2,1)S(1)}, u32[]{:S(2)}, u32[]{:S(2)}) collective-permute-start(bf16[512,128]{1,0:T(8,128)(2,1)S(1)} %get-tuple-element.46), channel_id=1, source_target_pairs={{0,2},{1,3},{2,0},{3,1},{4,6},{5,7},{6,4},{7,5},{8,10},{9,11},{10,... | collective-permute-start | bytes 393224 | tf_op jit(solution)/shard_map/ppermute | solution.py:23
  47.4 10.8 %collective-permute-start.13 = (bf16[512,128]{1,0:T(8,128)(2,1)S(1)}, bf16[512,128]{1,0:T(8,128)(2,1)S(1)}, u32[]{:S(2)}, u32[]{:S(2)}) collective-permute-start(bf16[512,128]{1,0:T(8,128)(2,1)S(1)} %get-tuple-element.47), channel_id=1, source_target_pairs={{0,3},{1,2},{2,1},{3,0},{4,7},{5,6},{6,5},{7,4},{8,11},{9,10},{10,... | collective-permute-start | bytes 393224 | tf_op jit(solution)/shard_map/ppermute | solution.py:23
  59.6 3.9 %collective-permute-start.14 = (bf16[512,128]{1,0:T(8,128)(2,1)S(1)}, bf16[512,128]{1,0:T(8,128)(2,1)S(1)}, u32[]{:S(2)}, u32[]{:S(2)}) collective-permute-start(bf16[512,128]{1,0:T(8,128)(2,1)S(1)} %get-tuple-element.52), channel_id=1, source_target_pairs={{0,1},{1,0},{2,3},{3,2},{4,5},{5,4},{6,7},{7,6},{8,9},{9,8},{10,11... | collective-permute-start | bytes 393224 | tf_op jit(solution)/shard_map/ppermute | solution.py:23
  59.7 6.3 %collective-permute-start.15 = (bf16[512,128]{1,0:T(8,128)(2,1)S(1)}, bf16[512,128]{1,0:T(8,128)(2,1)S(1)}, u32[]{:S(2)}, u32[]{:S(2)}) collective-permute-start(bf16[512,128]{1,0:T(8,128)(2,1)S(1)} %get-tuple-element.53), channel_id=1, source_target_pairs={{0,2},{1,3},{2,0},{3,1},{4,6},{5,7},{6,4},{7,5},{8,10},{9,11},{10,... | collective-permute-start | bytes 393224 | tf_op jit(solution)/shard_map/ppermute | solution.py:23
  61.9 11.7 %collective-permute-start.16 = (bf16[512,128]{1,0:T(8,128)(2,1)S(1)}, bf16[512,128]{1,0:T(8,128)(2,1)S(1)}, u32[]{:S(2)}, u32[]{:S(2)}) collective-permute-start(bf16[512,128]{1,0:T(8,128)(2,1)S(1)} %get-tuple-element.54), channel_id=1, source_target_pairs={{0,3},{1,2},{2,1},{3,0},{4,7},{5,6},{6,5},{7,4},{8,11},{9,10},{10,... | collective-permute-start | bytes 393224 | tf_op jit(solution)/shard_map/ppermute | solution.py:23
  73.6 3.4 %copy-start.1 = (bf16[2064,128]{1,0:T(8,128)(2,1)S(1)}, bf16[2064,128]{1,0:T(8,128)(2,1)}, u32[]{:S(2)}) copy-start(bf16[2064,128]{1,0:T(8,128)(2,1)} %get-tuple-element.40.refs_8_.refs_0_) | copy-start | bytes 1585156
  75.7 3.9 %collective-permute-start.17 = (bf16[5120,128]{1,0:T(8,128)(2,1)S(1)}, bf16[5120,128]{1,0:T(8,128)(2,1)S(1)}, u32[]{:S(2)}, u32[]{:S(2)}) collective-permute-start(bf16[5120,128]{1,0:T(8,128)(2,1)S(1)} %get-tuple-element.59), channel_id=1, source_target_pairs={{0,4},{4,0},{8,12},{12,8},{16,20},{20,16},{24,28},{28,24},{1,5},{5... | collective-permute-start | bytes 3932168 | tf_op jit(solution)/shard_map/ppermute | solution.py:23
  78.9 4.9 %collective-permute-start.21 = (bf16[4096,128]{1,0:T(8,128)(2,1)S(1)}, bf16[4096,128]{1,0:T(8,128)(2,1)S(1)}, u32[]{:S(2)}, u32[]{:S(2)}) collective-permute-start(bf16[4096,128]{1,0:T(8,128)(2,1)S(1)} %get-tuple-element.65), channel_id=1, source_target_pairs={{0,4},{4,0},{8,12},{12,8},{16,20},{20,16},{24,28},{28,24},{1,5},{5... | collective-permute-start | bytes 3145736 | tf_op jit(solution)/shard_map/ppermute | solution.py:23
  80.0 9.9 %collective-permute-start.18 = (bf16[1280,128]{1,0:T(8,128)(2,1)S(1)}, bf16[1280,128]{1,0:T(8,128)(2,1)S(1)}, u32[]{:S(2)}, u32[]{:S(2)}) collective-permute-start(bf16[1280,128]{1,0:T(8,128)(2,1)S(1)} %get-tuple-element.62), channel_id=1, source_target_pairs={{0,8},{4,12},{8,0},{12,4},{16,24},{20,28},{24,16},{28,20},{1,9},{5... | collective-permute-start | bytes 983048 | tf_op jit(solution)/shard_map/ppermute | solution.py:23
  82.1 9.4 %collective-permute-start.19 = (bf16[1280,128]{1,0:T(8,128)(2,1)S(1)}, bf16[1280,128]{1,0:T(8,128)(2,1)S(1)}, u32[]{:S(2)}, u32[]{:S(2)}) collective-permute-start(bf16[1280,128]{1,0:T(8,128)(2,1)S(1)} %get-tuple-element.63), channel_id=1, source_target_pairs={{0,16},{4,20},{8,24},{12,28},{16,0},{20,4},{24,8},{28,12},{1,17},{... | collective-permute-start | bytes 983048 | tf_op jit(solution)/shard_map/ppermute | solution.py:23
  82.7 15.6 %collective-permute-start.20 = (bf16[1280,128]{1,0:T(8,128)(2,1)S(1)}, bf16[1280,128]{1,0:T(8,128)(2,1)S(1)}, u32[]{:S(2)}, u32[]{:S(2)}) collective-permute-start(bf16[1280,128]{1,0:T(8,128)(2,1)S(1)} %get-tuple-element.64), channel_id=1, source_target_pairs={{0,24},{4,28},{8,16},{12,20},{16,8},{20,12},{24,0},{28,4},{1,25},{... | collective-permute-start | bytes 983048 | tf_op jit(solution)/shard_map/ppermute | solution.py:23
  84.0 18.5 %collective-permute-start.25 = (bf16[1024,128]{1,0:T(8,128)(2,1)S(1)}, bf16[1024,128]{1,0:T(8,128)(2,1)S(1)}, u32[]{:S(2)}, u32[]{:S(2)}) collective-permute-start(bf16[1024,128]{1,0:T(8,128)(2,1)S(1)} %get-tuple-element.70), channel_id=1, source_target_pairs={{0,8},{4,12},{8,0},{12,4},{16,24},{20,28},{24,16},{28,20},{1,9},{5... | collective-permute-start | bytes 786440 | tf_op jit(solution)/shard_map/ppermute | solution.py:23
  85.0 18.3 %collective-permute-start.26 = (bf16[1024,128]{1,0:T(8,128)(2,1)S(1)}, bf16[1024,128]{1,0:T(8,128)(2,1)S(1)}, u32[]{:S(2)}, u32[]{:S(2)}) collective-permute-start(bf16[1024,128]{1,0:T(8,128)(2,1)S(1)} %get-tuple-element.71), channel_id=1, source_target_pairs={{0,16},{4,20},{8,24},{12,28},{16,0},{20,4},{24,8},{28,12},{1,17},{... | collective-permute-start | bytes 786440 | tf_op jit(solution)/shard_map/ppermute | solution.py:23
  89.8 19.7 %collective-permute-start.27 = (bf16[1024,128]{1,0:T(8,128)(2,1)S(1)}, bf16[1024,128]{1,0:T(8,128)(2,1)S(1)}, u32[]{:S(2)}, u32[]{:S(2)}) collective-permute-start(bf16[1024,128]{1,0:T(8,128)(2,1)S(1)} %get-tuple-element.72), channel_id=1, source_target_pairs={{0,24},{4,28},{8,16},{12,20},{16,8},{20,12},{24,0},{28,4},{1,25},{... | collective-permute-start | bytes 786440 | tf_op jit(solution)/shard_map/ppermute | solution.py:23
  98.5 11.6 %collective-permute-start.23 = (bf16[768,128]{1,0:T(8,128)(2,1)S(1)}, bf16[768,128]{1,0:T(8,128)(2,1)S(1)}, u32[]{:S(2)}, u32[]{:S(2)}) collective-permute-start(bf16[768,128]{1,0:T(8,128)(2,1)S(1)} %get-tuple-element.68), channel_id=1, source_target_pairs={{0,2},{1,3},{2,0},{3,1},{4,6},{5,7},{6,4},{7,5},{8,10},{9,11},{10,... | collective-permute-start | bytes 589832 | tf_op jit(solution)/shard_map/ppermute | solution.py:23
  98.6 16.5 %collective-permute-start.24 = (bf16[768,128]{1,0:T(8,128)(2,1)S(1)}, bf16[768,128]{1,0:T(8,128)(2,1)S(1)}, u32[]{:S(2)}, u32[]{:S(2)}) collective-permute-start(bf16[768,128]{1,0:T(8,128)(2,1)S(1)} %get-tuple-element.69), channel_id=1, source_target_pairs={{0,3},{1,2},{2,1},{3,0},{4,7},{5,6},{6,5},{7,4},{8,11},{9,10},{10,... | collective-permute-start | bytes 589832 | tf_op jit(solution)/shard_map/ppermute | solution.py:23
  102.5 7.2 %collective-permute-start.22 = (bf16[256,128]{1,0:T(8,128)(2,1)S(1)}, bf16[256,128]{1,0:T(8,128)(2,1)S(1)}, u32[]{:S(2)}, u32[]{:S(2)}) collective-permute-start(bf16[256,128]{1,0:T(8,128)(2,1)S(1)} %get-tuple-element.67.refs_0_), channel_id=1, source_target_pairs={{0,1},{1,0},{2,3},{3,2},{4,5},{5,4},{6,7},{7,6},{8,9},{9,8},{10,11... | collective-permute-start | bytes 196616 | tf_op jit(solution)/shard_map/ppermute | solution.py:23
  109.7 15.4 %collective-permute-start.35 = (bf16[512,128]{1,0:T(8,128)(2,1)S(1)}, bf16[512,128]{1,0:T(8,128)(2,1)S(1)}, u32[]{:S(2)}, u32[]{:S(2)}) collective-permute-start(bf16[512,128]{1,0:T(8,128)(2,1)S(1)} %get-tuple-element.74), channel_id=1, source_target_pairs={{0,1},{1,0},{2,3},{3,2},{4,5},{5,4},{6,7},{7,6},{8,9},{9,8},{10,11... | collective-permute-start | bytes 393224 | tf_op jit(solution)/shard_map/ppermute | solution.py:23
  115.1 6.0 %collective-permute-start.28 = (bf16[256,128]{1,0:T(8,128)(2,1)S(1)}, bf16[256,128]{1,0:T(8,128)(2,1)S(1)}, u32[]{:S(2)}, u32[]{:S(2)}) collective-permute-start(bf16[256,128]{1,0:T(8,128)(2,1)S(1)} %weight_total.1.refs_0_), channel_id=1, source_target_pairs={{0,8},{4,12},{8,0},{12,4},{16,24},{20,28},{24,16},{28,20},{1,9},{5... | collective-permute-start | bytes 196616 | tf_op jit(solution)/shard_map/ppermute | solution.py:23
  116.5 5.7 %collective-permute-start.29 = (bf16[256,128]{1,0:T(8,128)(2,1)S(1)}, bf16[256,128]{1,0:T(8,128)(2,1)S(1)}, u32[]{:S(2)}, u32[]{:S(2)}) collective-permute-start(bf16[256,128]{1,0:T(8,128)(2,1)S(1)} %weight_total.1.refs_0_), channel_id=1, source_target_pairs={{0,16},{4,20},{8,24},{12,28},{16,0},{20,4},{24,8},{28,12},{1,17},{... | collective-permute-start | bytes 196616 | tf_op jit(solution)/shard_map/ppermute | solution.py:23
  117.7 5.6 %collective-permute-start.30 = (bf16[256,128]{1,0:T(8,128)(2,1)S(1)}, bf16[256,128]{1,0:T(8,128)(2,1)S(1)}, u32[]{:S(2)}, u32[]{:S(2)}) collective-permute-start(bf16[256,128]{1,0:T(8,128)(2,1)S(1)} %weight_total.1.refs_0_), channel_id=1, source_target_pairs={{0,24},{4,28},{8,16},{12,20},{16,8},{20,12},{24,0},{28,4},{1,25},{... | collective-permute-start | bytes 196616 | tf_op jit(solution)/shard_map/ppermute | solution.py:23
  117.9 8.1 %collective-permute-start.31 = (bf16[256,128]{1,0:T(8,128)(2,1)S(1)}, bf16[256,128]{1,0:T(8,128)(2,1)S(1)}, u32[]{:S(2)}, u32[]{:S(2)}) collective-permute-start(bf16[256,128]{1,0:T(8,128)(2,1)S(1)} %weight_total.1.refs_0_), channel_id=1, source_target_pairs={{0,4},{4,0},{8,12},{12,8},{16,20},{20,16},{24,28},{28,24},{1,5},{5... | collective-permute-start | bytes 196616 | tf_op jit(solution)/shard_map/ppermute | solution.py:23
  121.1 4.9 %collective-permute-start.32 = (bf16[256,128]{1,0:T(8,128)(2,1)S(1)}, bf16[256,128]{1,0:T(8,128)(2,1)S(1)}, u32[]{:S(2)}, u32[]{:S(2)}) collective-permute-start(bf16[256,128]{1,0:T(8,128)(2,1)S(1)} %collective-permute-done.28.refs_1_), channel_id=1, source_target_pairs={{0,4},{4,0},{8,12},{12,8},{16,20},{20,16},{24,28},{28,24},{1,5},{5... | collective-permute-start | bytes 196616 | tf_op jit(solution)/shard_map/ppermute | solution.py:23
  122.2 3.8 %collective-permute-start.33 = (bf16[256,128]{1,0:T(8,128)(2,1)S(1)}, bf16[256,128]{1,0:T(8,128)(2,1)S(1)}, u32[]{:S(2)}, u32[]{:S(2)}) collective-permute-start(bf16[256,128]{1,0:T(8,128)(2,1)S(1)} %collective-permute-done.29.refs_2_), channel_id=1, source_target_pairs={{0,4},{4,0},{8,12},{12,8},{16,20},{20,16},{24,28},{28,24},{1,5},{5... | collective-permute-start | bytes 196616 | tf_op jit(solution)/shard_map/ppermute | solution.py:23
  123.3 2.7 %collective-permute-start.34 = (bf16[256,128]{1,0:T(8,128)(2,1)S(1)}, bf16[256,128]{1,0:T(8,128)(2,1)S(1)}, u32[]{:S(2)}, u32[]{:S(2)}) collective-permute-start(bf16[256,128]{1,0:T(8,128)(2,1)S(1)} %collective-permute-done.30.refs_3_), channel_id=1, source_target_pairs={{0,4},{4,0},{8,12},{12,8},{16,20},{20,16},{24,28},{28,24},{1,5},{5... | collective-permute-start | bytes 196616 | tf_op jit(solution)/shard_map/ppermute | solution.py:23

commit v7 on v6

--- a/solution.py
+++ b/solution.py
@@ -44,14 +44,14 @@
         lax.fori_loop(0, (live + GROUP - 1) // GROUP, step, 0)
 
 
-def forward_visit(panels, panel_rows, lists, ids, totals):
+def forward_visit(panels, panel_rows, block_of, ids, totals):
     def visit(i, panel, first, live):
         products = []
         for u in range(GROUP):
             slot = first + u
             start = panel * panel_rows + ids[i, 1, slot] * BLOCK
             source = panels[pl.ds(pl.multiple_of(start, BLOCK), BLOCK), :]
-            block = lists[i, pl.ds(pl.multiple_of(slot * BLOCK, BLOCK), BLOCK), :]
+            block = block_of(i, pl.ds(pl.multiple_of(slot * BLOCK, BLOCK), BLOCK))
             product = jnp.dot(block, source, preferred_element_type=jnp.float32)
             products.append(jnp.where(slot < live, product, 0.0))
         for u in range(GROUP):
@@ -121,7 +121,7 @@
     load_ids(ids_vmem, ids_smem, lists, slots, id_sem, clear)
     for copy in copies[early:]:
         copy.wait()
-    visit = forward_visit(panels, panel_rows, lists, ids_smem, totals)
+    visit = forward_visit(panels, panel_rows, lambda i, here: lists[i, here, :], ids_smem, totals)
     each_group(ids_smem, place, range(early), visit)
     start = pl.multiple_of((team ^ early) * panel_rows, panel_rows)
     late_panel[...] = panels[pl.ds(start, panel_rows), :]
@@ -135,15 +135,15 @@
 def late_kernel(teams, slots, place, *refs):
     middle, relayed, begun, panel = refs[:4]
     outs = refs[4 : 4 + teams]
-    totals, lists, ids_vmem, ids_smem, id_sem = refs[4 + teams :]
+    totals, ids_vmem, ids_smem, id_sem = refs[4 + teams :]
     tail = pick(place, teams, middle, relayed, pl.ds(slots * BLOCK, ID_ROWS))
     ids_vmem[0] = tail.astype(jnp.float32).astype(jnp.int32)[:8]
     copy = pltpu.make_async_copy(ids_vmem, ids_smem, id_sem)
     copy.start()
     totals[...] = begun[...]
-    lists[0] = pick(place, teams, middle, relayed, slice(None))
     copy.wait()
-    visit = forward_visit(panel, 0, lists, ids_smem, totals)
+    late = functools.partial(pick, place, teams, middle, relayed)
+    visit = forward_visit(panel, 0, lambda i, here: late(here), ids_smem, totals)
     each_group(ids_smem, place, [teams - 1], visit)
     share = outs[0].shape[0]
     for d in range(teams):
@@ -472,7 +472,7 @@
         [shaped(share, part)] * teams,
         [
             pltpu.VMEM((slab, part), f32),
-            *ids,
+            *ids[1:],
             pltpu.SemaphoreType.DMA,
         ],
         list_flops,

time: 127 us -> 128 us (level)
  waiting for transfers between devices: 69.3 us -> 67.5 us
  starting transfers between devices: 38.9 us -> 40.5 us
    ppermute x34, starting transfers between devices: 34.1 us -> 35.8 us  [swap(): return lax.ppermute(value, axis, [(i, i ^ flip) for i in range(size)])]
    ppermute x34, waiting for transfers between devices: 68 us -> 66.4 us  [swap(): return lax.ppermute(value, axis, [(i, i ^ flip) for i in range(size)])]
  transfers between devices with their start and end apart: 36 -> 36, of which waited for: 18 -> 18; matrix products, arithmetic and copies ran while one was open for 0% -> 0% of each run, Pallas kernels for 5% -> 6%
where the time goes in v7:
time: 128 us; the launch traced here: 127 us
  waiting for transfers between devices  67.5 us (53%)
  starting transfers between devices  40.5 us (32%)
  Pallas kernels  15.7 us (12%)
  local copies, waits for them, and re-layouts  2.12 us (2%)
  between operations  1.5 us (1%)
    ppermute x34, waiting for transfers between devices, swap(): return lax.ppermute(value, axis, [(i, i ^ flip) for i in range(size)])  66.4 us
    ppermute x34, starting transfers between devices, swap(): return lax.ppermute(value, axis, [(i, i ^ flip) for i in range(size)])  35.8 us
    pallas_call x14, Pallas kernels, call(): pl.pallas_call(body, name=name, in_specs=specs, out_specs=[pl.BlockSpec(m...  15.7 us
    ppermute x1, starting transfers between devices, gather_lists(): middle = lax.ppermute(held, 'team', [(1, 2), (2, 1)])  3.38 us
  transfers between devices with their start and end apart: 36, of which 18 were waited for; matrix products, arithmetic and copies ran while one was open for 0% of the time, Pallas kernels for 6%

profile of v7, /device:TPU:9, one launch (start us, length us, event | category | flops | bytes accessed | tf_op | source)
XLA Modules:
  0.0 127.4 jit_solution(11440243213391486965)
XLA Ops:
  1.3 2.3 %prepare.1 = (bf16[2064,128]{1,0:T(8,128)(2,1)}, bf16[2048,128]{1,0:T(8,128)(2,1)}) custom-call(bf16[2048,128]{1,0:T(8,128)(2,1)} %bitcast.5, s32[1,16]{1,0:T(1,128)} %bitcast.6, s32[1,16]{1,0:T(1,128)} %bitcast.7, s32[1,1]{1,0:T(1,128)S(6)} %copy.12.refs_3_, bf16[2048,512]{1,0:T(8,128)(2,1)} %refs_4_.1), custom_call_target="tpu_custom_call" | custom-call | tf_op jit(solution)/shard_map/prepare/pallas_call | solution.py:356
  3.7 2.5 %collective-permute-start.2 = (bf16[2064,128]{1,0:T(8,128)(2,1)}, bf16[2064,128]{1,0:T(8,128)(2,1)S(1)}, u32[]{:S(2)}, u32[]{:S(2)}) collective-permute-start(bf16[2064,128]{1,0:T(8,128)(2,1)} %get-tuple-element.40.refs_8_.refs_0_), channel_id=1, source_target_pairs={{0,2},{1,3},{2,0},{3,1},{4,6},{5,7},{6,4},{7,5},{8,10},{9,11},{10,... | collective-permute-start | bytes 1585160 | tf_op jit(solution)/shard_map/ppermute | solution.py:23
  6.1 2.2 %collective-permute-start.6 = (bf16[2048,128]{1,0:T(8,128)(2,1)}, bf16[2048,128]{1,0:T(8,128)(2,1)S(1)}, u32[]{:S(2)}, u32[]{:S(2)}) collective-permute-start(bf16[2048,128]{1,0:T(8,128)(2,1)} %get-tuple-element.41.refs_0_), channel_id=1, source_target_pairs={{0,24},{4,28},{8,16},{12,20},{16,8},{20,12},{24,0},{28,4},{1,25},{... | collective-permute-start | bytes 1572872 | tf_op jit(solution)/shard_map/ppermute | solution.py:23
  8.3 0.3 collective-permute-start.4
  8.6 0.2 collective-permute-start.5
  8.8 17.4 %collective-permute-done.refs_9_.refs_1_ = bf16[2064,128]{1,0:T(8,128)(2,1)S(1)} collective-permute-done((bf16[2064,128]{1,0:T(8,128)(2,1)}, bf16[2064,128]{1,0:T(8,128)(2,1)S(1)}, u32[]{:S(2)}, u32[]{:S(2)}) %collective-permute-start) | collective-permute-done | bytes 528416 | tf_op jit(solution)/shard_map/ppermute | solution.py:23
  26.2 1.2 collective-permute-start.7
  27.4 3.4 %collective-permute-start.1 = (bf16[2064,128]{1,0:T(8,128)(2,1)}, bf16[2064,128]{1,0:T(8,128)(2,1)S(1)}, u32[]{:S(2)}, u32[]{:S(2)}) collective-permute-start(bf16[2064,128]{1,0:T(8,128)(2,1)} %get-tuple-element.40.refs_8_.refs_0_), channel_id=1, source_target_pairs={{1,2},{2,1},{5,6},{6,5},{9,10},{10,9},{13,14},{14,13},{17,18},{18,... | collective-permute-start | bytes 1585160 | tf_op jit(solution)/shard_map/ppermute | solution.py:376
  30.8 1.3 %collective-permute-start.3 = (bf16[2064,128]{1,0:T(8,128)(2,1)S(1)}, bf16[2064,128]{1,0:T(8,128)(2,1)S(1)}, u32[]{:S(2)}, u32[]{:S(2)}) collective-permute-start(bf16[2064,128]{1,0:T(8,128)(2,1)S(1)} %collective-permute-done.2.refs_10_.refs_0_), channel_id=1, source_target_pairs={{2,3},{1,0},{6,7},{5,4},{10,11},{9,8},{14,15},{13,12},{18,19},{17,... | collective-permute-start | bytes 1585160 | tf_op jit(solution)/shard_map/ppermute | solution.py:374
  32.2 2.2 %collective-permute-start.10 = (bf16[2048,128]{1,0:T(8,128)(2,1)S(1)}, bf16[2048,128]{1,0:T(8,128)(2,1)S(1)}, u32[]{:S(2)}, u32[]{:S(2)}) collective-permute-start(bf16[2048,128]{1,0:T(8,128)(2,1)S(1)} %collective-permute-done.6.refs_3_), channel_id=1, source_target_pairs={{0,4},{4,0},{8,12},{12,8},{16,20},{20,16},{24,28},{28,24},{1,5},{5... | collective-permute-start | bytes 1572872 | tf_op jit(solution)/shard_map/ppermute | solution.py:23
  34.4 0.1 collective-permute-start.8
  34.4 0.4 collective-permute-start.9
  34.9 1.0 collective-permute-done.10.refs_7_
  35.9 0.7 collective-permute-done.8.refs_5_
  36.6 0.7 collective-permute-done.9.refs_6_
  37.4 1.0 copy-done
  38.4 1.0 copy-done.3
  39.5 2.6 %early_products.1 = (f32[2048,128]{1,0:T(8,128)S(1)}, bf16[4096,128]{1,0:T(8,128)(2,1)S(1)}, bf16[512,512]{1,0:T(8,128)(2,1)S(1)}, bf16[8,512]{1,0:T(8,128)(2,1)S(1)}) custom-call(bf16[2048,128]{1,0:T(8,128)(2,1)S(1)} %copy-done.3, bf16[2048,128]{1,0:T(8,128)(2,1)S(1)} %collective-permute-done.4.refs_1_, ...), custom_call_target="tpu_custom_call" | custom-call | tf_op jit(solution)/shard_map/early_products/pallas_call | solution.py:356
  42.1 1.1 collective-permute-done.1.refs_0_.refs_1_
  43.2 1.7 %late_products.1 = (bf16[512,128]{1,0:T(8,128)(2,1)S(1)}, bf16[512,128]{1,0:T(8,128)(2,1)}, bf16[512,128]{1,0:T(8,128)(2,1)S(1)}, bf16[512,128]{1,0:T(8,128)(2,1)S(1)}) custom-call(bf16[2064,128]{1,0:T(8,128)(2,1)S(1)} %collective-permute-done.1.refs_0_.refs_1_, bf16[2064,128]{1,0:T(8,128)(2,1)S(1)} %collective-permute-done.3.refs_1_.refs_2_, ...), custom_call_target="tpu_custom_call" | custom-call | flops 67108864 | bytes 3678208 | tf_op jit(solution)/shard_map/late_products/pallas_call | solution.py:356
  45.0 0.6 collective-permute-start.11
  45.6 2.0 %collective-permute-start.12 = (bf16[512,128]{1,0:T(8,128)(2,1)S(1)}, bf16[512,128]{1,0:T(8,128)(2,1)S(1)}, u32[]{:S(2)}, u32[]{:S(2)}) collective-permute-start(bf16[512,128]{1,0:T(8,128)(2,1)S(1)} %get-tuple-element.46), channel_id=1, source_target_pairs={{0,2},{1,3},{2,0},{3,1},{4,6},{5,7},{6,4},{7,5},{8,10},{9,11},{10,... | collective-permute-start | bytes 393224 | tf_op jit(solution)/shard_map/ppermute | solution.py:23
  47.7 1.4 %collective-permute-done.11.refs_1_ = bf16[512,128]{1,0:T(8,128)(2,1)S(1)} collective-permute-done((bf16[512,128]{1,0:T(8,128)(2,1)}, bf16[512,128]{1,0:T(8,128)(2,1)S(1)}, u32[]{:S(2)}, u32[]{:S(2)}) %collective-permute-start.11) | collective-permute-done | bytes 131104 | tf_op jit(solution)/shard_map/ppermute | solution.py:23
  49.1 3.4 %collective-permute-done.12.refs_2_ = bf16[512,128]{1,0:T(8,128)(2,1)S(1)} collective-permute-done((bf16[512,128]{1,0:T(8,128)(2,1)S(1)}, bf16[512,128]{1,0:T(8,128)(2,1)S(1)}, u32[]{:S(2)}, u32[]{:S(2)}) %collective-permute-start.12) | collective-permute-done | bytes 131104 | tf_op jit(solution)/shard_map/ppermute | solution.py:23
  52.4 5.7 %collective-permute-done.13.refs_3_ = bf16[512,128]{1,0:T(8,128)(2,1)S(1)} collective-permute-done((bf16[512,128]{1,0:T(8,128)(2,1)S(1)}, bf16[512,128]{1,0:T(8,128)(2,1)S(1)}, u32[]{:S(2)}, u32[]{:S(2)}) %collective-permute-start.13) | collective-permute-done | bytes 131104 | tf_op jit(solution)/shard_map/ppermute | solution.py:23
  58.2 1.4 %layer.1 = (bf16[512,512]{1,0:T(8,128)(2,1)}, bf16[512,512]{1,0:T(8,128)(2,1)S(1)}, bf16[512,128]{1,0:T(8,128)(2,1)S(1)}, bf16[512,128]{1,0:T(8,128)(2,1)S(1)}, ...) custom-call(bf16[512,128]{1,0:T(8,128)(2,1)S(1)} %get-tuple-element.44.refs_0_, ...), custom_call_target="tpu_custom_call" | custom-call | flops 536870912 | bytes 2646016 | tf_op jit(solution)/shard_map/layer/pallas_call | solution.py:356
  59.6 0.1 collective-permute-start.14
  59.7 3.3 %collective-permute-start.15 = (bf16[512,128]{1,0:T(8,128)(2,1)S(1)}, bf16[512,128]{1,0:T(8,128)(2,1)S(1)}, u32[]{:S(2)}, u32[]{:S(2)}) collective-permute-start(bf16[512,128]{1,0:T(8,128)(2,1)S(1)} %get-tuple-element.53), channel_id=1, source_target_pairs={{0,2},{1,3},{2,0},{3,1},{4,6},{5,7},{6,4},{7,5},{8,10},{9,11},{10,... | collective-permute-start | bytes 393224 | tf_op jit(solution)/shard_map/ppermute | solution.py:23
  63.0 0.6 weight_term.1
  63.5 7.1 %collective-permute-done.15.refs_5_.refs_4_ = bf16[512,128]{1,0:T(8,128)(2,1)S(1)} collective-permute-done((bf16[512,128]{1,0:T(8,128)(2,1)S(1)}, bf16[512,128]{1,0:T(8,128)(2,1)S(1)}, u32[]{:S(2)}, u32[]{:S(2)}) %collective-permute-start.15) | collective-permute-done | bytes 131104 | tf_op jit(solution)/shard_map/ppermute | solution.py:23
  70.6 3.0 %collective-permute-done.16.refs_6_.refs_5_ = bf16[512,128]{1,0:T(8,128)(2,1)S(1)} collective-permute-done((bf16[512,128]{1,0:T(8,128)(2,1)S(1)}, bf16[512,128]{1,0:T(8,128)(2,1)S(1)}, u32[]{:S(2)}, u32[]{:S(2)}) %collective-permute-start.16) | collective-permute-done | bytes 131104 | tf_op jit(solution)/shard_map/ppermute | solution.py:23
  73.6 2.2 %backward.2 = (bf16[5120,128]{1,0:T(8,128)(2,1)S(1)}, bf16[5120,128]{1,0:T(8,128)(2,1)S(1)}) custom-call(bf16[2064,128]{1,0:T(8,128)(2,1)S(1)} %collective-permute-done.2.refs_10_.refs_0_, bf16[2064,128]{1,0:T(8,128)(2,1)S(1)} %collective-permute-done.1.refs_0_.refs_1_, bf16[2064,128]{1,0:T(8,128)(2,1)S(1)} %collective-permute-done.3.refs_1_.refs_2_, ...), custom_call_target="tpu_custom_call" | custom-call | flops 134217728 | bytes 5255168 | tf_op jit(solution)/shard_map/backward/pallas_call | solution.py:356
  75.8 2.3 %collective-permute-start.17 = (bf16[5120,128]{1,0:T(8,128)(2,1)S(1)}, bf16[5120,128]{1,0:T(8,128)(2,1)S(1)}, u32[]{:S(2)}, u32[]{:S(2)}) collective-permute-start(bf16[5120,128]{1,0:T(8,128)(2,1)S(1)} %get-tuple-element.59), channel_id=1, source_target_pairs={{0,4},{4,0},{8,12},{12,8},{16,20},{20,16},{24,28},{28,24},{1,5},{5... | collective-permute-start | bytes 3932168 | tf_op jit(solution)/shard_map/ppermute | solution.py:23
  78.1 2.1 %backward.3 = (bf16[4096,128]{1,0:T(8,128)(2,1)S(1)}, bf16[4096,128]{1,0:T(8,128)(2,1)S(1)}) custom-call(bf16[2064,128]{1,0:T(8,128)(2,1)S(1)} %copy-done.1, bf16[2064,128]{1,0:T(8,128)(2,1)S(1)} %collective-permute-done.refs_9_.refs_1_, bf16[512,128]{1,0:T(8,128)(2,1)S(1)} %get-tuple-element.51.refs_3_.refs_2_, ...), custom_call_target="tpu_custom_call" | custom-call | flops 134217728 | bytes 3678208 | tf_op jit(solution)/shard_map/backward/pallas_call | solution.py:356
  80.2 0.1 collective-permute-start.21
  80.2 0.5 collective-permute-done.17.refs_1_
  80.7 0.3 pair_sum.2
  81.0 0.9 collective-permute-start.18
  81.9 2.2 %collective-permute-start.19 = (bf16[1280,128]{1,0:T(8,128)(2,1)S(1)}, bf16[1280,128]{1,0:T(8,128)(2,1)S(1)}, u32[]{:S(2)}, u32[]{:S(2)}) collective-permute-start(bf16[1280,128]{1,0:T(8,128)(2,1)S(1)} %get-tuple-element.63), channel_id=1, source_target_pairs={{0,16},{4,20},{8,24},{12,28},{16,0},{20,4},{24,8},{28,12},{1,17},{... | collective-permute-start | bytes 983048 | tf_op jit(solution)/shard_map/ppermute | solution.py:23
  84.1 0.2 pair_sum.3
  84.3 1.2 collective-permute-start.25
  85.6 1.5 %collective-permute-start.26 = (bf16[1024,128]{1,0:T(8,128)(2,1)S(1)}, bf16[1024,128]{1,0:T(8,128)(2,1)S(1)}, u32[]{:S(2)}, u32[]{:S(2)}) collective-permute-start(bf16[1024,128]{1,0:T(8,128)(2,1)S(1)} %get-tuple-element.71), channel_id=1, source_target_pairs={{0,16},{4,20},{8,24},{12,28},{16,0},{20,4},{24,8},{28,12},{1,17},{... | collective-permute-start | bytes 786440 | tf_op jit(solution)/shard_map/ppermute | solution.py:23
  87.0 3.0 %collective-permute-done.18.refs_1_ = bf16[1280,128]{1,0:T(8,128)(2,1)S(1)} collective-permute-done((bf16[1280,128]{1,0:T(8,128)(2,1)S(1)}, bf16[1280,128]{1,0:T(8,128)(2,1)S(1)}, u32[]{:S(2)}, u32[]{:S(2)}) %collective-permute-start.18) | collective-permute-done | bytes 327712 | tf_op jit(solution)/shard_map/ppermute | solution.py:23
  90.0 2.6 %collective-permute-start.27 = (bf16[1024,128]{1,0:T(8,128)(2,1)S(1)}, bf16[1024,128]{1,0:T(8,128)(2,1)S(1)}, u32[]{:S(2)}, u32[]{:S(2)}) collective-permute-start(bf16[1024,128]{1,0:T(8,128)(2,1)S(1)} %get-tuple-element.72), channel_id=1, source_target_pairs={{0,24},{4,28},{8,16},{12,20},{16,8},{20,12},{24,0},{28,4},{1,25},{... | collective-permute-start | bytes 786440 | tf_op jit(solution)/shard_map/ppermute | solution.py:23
  92.6 4.0 %collective-permute-done.19.refs_2_ = bf16[1280,128]{1,0:T(8,128)(2,1)S(1)} collective-permute-done((bf16[1280,128]{1,0:T(8,128)(2,1)S(1)}, bf16[1280,128]{1,0:T(8,128)(2,1)S(1)}, u32[]{:S(2)}, u32[]{:S(2)}) %collective-permute-start.19) | collective-permute-done | bytes 327712 | tf_op jit(solution)/shard_map/ppermute | solution.py:23
  96.6 1.9 %collective-permute-done.20.refs_3_ = bf16[1280,128]{1,0:T(8,128)(2,1)S(1)} collective-permute-done((bf16[1280,128]{1,0:T(8,128)(2,1)S(1)}, bf16[1280,128]{1,0:T(8,128)(2,1)S(1)}, u32[]{:S(2)}, u32[]{:S(2)}) %collective-permute-start.20) | collective-permute-done | bytes 327712 | tf_op jit(solution)/shard_map/ppermute | solution.py:23
  98.5 0.2 plane_sum.2
  98.7 0.4 collective-permute-start.23
  99.1 1.0 collective-permute-start.24
  100.1 2.6 %collective-permute-done.25.refs_1_ = bf16[1024,128]{1,0:T(8,128)(2,1)S(1)} collective-permute-done((bf16[1024,128]{1,0:T(8,128)(2,1)S(1)}, bf16[1024,128]{1,0:T(8,128)(2,1)S(1)}, u32[]{:S(2)}, u32[]{:S(2)}) %collective-permute-start.25) | collective-permute-done | bytes 262176 | tf_op jit(solution)/shard_map/ppermute | solution.py:23
  102.7 5.8 %collective-permute-done.26.refs_2_ = bf16[1024,128]{1,0:T(8,128)(2,1)S(1)} collective-permute-done((bf16[1024,128]{1,0:T(8,128)(2,1)S(1)}, bf16[1024,128]{1,0:T(8,128)(2,1)S(1)}, u32[]{:S(2)}, u32[]{:S(2)}) %collective-permute-start.26) | collective-permute-done | bytes 262176 | tf_op jit(solution)/shard_map/ppermute | solution.py:23
  108.5 1.3 %collective-permute-done.27.refs_3_ = bf16[1024,128]{1,0:T(8,128)(2,1)S(1)} collective-permute-done((bf16[1024,128]{1,0:T(8,128)(2,1)S(1)}, bf16[1024,128]{1,0:T(8,128)(2,1)S(1)}, u32[]{:S(2)}, u32[]{:S(2)}) %collective-permute-start.27) | collective-permute-done | bytes 262176 | tf_op jit(solution)/shard_map/ppermute | solution.py:23
  109.8 0.1 plane_sum.3
  110.0 0.1 collective-permute-start.35
  110.1 6.8 %collective-permute-done.24.refs_3_ = bf16[768,128]{1,0:T(8,128)(2,1)S(1)} collective-permute-done((bf16[768,128]{1,0:T(8,128)(2,1)S(1)}, bf16[768,128]{1,0:T(8,128)(2,1)S(1)}, u32[]{:S(2)}, u32[]{:S(2)}) %collective-permute-start.24) | collective-permute-done | bytes 196640 | tf_op jit(solution)/shard_map/ppermute | solution.py:23
  116.9 1.2 collective-permute-start.28
  118.1 0.3 collective-permute-start.29
  118.4 1.2 collective-permute-start.30
  119.6 2.5 %collective-permute-start.31 = (bf16[256,128]{1,0:T(8,128)(2,1)S(1)}, bf16[256,128]{1,0:T(8,128)(2,1)S(1)}, u32[]{:S(2)}, u32[]{:S(2)}) collective-permute-start(bf16[256,128]{1,0:T(8,128)(2,1)S(1)} %weight_total.1.refs_0_), channel_id=1, source_target_pairs={{0,4},{4,0},{8,12},{12,8},{16,20},{20,16},{24,28},{28,24},{1,5},{5... | collective-permute-start | bytes 196616 | tf_op jit(solution)/shard_map/ppermute | solution.py:23
  122.1 1.3 collective-permute-start.32
  123.4 0.9 collective-permute-start.33
  124.3 1.1 collective-permute-start.34
  125.4 0.9 join.1
  126.3 1.1 weight_whole.1
  (38 shorter events, 0.2 us)
Async XLA Ops:
  1.3 36.1 %copy-start.2 = (bf16[512,512]{1,0:T(8,128)(2,1)S(1)}, bf16[512,512]{1,0:T(8,128)(2,1)}, u32[]{:S(2)}) copy-start(bf16[512,512]{1,0:T(8,128)(2,1)} %refs_11_.1) | copy-start | bytes 1572868
  1.3 36.1 %copy-start.4 = (bf16[8,512]{1,0:T(8,128)(2,1)S(1)}, bf16[8,512]{1,0:T(8,128)(2,1)}, u32[]{:S(2)}) copy-start(bf16[8,512]{1,0:T(8,128)(2,1)} %refs_12_.1) | copy-start | bytes 24580
  3.6 22.6 %collective-permute-start = (bf16[2064,128]{1,0:T(8,128)(2,1)}, bf16[2064,128]{1,0:T(8,128)(2,1)S(1)}, u32[]{:S(2)}, u32[]{:S(2)}) collective-permute-start(bf16[2064,128]{1,0:T(8,128)(2,1)} %get-tuple-element.40.refs_8_.refs_0_), channel_id=1, source_target_pairs={{0,1},{1,0},{2,3},{3,2},{4,5},{5,4},{6,7},{7,6},{8,9},{9,8},{10,11... | collective-permute-start | bytes 1585160 | tf_op jit(solution)/shard_map/ppermute | solution.py:23
  3.7 27.1 %collective-permute-start.2 = (bf16[2064,128]{1,0:T(8,128)(2,1)}, bf16[2064,128]{1,0:T(8,128)(2,1)S(1)}, u32[]{:S(2)}, u32[]{:S(2)}) collective-permute-start(bf16[2064,128]{1,0:T(8,128)(2,1)} %get-tuple-element.40.refs_8_.refs_0_), channel_id=1, source_target_pairs={{0,2},{1,3},{2,0},{3,1},{4,6},{5,7},{6,4},{7,5},{8,10},{9,11},{10,... | collective-permute-start | bytes 1585160 | tf_op jit(solution)/shard_map/ppermute | solution.py:23
  6.1 21.3 %collective-permute-start.6 = (bf16[2048,128]{1,0:T(8,128)(2,1)}, bf16[2048,128]{1,0:T(8,128)(2,1)S(1)}, u32[]{:S(2)}, u32[]{:S(2)}) collective-permute-start(bf16[2048,128]{1,0:T(8,128)(2,1)} %get-tuple-element.41.refs_0_), channel_id=1, source_target_pairs={{0,24},{4,28},{8,16},{12,20},{16,8},{20,12},{24,0},{28,4},{1,25},{... | collective-permute-start | bytes 1572872 | tf_op jit(solution)/shard_map/ppermute | solution.py:23
  8.3 23.8 %collective-permute-start.4 = (bf16[2048,128]{1,0:T(8,128)(2,1)}, bf16[2048,128]{1,0:T(8,128)(2,1)S(1)}, u32[]{:S(2)}, u32[]{:S(2)}) collective-permute-start(bf16[2048,128]{1,0:T(8,128)(2,1)} %get-tuple-element.41.refs_0_), channel_id=1, source_target_pairs={{0,8},{4,12},{8,0},{12,4},{16,24},{20,28},{24,16},{28,20},{1,9},{5... | collective-permute-start | bytes 1572872 | tf_op jit(solution)/shard_map/ppermute | solution.py:23
  8.6 25.8 %collective-permute-start.5 = (bf16[2048,128]{1,0:T(8,128)(2,1)}, bf16[2048,128]{1,0:T(8,128)(2,1)S(1)}, u32[]{:S(2)}, u32[]{:S(2)}) collective-permute-start(bf16[2048,128]{1,0:T(8,128)(2,1)} %get-tuple-element.41.refs_0_), channel_id=1, source_target_pairs={{0,16},{4,20},{8,24},{12,28},{16,0},{20,4},{24,8},{28,12},{1,17},{... | collective-permute-start | bytes 1572872 | tf_op jit(solution)/shard_map/ppermute | solution.py:23
  26.2 8.3 %collective-permute-start.7 = (bf16[2048,128]{1,0:T(8,128)(2,1)}, bf16[2048,128]{1,0:T(8,128)(2,1)S(1)}, u32[]{:S(2)}, u32[]{:S(2)}) collective-permute-start(bf16[2048,128]{1,0:T(8,128)(2,1)} %get-tuple-element.41.refs_0_), channel_id=1, source_target_pairs={{0,4},{4,0},{8,12},{12,8},{16,20},{20,16},{24,28},{28,24},{1,5},{5... | collective-permute-start | bytes 1572872 | tf_op jit(solution)/shard_map/ppermute | solution.py:23
  27.4 15.8 %collective-permute-start.1 = (bf16[2064,128]{1,0:T(8,128)(2,1)}, bf16[2064,128]{1,0:T(8,128)(2,1)S(1)}, u32[]{:S(2)}, u32[]{:S(2)}) collective-permute-start(bf16[2064,128]{1,0:T(8,128)(2,1)} %get-tuple-element.40.refs_8_.refs_0_), channel_id=1, source_target_pairs={{1,2},{2,1},{5,6},{6,5},{9,10},{10,9},{13,14},{14,13},{17,18},{18,... | collective-permute-start | bytes 1585160 | tf_op jit(solution)/shard_map/ppermute | solution.py:376
  30.8 12.4 %collective-permute-start.3 = (bf16[2064,128]{1,0:T(8,128)(2,1)S(1)}, bf16[2064,128]{1,0:T(8,128)(2,1)S(1)}, u32[]{:S(2)}, u32[]{:S(2)}) collective-permute-start(bf16[2064,128]{1,0:T(8,128)(2,1)S(1)} %collective-permute-done.2.refs_10_.refs_0_), channel_id=1, source_target_pairs={{2,3},{1,0},{6,7},{5,4},{10,11},{9,8},{14,15},{13,12},{18,19},{17,... | collective-permute-start | bytes 1585160 | tf_op jit(solution)/shard_map/ppermute | solution.py:374
  32.2 3.7 %collective-permute-start.10 = (bf16[2048,128]{1,0:T(8,128)(2,1)S(1)}, bf16[2048,128]{1,0:T(8,128)(2,1)S(1)}, u32[]{:S(2)}, u32[]{:S(2)}) collective-permute-start(bf16[2048,128]{1,0:T(8,128)(2,1)S(1)} %collective-permute-done.6.refs_3_), channel_id=1, source_target_pairs={{0,4},{4,0},{8,12},{12,8},{16,20},{20,16},{24,28},{28,24},{1,5},{5... | collective-permute-start | bytes 1572872 | tf_op jit(solution)/shard_map/ppermute | solution.py:23
  34.4 2.3 %collective-permute-start.8 = (bf16[2048,128]{1,0:T(8,128)(2,1)S(1)}, bf16[2048,128]{1,0:T(8,128)(2,1)S(1)}, u32[]{:S(2)}, u32[]{:S(2)}) collective-permute-start(bf16[2048,128]{1,0:T(8,128)(2,1)S(1)} %collective-permute-done.4.refs_1_), channel_id=1, source_target_pairs={{0,4},{4,0},{8,12},{12,8},{16,20},{20,16},{24,28},{28,24},{1,5},{5... | collective-permute-start | bytes 1572872 | tf_op jit(solution)/shard_map/ppermute | solution.py:23
  34.4 2.9 %collective-permute-start.9 = (bf16[2048,128]{1,0:T(8,128)(2,1)S(1)}, bf16[2048,128]{1,0:T(8,128)(2,1)S(1)}, u32[]{:S(2)}, u32[]{:S(2)}) collective-permute-start(bf16[2048,128]{1,0:T(8,128)(2,1)S(1)} %collective-permute-done.5.refs_2_), channel_id=1, source_target_pairs={{0,4},{4,0},{8,12},{12,8},{16,20},{20,16},{24,28},{28,24},{1,5},{5... | collective-permute-start | bytes 1572872 | tf_op jit(solution)/shard_map/ppermute | solution.py:23
  37.4 1.0 copy-start
  38.4 1.0 copy-start.3
  43.2 4.5 %copy-start.5 = (s32[2048]{0:T(1024)S(1)}, s32[2048]{0:T(1024)}, u32[]{:S(2)}) copy-start(s32[2048]{0:T(1024)} %param.12) | copy-start | bytes 24580
  43.2 4.5 %copy-start.6 = (s32[2048]{0:T(1024)S(1)}, s32[2048]{0:T(1024)}, u32[]{:S(2)}) copy-start(s32[2048]{0:T(1024)} %param.13) | copy-start | bytes 24580
  45.0 4.1 %collective-permute-start.11 = (bf16[512,128]{1,0:T(8,128)(2,1)}, bf16[512,128]{1,0:T(8,128)(2,1)S(1)}, u32[]{:S(2)}, u32[]{:S(2)}) collective-permute-start(bf16[512,128]{1,0:T(8,128)(2,1)} %get-tuple-element.45), channel_id=1, source_target_pairs={{0,1},{1,0},{2,3},{3,2},{4,5},{5,4},{6,7},{7,6},{8,9},{9,8},{10,11... | collective-permute-start | bytes 393224 | tf_op jit(solution)/shard_map/ppermute | solution.py:23
  45.6 6.8 %collective-permute-start.12 = (bf16[512,128]{1,0:T(8,128)(2,1)S(1)}, bf16[512,128]{1,0:T(8,128)(2,1)S(1)}, u32[]{:S(2)}, u32[]{:S(2)}) collective-permute-start(bf16[512,128]{1,0:T(8,128)(2,1)S(1)} %get-tuple-element.46), channel_id=1, source_target_pairs={{0,2},{1,3},{2,0},{3,1},{4,6},{5,7},{6,4},{7,5},{8,10},{9,11},{10,... | collective-permute-start | bytes 393224 | tf_op jit(solution)/shard_map/ppermute | solution.py:23
  47.6 10.5 %collective-permute-start.13 = (bf16[512,128]{1,0:T(8,128)(2,1)S(1)}, bf16[512,128]{1,0:T(8,128)(2,1)S(1)}, u32[]{:S(2)}, u32[]{:S(2)}) collective-permute-start(bf16[512,128]{1,0:T(8,128)(2,1)S(1)} %get-tuple-element.47), channel_id=1, source_target_pairs={{0,3},{1,2},{2,1},{3,0},{4,7},{5,6},{6,5},{7,4},{8,11},{9,10},{10,... | collective-permute-start | bytes 393224 | tf_op jit(solution)/shard_map/ppermute | solution.py:23
  59.6 3.9 %collective-permute-start.14 = (bf16[512,128]{1,0:T(8,128)(2,1)S(1)}, bf16[512,128]{1,0:T(8,128)(2,1)S(1)}, u32[]{:S(2)}, u32[]{:S(2)}) collective-permute-start(bf16[512,128]{1,0:T(8,128)(2,1)S(1)} %get-tuple-element.52), channel_id=1, source_target_pairs={{0,1},{1,0},{2,3},{3,2},{4,5},{5,4},{6,7},{7,6},{8,9},{9,8},{10,11... | collective-permute-start | bytes 393224 | tf_op jit(solution)/shard_map/ppermute | solution.py:23
  59.7 10.9 %collective-permute-start.15 = (bf16[512,128]{1,0:T(8,128)(2,1)S(1)}, bf16[512,128]{1,0:T(8,128)(2,1)S(1)}, u32[]{:S(2)}, u32[]{:S(2)}) collective-permute-start(bf16[512,128]{1,0:T(8,128)(2,1)S(1)} %get-tuple-element.53), channel_id=1, source_target_pairs={{0,2},{1,3},{2,0},{3,1},{4,6},{5,7},{6,4},{7,5},{8,10},{9,11},{10,... | collective-permute-start | bytes 393224 | tf_op jit(solution)/shard_map/ppermute | solution.py:23
  63.0 10.7 %collective-permute-start.16 = (bf16[512,128]{1,0:T(8,128)(2,1)S(1)}, bf16[512,128]{1,0:T(8,128)(2,1)S(1)}, u32[]{:S(2)}, u32[]{:S(2)}) collective-permute-start(bf16[512,128]{1,0:T(8,128)(2,1)S(1)} %get-tuple-element.54), channel_id=1, source_target_pairs={{0,3},{1,2},{2,1},{3,0},{4,7},{5,6},{6,5},{7,4},{8,11},{9,10},{10,... | collective-permute-start | bytes 393224 | tf_op jit(solution)/shard_map/ppermute | solution.py:23
  73.6 4.5 %copy-start.1 = (bf16[2064,128]{1,0:T(8,128)(2,1)S(1)}, bf16[2064,128]{1,0:T(8,128)(2,1)}, u32[]{:S(2)}) copy-start(bf16[2064,128]{1,0:T(8,128)(2,1)} %get-tuple-element.40.refs_8_.refs_0_) | copy-start | bytes 1585156
  75.8 4.9 %collective-permute-start.17 = (bf16[5120,128]{1,0:T(8,128)(2,1)S(1)}, bf16[5120,128]{1,0:T(8,128)(2,1)S(1)}, u32[]{:S(2)}, u32[]{:S(2)}) collective-permute-start(bf16[5120,128]{1,0:T(8,128)(2,1)S(1)} %get-tuple-element.59), channel_id=1, source_target_pairs={{0,4},{4,0},{8,12},{12,8},{16,20},{20,16},{24,28},{28,24},{1,5},{5... | collective-permute-start | bytes 3932168 | tf_op jit(solution)/shard_map/ppermute | solution.py:23
  80.2 3.9 %collective-permute-start.21 = (bf16[4096,128]{1,0:T(8,128)(2,1)S(1)}, bf16[4096,128]{1,0:T(8,128)(2,1)S(1)}, u32[]{:S(2)}, u32[]{:S(2)}) collective-permute-start(bf16[4096,128]{1,0:T(8,128)(2,1)S(1)} %get-tuple-element.65), channel_id=1, source_target_pairs={{0,4},{4,0},{8,12},{12,8},{16,20},{20,16},{24,28},{28,24},{1,5},{5... | collective-permute-start | bytes 3145736 | tf_op jit(solution)/shard_map/ppermute | solution.py:23
  81.0 9.0 %collective-permute-start.18 = (bf16[1280,128]{1,0:T(8,128)(2,1)S(1)}, bf16[1280,128]{1,0:T(8,128)(2,1)S(1)}, u32[]{:S(2)}, u32[]{:S(2)}) collective-permute-start(bf16[1280,128]{1,0:T(8,128)(2,1)S(1)} %get-tuple-element.62), channel_id=1, source_target_pairs={{0,8},{4,12},{8,0},{12,4},{16,24},{20,28},{24,16},{28,20},{1,9},{5... | collective-permute-start | bytes 983048 | tf_op jit(solution)/shard_map/ppermute | solution.py:23
  81.9 14.7 %collective-permute-start.19 = (bf16[1280,128]{1,0:T(8,128)(2,1)S(1)}, bf16[1280,128]{1,0:T(8,128)(2,1)S(1)}, u32[]{:S(2)}, u32[]{:S(2)}) collective-permute-start(bf16[1280,128]{1,0:T(8,128)(2,1)S(1)} %get-tuple-element.63), channel_id=1, source_target_pairs={{0,16},{4,20},{8,24},{12,28},{16,0},{20,4},{24,8},{28,12},{1,17},{... | collective-permute-start | bytes 983048 | tf_op jit(solution)/shard_map/ppermute | solution.py:23
  84.1 14.5 %collective-permute-start.20 = (bf16[1280,128]{1,0:T(8,128)(2,1)S(1)}, bf16[1280,128]{1,0:T(8,128)(2,1)S(1)}, u32[]{:S(2)}, u32[]{:S(2)}) collective-permute-start(bf16[1280,128]{1,0:T(8,128)(2,1)S(1)} %get-tuple-element.64), channel_id=1, source_target_pairs={{0,24},{4,28},{8,16},{12,20},{16,8},{20,12},{24,0},{28,4},{1,25},{... | collective-permute-start | bytes 983048 | tf_op jit(solution)/shard_map/ppermute | solution.py:23
  84.3 18.4 %collective-permute-start.25 = (bf16[1024,128]{1,0:T(8,128)(2,1)S(1)}, bf16[1024,128]{1,0:T(8,128)(2,1)S(1)}, u32[]{:S(2)}, u32[]{:S(2)}) collective-permute-start(bf16[1024,128]{1,0:T(8,128)(2,1)S(1)} %get-tuple-element.70), channel_id=1, source_target_pairs={{0,8},{4,12},{8,0},{12,4},{16,24},{20,28},{24,16},{28,20},{1,9},{5... | collective-permute-start | bytes 786440 | tf_op jit(solution)/shard_map/ppermute | solution.py:23
  85.6 22.9 %collective-permute-start.26 = (bf16[1024,128]{1,0:T(8,128)(2,1)S(1)}, bf16[1024,128]{1,0:T(8,128)(2,1)S(1)}, u32[]{:S(2)}, u32[]{:S(2)}) collective-permute-start(bf16[1024,128]{1,0:T(8,128)(2,1)S(1)} %get-tuple-element.71), channel_id=1, source_target_pairs={{0,16},{4,20},{8,24},{12,28},{16,0},{20,4},{24,8},{28,12},{1,17},{... | collective-permute-start | bytes 786440 | tf_op jit(solution)/shard_map/ppermute | solution.py:23
  90.0 19.8 %collective-permute-start.27 = (bf16[1024,128]{1,0:T(8,128)(2,1)S(1)}, bf16[1024,128]{1,0:T(8,128)(2,1)S(1)}, u32[]{:S(2)}, u32[]{:S(2)}) collective-permute-start(bf16[1024,128]{1,0:T(8,128)(2,1)S(1)} %get-tuple-element.72), channel_id=1, source_target_pairs={{0,24},{4,28},{8,16},{12,20},{16,8},{20,12},{24,0},{28,4},{1,25},{... | collective-permute-start | bytes 786440 | tf_op jit(solution)/shard_map/ppermute | solution.py:23
  98.7 11.3 %collective-permute-start.23 = (bf16[768,128]{1,0:T(8,128)(2,1)S(1)}, bf16[768,128]{1,0:T(8,128)(2,1)S(1)}, u32[]{:S(2)}, u32[]{:S(2)}) collective-permute-start(bf16[768,128]{1,0:T(8,128)(2,1)S(1)} %get-tuple-element.68), channel_id=1, source_target_pairs={{0,2},{1,3},{2,0},{3,1},{4,6},{5,7},{6,4},{7,5},{8,10},{9,11},{10,... | collective-permute-start | bytes 589832 | tf_op jit(solution)/shard_map/ppermute | solution.py:23
  99.1 17.8 %collective-permute-start.24 = (bf16[768,128]{1,0:T(8,128)(2,1)S(1)}, bf16[768,128]{1,0:T(8,128)(2,1)S(1)}, u32[]{:S(2)}, u32[]{:S(2)}) collective-permute-start(bf16[768,128]{1,0:T(8,128)(2,1)S(1)} %get-tuple-element.69), channel_id=1, source_target_pairs={{0,3},{1,2},{2,1},{3,0},{4,7},{5,6},{6,5},{7,4},{8,11},{9,10},{10,... | collective-permute-start | bytes 589832 | tf_op jit(solution)/shard_map/ppermute | solution.py:23
  102.7 7.3 %collective-permute-start.22 = (bf16[256,128]{1,0:T(8,128)(2,1)S(1)}, bf16[256,128]{1,0:T(8,128)(2,1)S(1)}, u32[]{:S(2)}, u32[]{:S(2)}) collective-permute-start(bf16[256,128]{1,0:T(8,128)(2,1)S(1)} %get-tuple-element.67.refs_0_), channel_id=1, source_target_pairs={{0,1},{1,0},{2,3},{3,2},{4,5},{5,4},{6,7},{7,6},{8,9},{9,8},{10,11... | collective-permute-start | bytes 196616 | tf_op jit(solution)/shard_map/ppermute | solution.py:23
  110.0 15.4 %collective-permute-start.35 = (bf16[512,128]{1,0:T(8,128)(2,1)S(1)}, bf16[512,128]{1,0:T(8,128)(2,1)S(1)}, u32[]{:S(2)}, u32[]{:S(2)}) collective-permute-start(bf16[512,128]{1,0:T(8,128)(2,1)S(1)} %get-tuple-element.74), channel_id=1, source_target_pairs={{0,1},{1,0},{2,3},{3,2},{4,5},{5,4},{6,7},{7,6},{8,9},{9,8},{10,11... | collective-permute-start | bytes 393224 | tf_op jit(solution)/shard_map/ppermute | solution.py:23
  116.9 5.2 %collective-permute-start.28 = (bf16[256,128]{1,0:T(8,128)(2,1)S(1)}, bf16[256,128]{1,0:T(8,128)(2,1)S(1)}, u32[]{:S(2)}, u32[]{:S(2)}) collective-permute-start(bf16[256,128]{1,0:T(8,128)(2,1)S(1)} %weight_total.1.refs_0_), channel_id=1, source_target_pairs={{0,8},{4,12},{8,0},{12,4},{16,24},{20,28},{24,16},{28,20},{1,9},{5... | collective-permute-start | bytes 196616 | tf_op jit(solution)/shard_map/ppermute | solution.py:23
  118.1 5.3 %collective-permute-start.29 = (bf16[256,128]{1,0:T(8,128)(2,1)S(1)}, bf16[256,128]{1,0:T(8,128)(2,1)S(1)}, u32[]{:S(2)}, u32[]{:S(2)}) collective-permute-start(bf16[256,128]{1,0:T(8,128)(2,1)S(1)} %weight_total.1.refs_0_), channel_id=1, source_target_pairs={{0,16},{4,20},{8,24},{12,28},{16,0},{20,4},{24,8},{28,12},{1,17},{... | collective-permute-start | bytes 196616 | tf_op jit(solution)/shard_map/ppermute | solution.py:23
  118.4 5.9 %collective-permute-start.30 = (bf16[256,128]{1,0:T(8,128)(2,1)S(1)}, bf16[256,128]{1,0:T(8,128)(2,1)S(1)}, u32[]{:S(2)}, u32[]{:S(2)}) collective-permute-start(bf16[256,128]{1,0:T(8,128)(2,1)S(1)} %weight_total.1.refs_0_), channel_id=1, source_target_pairs={{0,24},{4,28},{8,16},{12,20},{16,8},{20,12},{24,0},{28,4},{1,25},{... | collective-permute-start | bytes 196616 | tf_op jit(solution)/shard_map/ppermute | solution.py:23
  119.6 6.7 %collective-permute-start.31 = (bf16[256,128]{1,0:T(8,128)(2,1)S(1)}, bf16[256,128]{1,0:T(8,128)(2,1)S(1)}, u32[]{:S(2)}, u32[]{:S(2)}) collective-permute-start(bf16[256,128]{1,0:T(8,128)(2,1)S(1)} %weight_total.1.refs_0_), channel_id=1, source_target_pairs={{0,4},{4,0},{8,12},{12,8},{16,20},{20,16},{24,28},{28,24},{1,5},{5... | collective-permute-start | bytes 196616 | tf_op jit(solution)/shard_map/ppermute | solution.py:23
  122.1 4.2 %collective-permute-start.32 = (bf16[256,128]{1,0:T(8,128)(2,1)S(1)}, bf16[256,128]{1,0:T(8,128)(2,1)S(1)}, u32[]{:S(2)}, u32[]{:S(2)}) collective-permute-start(bf16[256,128]{1,0:T(8,128)(2,1)S(1)} %collective-permute-done.28.refs_1_), channel_id=1, source_target_pairs={{0,4},{4,0},{8,12},{12,8},{16,20},{20,16},{24,28},{28,24},{1,5},{5... | collective-permute-start | bytes 196616 | tf_op jit(solution)/shard_map/ppermute | solution.py:23
  123.4 2.9 %collective-permute-start.33 = (bf16[256,128]{1,0:T(8,128)(2,1)S(1)}, bf16[256,128]{1,0:T(8,128)(2,1)S(1)}, u32[]{:S(2)}, u32[]{:S(2)}) collective-permute-start(bf16[256,128]{1,0:T(8,128)(2,1)S(1)} %collective-permute-done.29.refs_2_), channel_id=1, source_target_pairs={{0,4},{4,0},{8,12},{12,8},{16,20},{20,16},{24,28},{28,24},{1,5},{5... | collective-permute-start | bytes 196616 | tf_op jit(solution)/shard_map/ppermute | solution.py:23
  124.3 2.0 %collective-permute-start.34 = (bf16[256,128]{1,0:T(8,128)(2,1)S(1)}, bf16[256,128]{1,0:T(8,128)(2,1)S(1)}, u32[]{:S(2)}, u32[]{:S(2)}) collective-permute-start(bf16[256,128]{1,0:T(8,128)(2,1)S(1)} %collective-permute-done.30.refs_3_), channel_id=1, source_target_pairs={{0,4},{4,0},{8,12},{12,8},{16,20},{20,16},{24,28},{28,24},{1,5},{5... | collective-permute-start | bytes 196616 | tf_op jit(solution)/shard_map/ppermute | solution.py:23
